TPU v7x, 32 devices: a whole 2x2x4 slice. The times are simulated.
32 devices in a mesh: fsdp: 8 (over z, y), dp: 4 (over x, core).
Axes of the slice: x: 2, y: 2, z: 4, core: 2. Of those that a mesh axis runs over, the one named last changes fastest.
Arguments:
- images: bfloat16 [128, 14, 14, 1024], P(('fsdp', 'dp')), may hold values from -6 to 6
- image_sides: int32 [128], P(('fsdp', 'dp')), may hold values from 0 to 14, as said below
- widths: int32 [2], replicated, may hold values from 128 to 512, as said below
- keep_gate: int32 [128], P(('fsdp', 'dp')), may hold values 0 or 1
- w_in_a: bfloat16 [1024, 512], P('fsdp'), may hold values from -0.1875 to 0.1875
- w_mid_a: bfloat16 [4608, 512], P('fsdp'), may hold values from -0.09375 to 0.09375
- w_out_a: bfloat16 [512, 2048], P('fsdp'), may hold values from -0.25 to 0.25
- w_proj_a: bfloat16 [1024, 2048], P('fsdp'), may hold values from -0.1875 to 0.1875
- norm_in_a: bfloat16 [2, 512], P(None, 'fsdp'), may hold values from -0.5 to 1.5, as said below
- norm_mid_a: bfloat16 [2, 512], P(None, 'fsdp'), may hold values from -0.5 to 1.5, as said below
- norm_out_a: bfloat16 [2, 2048], P(None, 'fsdp'), may hold values from -0.5 to 1.5, as said below
- norm_proj_a: bfloat16 [2, 2048], P(None, 'fsdp'), may hold values from -0.5 to 1.5, as said below
- w_in_b: bfloat16 [2048, 512], P('fsdp'), may hold values from -0.125 to 0.125
- w_mid_b: bfloat16 [4608, 512], P('fsdp'), may hold values from -0.09375 to 0.09375
- w_out_b: bfloat16 [512, 2048], P('fsdp'), may hold values from -0.25 to 0.25
- norm_in_b: bfloat16 [2, 512], P(None, 'fsdp'), may hold values from -0.5 to 1.5, as said below
- norm_mid_b: bfloat16 [2, 512], P(None, 'fsdp'), may hold values from -0.5 to 1.5, as said below
- norm_out_b: bfloat16 [2, 2048], P(None, 'fsdp'), may hold values from -0.5 to 1.5, as said below
- cotangent: bfloat16 [128, 7, 7, 2048], P(('fsdp', 'dp')), may hold values from -6 to 6
Outputs:
- result: bfloat16 [128, 7, 7, 2048], P(('fsdp', 'dp'))
- grad_images: bfloat16 [128, 14, 14, 1024], P(('fsdp', 'dp'))
- grad_w_in_a: float32 [1024, 512], P('fsdp')
- grad_w_mid_a: float32 [4608, 512], P('fsdp')
- grad_w_out_a: float32 [512, 2048], P('fsdp')
- grad_w_proj_a: float32 [1024, 2048], P('fsdp')
- grad_norm_in_a: float32 [2, 512], P(None, 'fsdp')
- grad_norm_mid_a: float32 [2, 512], P(None, 'fsdp')
- grad_norm_out_a: float32 [2, 2048], P(None, 'fsdp')
- grad_norm_proj_a: float32 [2, 2048], P(None, 'fsdp')
- grad_w_in_b: float32 [2048, 512], P('fsdp')
- grad_w_mid_b: float32 [4608, 512], P('fsdp')
- grad_w_out_b: float32 [512, 2048], P('fsdp')
- grad_norm_in_b: float32 [2, 512], P(None, 'fsdp')
- grad_norm_mid_b: float32 [2, 512], P(None, 'fsdp')
- grad_norm_out_b: float32 [2, 2048], P(None, 'fsdp')
Inputs may be any that keep to these rules, and one draw needn't show every extreme that they name: `image_sides`: each slot's side is 0 (empty), 10, 12 or 14; on each device the live slots come first and at least 2 of its 4 slots are live; some device has all 4 slots live, one of them of side 14. `widths`: both are multiples of 128, and one of them is 512. `norm_in_a`: row 0 (gains) lies in 0.6 to 1.5, row 1 (shifts) in -0.5 to 0.5. `norm_mid_a`: row 0 (gains) lies in 0.6 to 1.5, row 1 (shifts) in -0.5 to 0.5. `norm_out_a`: row 0 (gains) lies in 0.6 to 1.5, row 1 (shifts) in -0.5 to 0.5. `norm_proj_a`: row 0 (gains) lies in 0.6 to 1.5, row 1 (shifts) in -0.5 to 0.5. `norm_in_b`: row 0 (gains) lies in 0.6 to 1.5, row 1 (shifts) in -0.5 to 0.5. `norm_mid_b`: row 0 (gains) lies in 0.6 to 1.5, row 1 (shifts) in -0.5 to 0.5. `norm_out_b`: row 0 (gains) lies in 0.6 to 1.5, row 1 (shifts) in -0.5 to 0.5.
All inputs are finite; a program needn't handle non-finite values. No bound on the sum of `keep_gate` on one device may be relied on, other than what follows from the above.
Results may differ from a plain program's by a relative error of at most 0.019.
Values may be sent and summed in bfloat16 or wider, within the bound.
A program may use at most 192 MiB of HBM per device.

v0:
```python
import jax
import jax.numpy as jnp
from jax import lax
from jax.sharding import PartitionSpec as P

EPSILON = 1e-05


def silu_slope(values):
    sigmoid_part = jax.nn.sigmoid(values)
    return sigmoid_part * (1.0 + values * (1.0 - sigmoid_part))


def pixel_masks(image_sides, side_in, side_out):
    half_sides = image_sides // 2
    rows_in = jnp.arange(side_in, dtype=jnp.int32)
    rows_out = jnp.arange(side_out, dtype=jnp.int32)
    inside_in = (rows_in[None, :, None] < image_sides[:, None, None]) & (
        rows_in[None, None, :] < image_sides[:, None, None]
    )
    inside_out = (rows_out[None, :, None] < half_sides[:, None, None]) & (
        rows_out[None, None, :] < half_sides[:, None, None]
    )
    local_counts = jnp.stack(
        [jnp.sum(image_sides * image_sides), jnp.sum(half_sides * half_sides)]
    ).astype(jnp.float32)
    return (
        inside_in.astype(jnp.float32)[..., None],
        inside_out.astype(jnp.float32)[..., None],
        local_counts,
    )


def norm_stats(hidden, pixel_mask, local_counts, count_slot):
    sum_values, sum_squares, totals = lax.psum(
        (
            jnp.sum(hidden * pixel_mask, axis=(0, 1, 2)),
            jnp.sum(hidden * hidden * pixel_mask, axis=(0, 1, 2)),
            local_counts,
        ),
        ("fsdp", "dp"),
    )
    pixel_total = totals[count_slot]
    average = sum_values / pixel_total
    inv_std = lax.rsqrt(sum_squares / pixel_total - average * average + EPSILON)
    return (average, inv_std, pixel_total)


def normalize(hidden, stats_now, params, channel):
    average, inv_std, pixel_total = stats_now
    scaled = (hidden - average) * inv_std
    params_wide = params.astype(jnp.float32)
    return (scaled, (scaled * params_wide[0] + params_wide[1]) * channel)


def norm_backward(grad_norm, scaled, stats_now, params, pixel_mask):
    average, inv_std, pixel_total = stats_now
    shift_sum, gain_sum = lax.psum(
        (jnp.sum(grad_norm, axis=(0, 1, 2)), jnp.sum(grad_norm * scaled, axis=(0, 1, 2))),
        ("fsdp", "dp"),
    )
    gain_row = params[0].astype(jnp.float32)
    grad_hidden = (
        gain_row
        * inv_std
        * (grad_norm - shift_sum / pixel_total - scaled * gain_sum / pixel_total)
        * pixel_mask
    )
    return (grad_hidden.astype(jnp.bfloat16), gain_sum, shift_sum)


def taps_stride_two(activations):
    slot_count = activations.shape[0]
    half_side = activations.shape[1] // 2
    lane_count = activations.shape[3]
    padded = jnp.pad(activations, ((0, 0), (1, 1), (1, 1), (0, 0)))
    parity_grid = padded.reshape(slot_count, half_side + 1, 2, half_side + 1, 2, lane_count)
    pieces = [
        parity_grid[
            :,
            row_tap // 2 : row_tap // 2 + half_side,
            row_tap % 2,
            col_tap // 2 : col_tap // 2 + half_side,
            col_tap % 2,
            :,
        ]
        for row_tap in range(3)
        for col_tap in range(3)
    ]
    return jnp.concatenate(pieces, axis=-1)


def fold_stride_two(grad_cols, side_in):
    slot_count = grad_cols.shape[0]
    half_side = grad_cols.shape[1]
    lane_count = grad_cols.shape[3] // 9
    planes = [
        [
            jnp.zeros((slot_count, half_side + 1, half_side + 1, lane_count), jnp.float32)
            for col_par in range(2)
        ]
        for row_par in range(2)
    ]
    for row_tap in range(3):
        for col_tap in range(3):
            tap_index = row_tap * 3 + col_tap
            tap_piece = grad_cols[..., tap_index * lane_count : (tap_index + 1) * lane_count]
            placed = jnp.pad(
                tap_piece,
                (
                    (0, 0),
                    (row_tap // 2, 1 - row_tap // 2),
                    (col_tap // 2, 1 - col_tap // 2),
                    (0, 0),
                ),
            )
            planes[row_tap % 2][col_tap % 2] = planes[row_tap % 2][col_tap % 2] + placed
    parity_grid = jnp.stack([jnp.stack(planes[0], axis=3), jnp.stack(planes[1], axis=3)], axis=2)
    whole_grid = parity_grid.reshape(slot_count, side_in + 2, side_in + 2, lane_count)
    return whole_grid[:, 1:-1, 1:-1, :]


def taps_stride_one(activations):
    side_now = activations.shape[1]
    padded = jnp.pad(activations, ((0, 0), (1, 1), (1, 1), (0, 0)))
    pieces = [
        padded[:, row_tap : row_tap + side_now, col_tap : col_tap + side_now, :]
        for row_tap in range(3)
        for col_tap in range(3)
    ]
    return jnp.concatenate(pieces, axis=-1)


def fold_stride_one(grad_cols):
    lane_count = grad_cols.shape[3] // 9
    whole_grid = None
    for row_tap in range(3):
        for col_tap in range(3):
            tap_index = row_tap * 3 + col_tap
            tap_piece = grad_cols[..., tap_index * lane_count : (tap_index + 1) * lane_count]
            placed = jnp.pad(
                tap_piece, ((0, 0), (row_tap, 2 - row_tap), (col_tap, 2 - col_tap), (0, 0))
            )
            whole_grid = placed if whole_grid is None else whole_grid + placed
    return whole_grid[:, 1:-1, 1:-1, :]


def contract(left_side, right_side):
    return lax.dot_general(
        left_side,
        right_side,
        (((0, 1, 2), (0, 1, 2)), ((), ())),
        preferred_element_type=jnp.float32,
    )


def back_project(gradient, weight):
    return lax.dot_general(
        gradient, weight, (((3,), (1,)), ((), ())), preferred_element_type=jnp.float32
    )


def own_shard(pair_sums):
    gain_sum, shift_sum = pair_sums
    shard_width = gain_sum.shape[0] // lax.axis_size("fsdp")
    offset = lax.axis_index("fsdp") * shard_width
    return jnp.stack(
        [
            lax.dynamic_slice_in_dim(gain_sum, offset, shard_width, 0),
            lax.dynamic_slice_in_dim(shift_sum, offset, shard_width, 0),
        ]
    )


def block_a_forward(inputs, weights, mask_in, mask_out, local_counts, channel, saved_stats):
    w_in, w_mid, w_out, w_proj, norm_in, norm_mid, norm_out, norm_proj = weights
    conv_first = jnp.dot(inputs, w_in, preferred_element_type=jnp.float32)
    stats_first = (
        norm_stats(conv_first, mask_in, local_counts, 0) if saved_stats is None else saved_stats[0]
    )
    scaled_first, normed_first = normalize(conv_first, stats_first, norm_in, channel)
    act_first = (jax.nn.silu(normed_first) * mask_in).astype(jnp.bfloat16)
    cols_mid = taps_stride_two(act_first)
    conv_mid = jnp.dot(cols_mid, w_mid, preferred_element_type=jnp.float32)
    stats_mid = (
        norm_stats(conv_mid, mask_out, local_counts, 1) if saved_stats is None else saved_stats[1]
    )
    scaled_mid, normed_mid = normalize(conv_mid, stats_mid, norm_mid, channel)
    act_mid = (jax.nn.silu(normed_mid) * mask_out).astype(jnp.bfloat16)
    conv_out = jnp.dot(act_mid, w_out, preferred_element_type=jnp.float32)
    slot_count, side_in, lane_count = (inputs.shape[0], inputs.shape[1], inputs.shape[3])
    sampled = inputs.reshape(slot_count, side_in // 2, 2, side_in // 2, 2, lane_count)[
        :, :, 0, :, 0, :
    ]
    conv_proj = jnp.dot(sampled, w_proj, preferred_element_type=jnp.float32)
    conv_both = jnp.concatenate([conv_out, conv_proj], axis=-1)
    norm_both = jnp.concatenate([norm_out, norm_proj], axis=-1)
    stats_both = (
        norm_stats(conv_both, mask_out, local_counts, 1) if saved_stats is None else saved_stats[2]
    )
    scaled_both, normed_both = normalize(conv_both, stats_both, norm_both, 1.0)
    width_out = conv_out.shape[-1]
    pre_sum = normed_both[..., :width_out] + normed_both[..., width_out:]
    block_out = jax.nn.silu(pre_sum) * mask_out
    saved_values = (
        scaled_first,
        normed_first,
        act_first,
        cols_mid,
        scaled_mid,
        normed_mid,
        act_mid,
        sampled,
        scaled_both,
        pre_sum,
    )
    return (block_out, (stats_first, stats_mid, stats_both), saved_values)


def block_a_backward(
    grad_out, inputs, weights, stats_all, saved_values, mask_in, mask_out, channel
):
    w_in, w_mid, w_out, w_proj, norm_in, norm_mid, norm_out, norm_proj = weights
    stats_first, stats_mid, stats_both = stats_all
    (
        scaled_first,
        normed_first,
        act_first,
        cols_mid,
        scaled_mid,
        normed_mid,
        act_mid,
        sampled,
        scaled_both,
        pre_sum,
    ) = saved_values
    grad_pre = grad_out * mask_out * silu_slope(pre_sum)
    grad_both = jnp.concatenate([grad_pre, grad_pre], axis=-1)
    norm_both = jnp.concatenate([norm_out, norm_proj], axis=-1)
    low_both, gain_both, shift_both = norm_backward(
        grad_both, scaled_both, stats_both, norm_both, mask_out
    )
    width_out = grad_pre.shape[-1]
    low_out = low_both[..., :width_out]
    low_proj = low_both[..., width_out:]
    grad_w_out = contract(act_mid, low_out)
    grad_w_proj = contract(sampled, low_proj)
    grad_norm_mid = back_project(low_out, w_out) * mask_out * channel * silu_slope(normed_mid)
    low_mid, gain_mid, shift_mid = norm_backward(
        grad_norm_mid, scaled_mid, stats_mid, norm_mid, mask_out
    )
    grad_w_mid = contract(cols_mid, low_mid)
    grad_act_first = fold_stride_two(back_project(low_mid, w_mid), inputs.shape[1])
    grad_norm_first = grad_act_first * mask_in * channel * silu_slope(normed_first)
    low_first, gain_first, shift_first = norm_backward(
        grad_norm_first, scaled_first, stats_first, norm_in, mask_in
    )
    grad_w_in = contract(inputs, low_first)
    spread = lax.pad(
        back_project(low_proj, w_proj),
        jnp.float32(0.0),
        ((0, 0, 0), (0, 1, 1), (0, 1, 1), (0, 0, 0)),
    )
    grad_inputs = (back_project(low_first, w_in) + spread) * mask_in
    norm_grads = (
        (gain_first, shift_first),
        (gain_mid, shift_mid),
        (gain_both[:width_out], shift_both[:width_out]),
        (gain_both[width_out:], shift_both[width_out:]),
    )
    return (grad_inputs, (grad_w_in, grad_w_mid, grad_w_out, grad_w_proj), norm_grads)


def block_b_forward(block_in, weights, mask_out, local_counts, channel, depth_gate, saved_stats):
    w_in, w_mid, w_out, norm_in, norm_mid, norm_out = weights
    feed_in = block_in.astype(jnp.bfloat16)
    conv_first = jnp.dot(feed_in, w_in, preferred_element_type=jnp.float32)
    stats_first = (
        norm_stats(conv_first, mask_out, local_counts, 1) if saved_stats is None else saved_stats[0]
    )
    scaled_first, normed_first = normalize(conv_first, stats_first, norm_in, channel)
    act_first = (jax.nn.silu(normed_first) * mask_out).astype(jnp.bfloat16)
    cols_mid = taps_stride_one(act_first)
    conv_mid = jnp.dot(cols_mid, w_mid, preferred_element_type=jnp.float32)
    stats_mid = (
        norm_stats(conv_mid, mask_out, local_counts, 1) if saved_stats is None else saved_stats[1]
    )
    scaled_mid, normed_mid = normalize(conv_mid, stats_mid, norm_mid, channel)
    act_mid = (jax.nn.silu(normed_mid) * mask_out).astype(jnp.bfloat16)
    conv_out = jnp.dot(act_mid, w_out, preferred_element_type=jnp.float32)
    stats_out = (
        norm_stats(conv_out, mask_out, local_counts, 1) if saved_stats is None else saved_stats[2]
    )
    scaled_out, normed_out = normalize(conv_out, stats_out, norm_out, 1.0)
    pre_sum = block_in + depth_gate * normed_out
    result = jax.nn.silu(pre_sum) * mask_out
    saved_values = (
        feed_in,
        scaled_first,
        normed_first,
        act_first,
        cols_mid,
        scaled_mid,
        normed_mid,
        act_mid,
        scaled_out,
        pre_sum,
    )
    return (result, (stats_first, stats_mid, stats_out), saved_values)


def block_b_backward(grad_out, weights, stats_all, saved_values, mask_out, channel, depth_gate):
    w_in, w_mid, w_out, norm_in, norm_mid, norm_out = weights
    stats_first, stats_mid, stats_out = stats_all
    (
        feed_in,
        scaled_first,
        normed_first,
        act_first,
        cols_mid,
        scaled_mid,
        normed_mid,
        act_mid,
        scaled_out,
        pre_sum,
    ) = saved_values
    grad_pre = grad_out * mask_out * silu_slope(pre_sum)
    low_out, gain_out, shift_out = norm_backward(
        grad_pre * depth_gate, scaled_out, stats_out, norm_out, mask_out
    )
    grad_w_out = contract(act_mid, low_out)
    grad_norm_mid = back_project(low_out, w_out) * mask_out * channel * silu_slope(normed_mid)
    low_mid, gain_mid, shift_mid = norm_backward(
        grad_norm_mid, scaled_mid, stats_mid, norm_mid, mask_out
    )
    grad_w_mid = contract(cols_mid, low_mid)
    grad_norm_first = (
        fold_stride_one(back_project(low_mid, w_mid))
        * mask_out
        * channel
        * silu_slope(normed_first)
    )
    low_first, gain_first, shift_first = norm_backward(
        grad_norm_first, scaled_first, stats_first, norm_in, mask_out
    )
    grad_w_in = contract(feed_in, low_first)
    grad_in = grad_pre + back_project(low_first, w_in)
    norm_grads = ((gain_first, shift_first), (gain_mid, shift_mid), (gain_out, shift_out))
    return (grad_in, (grad_w_in, grad_w_mid, grad_w_out), norm_grads)


def body(
    images,
    image_sides,
    widths,
    keep_gate,
    w_in_a,
    w_mid_a,
    w_out_a,
    w_proj_a,
    norm_in_a,
    norm_mid_a,
    norm_out_a,
    norm_proj_a,
    w_in_b,
    w_mid_b,
    w_out_b,
    norm_in_b,
    norm_mid_b,
    norm_out_b,
    cotangent,
):
    mask_in, mask_out, local_counts = pixel_masks(image_sides, images.shape[1], cotangent.shape[1])
    lane_ids = jnp.arange(w_mid_a.shape[1], dtype=jnp.int32)
    channel_a = (lane_ids < widths[0]).astype(jnp.float32)
    channel_b = (lane_ids < widths[1]).astype(jnp.float32)
    depth_gate = keep_gate.astype(jnp.float32)[:, None, None, None]
    inputs = images * mask_in.astype(jnp.bfloat16)
    weights_a = (
        lax.all_gather(w_in_a, "fsdp", axis=0, tiled=True),
        lax.all_gather(w_mid_a, "fsdp", axis=0, tiled=True),
        lax.all_gather(w_out_a, "fsdp", axis=0, tiled=True),
        lax.all_gather(w_proj_a, "fsdp", axis=0, tiled=True),
        lax.all_gather(norm_in_a, "fsdp", axis=1, tiled=True),
        lax.all_gather(norm_mid_a, "fsdp", axis=1, tiled=True),
        lax.all_gather(norm_out_a, "fsdp", axis=1, tiled=True),
        lax.all_gather(norm_proj_a, "fsdp", axis=1, tiled=True),
    )
    block_out, stats_a, unused_a = block_a_forward(
        inputs, weights_a, mask_in, mask_out, local_counts, channel_a, None
    )
    weights_b = (
        lax.all_gather(w_in_b, "fsdp", axis=0, tiled=True),
        lax.all_gather(w_mid_b, "fsdp", axis=0, tiled=True),
        lax.all_gather(w_out_b, "fsdp", axis=0, tiled=True),
        lax.all_gather(norm_in_b, "fsdp", axis=1, tiled=True),
        lax.all_gather(norm_mid_b, "fsdp", axis=1, tiled=True),
        lax.all_gather(norm_out_b, "fsdp", axis=1, tiled=True),
    )
    result, stats_b, unused_b = block_b_forward(
        block_out, weights_b, mask_out, local_counts, channel_b, depth_gate, None
    )
    backward_b = (
        lax.all_gather(w_in_b, "fsdp", axis=0, tiled=True),
        lax.all_gather(w_mid_b, "fsdp", axis=0, tiled=True),
        lax.all_gather(w_out_b, "fsdp", axis=0, tiled=True),
        lax.all_gather(norm_in_b, "fsdp", axis=1, tiled=True),
        lax.all_gather(norm_mid_b, "fsdp", axis=1, tiled=True),
        lax.all_gather(norm_out_b, "fsdp", axis=1, tiled=True),
    )
    redone_b = block_b_forward(
        block_out, backward_b, mask_out, local_counts, channel_b, depth_gate, stats_b
    )[2]
    grad_block, grads_b, norms_b = block_b_backward(
        cotangent.astype(jnp.float32),
        backward_b,
        stats_b,
        redone_b,
        mask_out,
        channel_b,
        depth_gate,
    )
    backward_a = (
        lax.all_gather(w_in_a, "fsdp", axis=0, tiled=True),
        lax.all_gather(w_mid_a, "fsdp", axis=0, tiled=True),
        lax.all_gather(w_out_a, "fsdp", axis=0, tiled=True),
        lax.all_gather(w_proj_a, "fsdp", axis=0, tiled=True),
        lax.all_gather(norm_in_a, "fsdp", axis=1, tiled=True),
        lax.all_gather(norm_mid_a, "fsdp", axis=1, tiled=True),
        lax.all_gather(norm_out_a, "fsdp", axis=1, tiled=True),
        lax.all_gather(norm_proj_a, "fsdp", axis=1, tiled=True),
    )
    redone_a = block_a_forward(
        inputs, backward_a, mask_in, mask_out, local_counts, channel_a, stats_a
    )[2]
    grad_inputs, grads_a, norms_a = block_a_backward(
        grad_block, inputs, backward_a, stats_a, redone_a, mask_in, mask_out, channel_a
    )
    part_in_a, part_mid_a, part_out_a, part_proj_a, part_in_b, part_mid_b, part_out_b = (
        lax.psum_scatter(grads_a[0], "fsdp", scatter_dimension=0, tiled=True),
        lax.psum_scatter(grads_a[1], "fsdp", scatter_dimension=0, tiled=True),
        lax.psum_scatter(grads_a[2], "fsdp", scatter_dimension=0, tiled=True),
        lax.psum_scatter(grads_a[3], "fsdp", scatter_dimension=0, tiled=True),
        lax.psum_scatter(grads_b[0], "fsdp", scatter_dimension=0, tiled=True),
        lax.psum_scatter(grads_b[1], "fsdp", scatter_dimension=0, tiled=True),
        lax.psum_scatter(grads_b[2], "fsdp", scatter_dimension=0, tiled=True),
    )
    final_in_a, final_mid_a, final_out_a, final_proj_a, final_in_b, final_mid_b, final_out_b = (
        lax.psum(part_in_a.astype(jnp.bfloat16), "dp").astype(jnp.float32),
        lax.psum(part_mid_a.astype(jnp.bfloat16), "dp").astype(jnp.float32),
        lax.psum(part_out_a.astype(jnp.bfloat16), "dp").astype(jnp.float32),
        lax.psum(part_proj_a.astype(jnp.bfloat16), "dp").astype(jnp.float32),
        lax.psum(part_in_b.astype(jnp.bfloat16), "dp").astype(jnp.float32),
        lax.psum(part_mid_b.astype(jnp.bfloat16), "dp").astype(jnp.float32),
        lax.psum(part_out_b.astype(jnp.bfloat16), "dp").astype(jnp.float32),
    )
    return (
        result.astype(jnp.bfloat16),
        grad_inputs.astype(jnp.bfloat16),
        final_in_a,
        final_mid_a,
        final_out_a,
        final_proj_a,
        own_shard(norms_a[0]),
        own_shard(norms_a[1]),
        own_shard(norms_a[2]),
        own_shard(norms_a[3]),
        final_in_b,
        final_mid_b,
        final_out_b,
        own_shard(norms_b[0]),
        own_shard(norms_b[1]),
        own_shard(norms_b[2]),
    )


def solution(mesh):
    in_specs = (
        P(("fsdp", "dp"), None, None, None),
        P(("fsdp", "dp")),
        P(),
        P(("fsdp", "dp")),
        P("fsdp", None),
        P("fsdp", None),
        P("fsdp", None),
        P("fsdp", None),
        P(None, "fsdp"),
        P(None, "fsdp"),
        P(None, "fsdp"),
        P(None, "fsdp"),
        P("fsdp", None),
        P("fsdp", None),
        P("fsdp", None),
        P(None, "fsdp"),
        P(None, "fsdp"),
        P(None, "fsdp"),
        P(("fsdp", "dp"), None, None, None),
    )
    out_specs = (
        P(("fsdp", "dp"), None, None, None),
        P(("fsdp", "dp"), None, None, None),
        P("fsdp", None),
        P("fsdp", None),
        P("fsdp", None),
        P("fsdp", None),
        P(None, "fsdp"),
        P(None, "fsdp"),
        P(None, "fsdp"),
        P(None, "fsdp"),
        P("fsdp", None),
        P("fsdp", None),
        P("fsdp", None),
        P(None, "fsdp"),
        P(None, "fsdp"),
        P(None, "fsdp"),
    )
    return jax.shard_map(body, mesh=mesh, in_specs=in_specs, out_specs=out_specs, check_vma=False)
```

profile of v0, /device:TPU:1, one launch (start us, length us, event | category | flops | bytes accessed | tf_op | source)
XLA Modules:
  0.0 1693.7 jit_solution(16078921555230461731)
XLA Ops:
  12.0 17.9 %all_gather.62 = bf16[2,2048]{1,0:T(2,128)(2,1)S(1)} all-gather(bf16[2,256]{1,0:T(2,128)(2,1)S(1)} %copy-done.51), channel_id=1, replica_groups=mesh['fsdp'=8,'dp'=4] {'fsdp'}, dimensions={1}, use_global_device_ids=true | all-gather | bytes 9216 | tf_op jit(solution)/shard_map/all_gather | solution.py:386
  43.5 15.0 all_gather.69
  75.4 15.0 all-gather.1
  123.8 64.0 %all-reduce.32 = (f32[512]{0:T(512)S(1)}, f32[2]{0:T(128)S(1)}, f32[512]{0:T(512)S(1)}) all-reduce(f32[512]{0:T(512)S(1)} %get-tuple-element.67, f32[2]{0:T(128)S(1)} %add_convert_fusion, f32[512]{0:T(512)S(1)} %get-tuple-element.66), channel_id=1, replica_groups=mesh['fsdp'=8,'dp'=4] {'fsdp','dp'}, use_global_device_ids=true, to_apply=%region_6.7 | all-reduce | flops 1026 | bytes 8208 | tf_op jit(solution)/shard_map/psum | solution.py:35
  212.4 40.4 %all-reduce.31 = (f32[512]{0:T(512)S(1)}, f32[512]{0:T(512)S(1)}) all-reduce(f32[512]{0:T(512)S(1)} %get-tuple-element.81, f32[512]{0:T(512)S(1)} %get-tuple-element.80), channel_id=1, replica_groups=mesh['fsdp'=8,'dp'=4] {'fsdp','dp'}, use_global_device_ids=true, to_apply=%region_10.11 | all-reduce | flops 1024 | bytes 8192 | tf_op jit(solution)/shard_map/psum | solution.py:35
  260.6 41.2 %all-reduce.30 = (f32[4096]{0:T(1024)S(1)}, f32[4096]{0:T(1024)S(1)}) all-reduce(f32[4096]{0:T(1024)S(1)} %get-tuple-element.65, f32[4096]{0:T(1024)S(1)} %get-tuple-element.64), channel_id=1, replica_groups=mesh['fsdp'=8,'dp'=4] {'fsdp','dp'}, use_global_device_ids=true, to_apply=%region_12.13 | all-reduce | flops 8192 | bytes 65536 | tf_op jit(solution)/shard_map/psum | solution.py:35
  312.3 41.2 %all-reduce.29 = (f32[512]{0:T(512)S(1)}, f32[512]{0:T(512)S(1)}) all-reduce(f32[512]{0:T(512)S(1)} %get-tuple-element.79, f32[512]{0:T(512)S(1)} %get-tuple-element.78), channel_id=1, replica_groups=mesh['fsdp'=8,'dp'=4] {'fsdp','dp'}, use_global_device_ids=true, to_apply=%region_18.19 | all-reduce | flops 1024 | bytes 8192 | tf_op jit(solution)/shard_map/psum | solution.py:35
  361.5 28.0 %all-gather.22.cloned.1.call-done = bf16[4608,512]{1,0:T(8,128)(2,1)} async-done(((bf16[576,512]{1,0:T(8,128)(2,1)}), bf16[4608,512]{1,0:T(8,128)(2,1)}) %all-gather.22.cloned.1.call-update) | async-done | bytes 4718608 | tf_op jit(solution)/shard_map/all_gather | solution.py:394
  394.7 40.1 %all-reduce.28 = (f32[512]{0:T(512)S(1)}, f32[512]{0:T(512)S(1)}) all-reduce(f32[512]{0:T(512)S(1)} %get-tuple-element.77, f32[512]{0:T(512)S(1)} %get-tuple-element.76), channel_id=1, replica_groups=mesh['fsdp'=8,'dp'=4] {'fsdp','dp'}, use_global_device_ids=true, to_apply=%region_22.23 | all-reduce | flops 1024 | bytes 8192 | tf_op jit(solution)/shard_map/psum | solution.py:35
  443.7 40.1 %all-reduce.27 = (f32[2048]{0:T(1024)S(1)}, f32[2048]{0:T(1024)S(1)}) all-reduce(f32[2048]{0:T(1024)S(1)} %get-tuple-element.69, f32[2048]{0:T(1024)S(1)} %get-tuple-element.68), channel_id=1, replica_groups=mesh['fsdp'=8,'dp'=4] {'fsdp','dp'}, use_global_device_ids=true, to_apply=%region_26.27 | all-reduce | flops 4096 | bytes 32768 | tf_op jit(solution)/shard_map/psum | solution.py:35
  489.7 39.6 %all-reduce.26 = (f32[2048]{0:T(1024)S(1)}, f32[2048]{0:T(1024)S(1)}) all-reduce(f32[2048]{0:T(1024)S(1)} %get-tuple-element.71, f32[2048]{0:T(1024)S(1)} %get-tuple-element.70), channel_id=1, replica_groups=mesh['fsdp'=8,'dp'=4] {'fsdp','dp'}, use_global_device_ids=true, to_apply=%region_30.31 | all-reduce | flops 4096 | bytes 32768 | tf_op jit(solution)/shard_map/psum | solution.py:58
  535.6 40.5 %all-reduce.25 = (f32[512]{0:T(512)S(1)}, f32[512]{0:T(512)S(1)}) all-reduce(f32[512]{0:T(512)S(1)} %get-tuple-element.87, f32[512]{0:T(512)S(1)} %get-tuple-element.86), channel_id=1, replica_groups=mesh['fsdp'=8,'dp'=4] {'fsdp','dp'}, use_global_device_ids=true, to_apply=%region_34.35 | all-reduce | flops 1024 | bytes 8192 | tf_op jit(solution)/shard_map/psum | solution.py:58
  585.2 39.4 %all-reduce.24 = (f32[512]{0:T(512)S(1)}, f32[512]{0:T(512)S(1)}) all-reduce(f32[512]{0:T(512)S(1)} %get-tuple-element.85, f32[512]{0:T(512)S(1)} %get-tuple-element.84), channel_id=1, replica_groups=mesh['fsdp'=8,'dp'=4] {'fsdp','dp'}, use_global_device_ids=true, to_apply=%region_38.39 | all-reduce | flops 1024 | bytes 8192 | tf_op jit(solution)/shard_map/psum | solution.py:58
  632.8 41.0 %all-reduce.23 = (f32[4096]{0:T(1024)S(1)}, f32[4096]{0:T(1024)S(1)}) all-reduce(f32[4096]{0:T(1024)S(1)} %get-tuple-element.75, f32[4096]{0:T(1024)S(1)} %get-tuple-element.74), channel_id=1, replica_groups=mesh['fsdp'=8,'dp'=4] {'fsdp','dp'}, use_global_device_ids=true, to_apply=%region_42.43 | all-reduce | flops 8192 | bytes 65536 | tf_op jit(solution)/shard_map/psum | solution.py:58
  680.1 39.4 %all-reduce.22 = (f32[512]{0:T(512)S(1)}, f32[512]{0:T(512)S(1)}) all-reduce(f32[512]{0:T(512)S(1)} %get-tuple-element.83, f32[512]{0:T(512)S(1)} %get-tuple-element.82), channel_id=1, replica_groups=mesh['fsdp'=8,'dp'=4] {'fsdp','dp'}, use_global_device_ids=true, to_apply=%region_46.47 | all-reduce | flops 1024 | bytes 8192 | tf_op jit(solution)/shard_map/psum | solution.py:58
  738.5 40.8 %all-reduce.21 = (f32[512]{0:T(512)S(1)}, f32[512]{0:T(512)S(1)}) all-reduce(f32[512]{0:T(512)S(1)} %get-tuple-element.73, f32[512]{0:T(512)S(1)} %get-tuple-element.72), channel_id=1, replica_groups=mesh['fsdp'=8,'dp'=4] {'fsdp','dp'}, use_global_device_ids=true, to_apply=%region_50.51 | all-reduce | flops 1024 | bytes 8192 | tf_op jit(solution)/shard_map/psum | solution.py:58
  832.0 15.9 pad.100
  855.5 90.8 %reduce-scatter.12.cloned.1.call-done = f32[64,2048]{1,0:T(8,128)} async-done(((f32[512,2048]{1,0:T(8,128)}), f32[64,2048]{1,0:T(8,128)}) %reduce-scatter.12.cloned.1.call-update) | async-done | bytes 524304 | tf_op jit(solution)/shard_map/reduce_scatter | solution.py:442
  948.1 90.0 %reduce-scatter.16.cloned.1.call-done = f32[256,512]{1,0:T(8,128)} async-done(((f32[2048,512]{1,0:T(8,128)}), f32[256,512]{1,0:T(8,128)}) %reduce-scatter.16.cloned.1.call-update) | async-done | bytes 524304 | tf_op jit(solution)/shard_map/reduce_scatter | solution.py:444
  1039.9 89.7 %reduce-scatter.20.cloned.1.call-done = f32[64,2048]{1,0:T(8,128)} async-done(((f32[512,2048]{1,0:T(8,128)}), f32[64,2048]{1,0:T(8,128)}) %reduce-scatter.20.cloned.1.call-update) | async-done | bytes 524304 | tf_op jit(solution)/shard_map/reduce_scatter | solution.py:446
  1131.3 151.0 %reduce-scatter.14.cloned.1.call-done = f32[128,2048]{1,0:T(8,128)} async-done(((f32[1024,2048]{1,0:T(8,128)}), f32[128,2048]{1,0:T(8,128)}) %reduce-scatter.14.cloned.1.call-update) | async-done | bytes 1048592 | tf_op jit(solution)/shard_map/reduce_scatter | solution.py:443
  1284.4 164.0 %reduce-scatter.10.cloned.1.call-done = f32[576,512]{1,0:T(8,128)} async-done(((f32[4608,512]{1,0:T(8,128)}), f32[576,512]{1,0:T(8,128)}) %reduce-scatter.10.cloned.1.call-update) | async-done | bytes 1179664 | tf_op jit(solution)/shard_map/reduce_scatter | solution.py:441
  1450.6 163.7 %reduce-scatter.18.cloned.1.call-done = f32[576,512]{1,0:T(8,128)} async-done(((f32[4608,512]{1,0:T(8,128)}), f32[576,512]{1,0:T(8,128)}) %reduce-scatter.18.cloned.1.call-update) | async-done | bytes 1179664 | tf_op jit(solution)/shard_map/reduce_scatter | solution.py:445
  1624.3 53.7 %all-reduce.36.cloned.1.call-done = (bf16[128,512]{1,0:T(8,128)(2,1)}, bf16[576,512]{1,0:T(8,128)(2,1)}, bf16[64,2048]{1,0:T(8,128)(2,1)}, bf16[128,2048]{1,0:T(...) async-done(((bf16[128,512]{1,0:T(8,128)(2,1)}, bf16[576,512]{1,0:T(8,128)(2,1)}, bf16[64,2048]{1,0:T(8,128)(2,1)}, ...) | async-done | bytes 2621456 | tf_op jit(solution)/shard_map/psum | solution.py:449
  (320 shorter events, 275.8 us)
Async XLA Ops:
  7.2 35.6 %copy-start.58 = (s32[4]{0:T(128)S(1)}, s32[4]{0:T(128)}, u32[]{:S(2)}) copy-start(s32[4]{0:T(128)} %param.20) | copy-start | bytes 52
  7.2 36.3 %copy-start.53 = (bf16[2,256]{1,0:T(2,128)(2,1)S(1)}, bf16[2,256]{1,0:T(2,128)(2,1)}, u32[]{:S(2)}) copy-start(bf16[2,256]{1,0:T(2,128)(2,1)} %param.36) | copy-start | bytes 3076
  7.2 51.4 %copy-start.61 = (s32[4]{0:T(128)S(1)}, s32[4]{0:T(128)}, u32[]{:S(2)}) copy-start(s32[4]{0:T(128)} %param.22) | copy-start | bytes 52
  7.2 51.8 %copy-start.15 = (bf16[4,14,14,1024]{3,0,2,1:T(4,128)(2,1)S(1)}, bf16[4,14,14,1024]{3,0,2,1:T(4,128)(2,1)}, u32[]{:S(2)}) copy-start(bf16[4,14,14,1024]{3,0,2,1:T(4,128)(2,1)} %param.19) | copy-start | bytes 4816900
  7.2 113.5 %all-gather.12.cloned.1.call-start = ((), (), s32[]{:S(2)}) async-start(), calls=%async_computation.7 | async-start | bytes 1179648 | tf_op jit(solution)/shard_map/all_gather | solution.py:380
  8.0 192.0 %all-gather.18.cloned.1.call-start = ((), (), s32[]{:S(2)}) async-start(), calls=%async_computation.10 | async-start | bytes 4718592 | tf_op jit(solution)/shard_map/all_gather | solution.py:383
  8.7 198.4 %all-gather.14.cloned.1.call-start = ((), (), s32[]{:S(2)}) async-start(), calls=%async_computation.8 | async-start | bytes 5308416 | tf_op jit(solution)/shard_map/all_gather | solution.py:381
  9.5 247.3 %all-gather.16.cloned.1.call-start = ((), (), s32[]{:S(2)}) async-start(), calls=%async_computation.9 | async-start | bytes 2359296 | tf_op jit(solution)/shard_map/all_gather | solution.py:382
  10.0 299.0 %all-gather.20.cloned.1.call-start = ((), (), s32[]{:S(2)}) async-start(), calls=%async_computation.11 | async-start | bytes 2359296 | tf_op jit(solution)/shard_map/all_gather | solution.py:393
  10.6 378.8 %all-gather.22.cloned.1.call-start = ((), (), s32[]{:S(2)}) async-start(), calls=%async_computation.12 | async-start | bytes 5308416 | tf_op jit(solution)/shard_map/all_gather | solution.py:394
  11.2 428.4 %all-gather.24.cloned.1.call-start = ((), (), s32[]{:S(2)}) async-start(), calls=%async_computation.13 | async-start | bytes 2359296 | tf_op jit(solution)/shard_map/all_gather | solution.py:395
  11.9 842.0 %reduce-scatter.8.cloned.1.call-start = ((), (), s32[]{:S(2)}) async-start(), calls=%async_computation.14 | async-start | bytes 2359296 | tf_op jit(solution)/shard_map/reduce_scatter | solution.py:440
  58.8 721.1 %copy-start.17 = (f32[4,14,14]{2,1,0:T(8,128)}, f32[4,14,14]{2,1,0:T(8,128)S(1)}, u32[]{:S(2)}) copy-start(f32[4,14,14]{2,1,0:T(8,128)S(1)} %get-tuple-element.191) | copy-start | bytes 9412
  59.1 45.2 %copy-start.57 = (bf16[2,64]{1,0:T(2,128)(2,1)S(1)}, bf16[2,64]{1,0:T(2,128)(2,1)}, u32[]{:S(2)}) copy-start(bf16[2,64]{1,0:T(2,128)(2,1)} %param.35) | copy-start | bytes 772
  123.8 66.0 %copy-start.3 = (f32[4,14,14,512]{3,2,1,0:T(8,128)}, f32[4,14,14,512]{3,2,1,0:T(8,128)S(1)}, u32[]{:S(2)}) copy-start(f32[4,14,14,512]{3,2,1,0:T(8,128)S(1)} %get-tuple-element.193) | copy-start | bytes 4816900
  212.4 47.0 %copy-start.27 = (f32[4,7,7,512]{3,2,1,0:T(8,128)}, f32[4,7,7,512]{3,2,1,0:T(8,128)S(1)}, u32[]{:S(2)}) copy-start(f32[4,7,7,512]{3,2,1,0:T(8,128)S(1)} %get-tuple-element.194) | copy-start | bytes 1204228
  394.7 138.7 %copy-start.29 = (f32[4,7,7,512]{3,2,1,0:T(8,128)}, f32[4,7,7,512]{3,2,1,0:T(8,128)S(1)}, u32[]{:S(2)}) copy-start(f32[4,7,7,512]{3,2,1,0:T(8,128)S(1)} %get-tuple-element.196) | copy-start | bytes 1204228
  786.7 159.6 %reduce-scatter.12.cloned.1.call-start = ((), (), s32[]{:S(2)}) async-start(), calls=%async_computation.16 | async-start | bytes 4718592 | tf_op jit(solution)/shard_map/reduce_scatter | solution.py:442
  791.3 246.7 %reduce-scatter.16.cloned.1.call-start = ((), (), s32[]{:S(2)}) async-start(), calls=%async_computation.18 | async-start | bytes 4718592 | tf_op jit(solution)/shard_map/reduce_scatter | solution.py:444
  795.9 333.7 %reduce-scatter.20.cloned.1.call-start = ((), (), s32[]{:S(2)}) async-start(), calls=%async_computation.20 | async-start | bytes 4718592 | tf_op jit(solution)/shard_map/reduce_scatter | solution.py:446
  800.4 481.9 %reduce-scatter.14.cloned.1.call-start = ((), (), s32[]{:S(2)}) async-start(), calls=%async_computation.17 | async-start | bytes 9437184 | tf_op jit(solution)/shard_map/reduce_scatter | solution.py:443
  807.1 641.3 %reduce-scatter.10.cloned.1.call-start = ((), (), s32[]{:S(2)}) async-start(), calls=%async_computation.15 | async-start | bytes 10616832 | tf_op jit(solution)/shard_map/reduce_scatter | solution.py:441
  815.5 798.8 %reduce-scatter.18.cloned.1.call-start = ((), (), s32[]{:S(2)}) async-start(), calls=%async_computation.19 | async-start | bytes 10616832 | tf_op jit(solution)/shard_map/reduce_scatter | solution.py:445
  823.8 854.2 %all-reduce.36.cloned.1.call-start = ((), (), s32[]{:S(2)}) async-start(), calls=%async_computation.21 | async-start | bytes 5242880 | tf_op jit(solution)/shard_map/psum | solution.py:449
  (53 other events, 257.3 us)
Sparse Core Ops, SparseCore 0:
  10.2 41.3 all-gather.11
  53.7 72.1 all-gather.17
  128.1 79.0 all-gather.13
  209.1 47.5 all-gather.15
  258.7 48.4 all-gather.19
  309.3 80.1 all-gather.21
  391.6 48.0 all-gather.23
  786.8 66.8 reduce-scatter.7
  857.3 88.9 reduce-scatter.11
  950.2 87.8 reduce-scatter.15
  1041.7 87.7 reduce-scatter.19
  1133.5 148.7 reduce-scatter.13
  1285.9 162.4 reduce-scatter.9
  1451.8 162.3 reduce-scatter.17
  1618.1 59.7 all-reduce.35
where the time goes:
time: 1710 us; the launch traced here: 1690 us
  waiting for transfers between devices  846 us (49%)
  blocking collectives  609 us (36%)
  matrix products  84.6 us (5%)
  other arithmetic  72 us (4%)
  local copies, waits for them, and re-layouts  65.7 us (4%)
    psum x6, blocking collectives, norm_stats(): lax.psum((jnp.sum(hidden * pixel_mask, axis=(0, 1, 2)), jnp.sum(hidden *...  267 us
    psum x6, blocking collectives, norm_backward(): lax.psum((jnp.sum(grad_norm, axis=(0, 1, 2)), jnp.sum(grad_norm * scaled,...  241 us
    reduce_scatter x1, waiting for transfers between devices, body(): lax.psum_scatter(grads_a[1], 'fsdp', scatter_dimension=0, tiled=True)  164 us
    reduce_scatter x1, waiting for transfers between devices, body(): lax.psum_scatter(grads_b[1], 'fsdp', scatter_dimension=0, tiled=True)  164 us
    reduce_scatter x1, waiting for transfers between devices, body(): lax.psum_scatter(grads_a[3], 'fsdp', scatter_dimension=0, tiled=True)  151 us
    reduce_scatter x1, waiting for transfers between devices, body(): lax.psum_scatter(grads_a[2], 'fsdp', scatter_dimension=0, tiled=True)  90.8 us
    reduce_scatter x1, waiting for transfers between devices, body(): lax.psum_scatter(grads_b[0], 'fsdp', scatter_dimension=0, tiled=True)  90 us
    reduce_scatter x1, waiting for transfers between devices, body(): lax.psum_scatter(grads_b[2], 'fsdp', scatter_dimension=0, tiled=True)  89.7 us
  transfers between devices with their start and end apart: 15, of which 11 were waited for; matrix products, arithmetic and copies ran while one was open for 8% of the time, Pallas kernels for 0%

commit v1 on v0

--- a/solution.py
+++ b/solution.py
@@ -1,9 +1,444 @@
+import functools
+
 import jax
 import jax.numpy as jnp
 from jax import lax
+from jax.experimental import pallas as pl
+from jax.experimental.pallas import tpu as pltpu
 from jax.sharding import PartitionSpec as P
 
 EPSILON = 1e-05
+BY_MESH = pl.DeviceIdType.MESH
+
+
+def flip(index, bits):
+    out = index
+    for bit in (1, 2, 4):
+        if bits & bit:
+            out = out + bit - 2 * bit * ((index // bit) % 2)
+    return out
+
+
+class Place:
+    def __init__(self):
+        self.f = lax.axis_index("fsdp")
+        self.d = lax.axis_index("dp")
+        self.y = self.f % 2
+        self.z = self.f // 2
+        self.c = self.d % 2
+        self.x = self.d // 2
+
+    def peer(self, f_bits, d_bits):
+        return (flip(self.f, f_bits), flip(self.d, d_bits))
+
+
+def enter(place, peers):
+    barrier = pltpu.get_barrier_semaphore()
+    for f_bits, d_bits in peers:
+        pl.semaphore_signal(barrier, inc=1, device_id=place.peer(f_bits, d_bits), device_id_type=BY_MESH)
+    pl.semaphore_wait(barrier, len(peers))
+
+
+def push(source, target, send_sem, recv_sem, device):
+    pltpu.make_async_remote_copy(
+        src_ref=source,
+        dst_ref=target,
+        send_sem=send_sem,
+        recv_sem=recv_sem,
+        device_id=device,
+        device_id_type=BY_MESH,
+    ).start()
+
+
+def await_bytes(view, sem):
+    pltpu.make_async_copy(view, view, sem).wait()
+
+
+def rows_of(start, size):
+    return pl.ds(pl.multiple_of(start, 16), size)
+
+
+def cols_of(start, size):
+    return pl.ds(pl.multiple_of(start, 128), size)
+
+
+LINK_PEERS = ((2, 0), (4, 0), (6, 0), (1, 0), (0, 2), (0, 1))
+
+
+def split_of(columns):
+    half = columns // 2
+    return half // 2
+
+
+def gather_steps(place, shard, whole, local_sem, send, recv):
+    rows, columns = shard.shape
+    half = columns // 2
+    wide_a = split_of(columns)
+    wide_b = half - wide_a
+    part = rows // 2
+    col_0 = place.c * half
+    col_b = col_0 + wide_a
+    row_q = place.x * part
+    mine = place.f * rows
+    pltpu.make_async_copy(
+        shard.at[:, cols_of(col_0, half)], whole.at[rows_of(mine, rows), cols_of(col_0, half)], local_sem
+    ).start()
+    for bits in (2, 4, 6):
+        push(
+            shard.at[rows_of(row_q, part), cols_of(col_0, half)],
+            whole.at[rows_of(mine + row_q, part), cols_of(col_0, half)],
+            send.at[0],
+            recv.at[0],
+            place.peer(bits, 0),
+        )
+    yield
+    await_bytes(whole.at[pl.ds(0, rows), pl.ds(0, half)], local_sem)
+    await_bytes(whole.at[pl.ds(0, 3 * part), pl.ds(0, half)], recv.at[0])
+    for bits in (0, 2, 4, 6):
+        block = whole.at[rows_of(flip(place.f, bits) * rows + row_q, part), cols_of(col_0, wide_a)]
+        push(block, block, send.at[1], recv.at[1], place.peer(1, 0))
+    for bits in (2, 4, 6):
+        block = whole.at[rows_of(flip(place.f, bits) * rows + row_q, part), cols_of(col_b, wide_b)]
+        push(block, block, send.at[2], recv.at[2], place.peer(0, 2))
+    yield
+    await_bytes(whole.at[pl.ds(0, 4 * part), pl.ds(0, wide_a)], recv.at[1])
+    await_bytes(whole.at[pl.ds(0, 3 * part), pl.ds(0, wide_b)], recv.at[2])
+    for bits in range(1, 8):
+        block = whole.at[rows_of(flip(place.f, bits) * rows + row_q, part), cols_of(col_0, wide_a)]
+        push(block, block, send.at[3], recv.at[3], place.peer(0, 2))
+    for bits in (0, 2, 4, 6):
+        block = whole.at[rows_of(flip(place.f, bits) * rows, rows), cols_of(col_b, wide_b)]
+        push(block, block, send.at[4], recv.at[4], place.peer(1, 0))
+    yield
+    await_bytes(whole.at[pl.ds(0, 7 * part), pl.ds(0, wide_a)], recv.at[3])
+    await_bytes(whole.at[pl.ds(0, 4 * rows), pl.ds(0, wide_b)], recv.at[4])
+    block = whole.at[:, cols_of(col_0, half)]
+    push(block, block, send.at[5], recv.at[5], place.peer(0, 1))
+    yield
+    await_bytes(whole.at[:, pl.ds(0, half)], recv.at[5])
+
+
+def gather_sent(shard, whole, send):
+    rows, columns = shard.shape
+    half = columns // 2
+    wide_a = split_of(columns)
+    wide_b = half - wide_a
+    part = rows // 2
+    await_bytes(whole.at[pl.ds(0, 3 * part), pl.ds(0, half)], send.at[0])
+    await_bytes(whole.at[pl.ds(0, 4 * part), pl.ds(0, wide_a)], send.at[1])
+    await_bytes(whole.at[pl.ds(0, 3 * part), pl.ds(0, wide_b)], send.at[2])
+    await_bytes(whole.at[pl.ds(0, 7 * part), pl.ds(0, wide_a)], send.at[3])
+    await_bytes(whole.at[pl.ds(0, 4 * rows), pl.ds(0, wide_b)], send.at[4])
+    await_bytes(whole.at[:, pl.ds(0, half)], send.at[5])
+
+
+def add_rows(target, source, total, chunk):
+    def step(index, carry):
+        start = pl.multiple_of(index * chunk, chunk)
+        into = target(start, chunk)
+        into[...] = (into[...].astype(jnp.float32) + source(start, chunk)[...].astype(jnp.float32)).astype(into.dtype)
+        return carry
+
+    lax.fori_loop(0, total // chunk, step, 0)
+
+
+def scatter_steps(place, grad, room, out, send, recv):
+    from_core, from_x, from_y, from_y2, from_x2, from_z = room
+    total_rows, columns = grad.shape
+    rows = total_rows // 8
+    half = columns // 2
+    wide_a = split_of(columns)
+    wide_b = half - wide_a
+    part = rows // 2
+    col_0 = place.c * half
+    col_1 = half - col_0
+    row_q = place.x * part
+    row_o = part - row_q
+    chunk = 32 if part % 32 == 0 else 16
+    push(grad.at[:, cols_of(col_1, half)], from_core, send.at[0], recv.at[0], place.peer(0, 1))
+    yield
+    await_bytes(from_core, recv.at[0])
+    add_rows(
+        lambda s, n: from_core.at[pl.ds(s, n)],
+        lambda s, n: grad.at[pl.ds(s, n), cols_of(col_0, half)],
+        total_rows,
+        chunk,
+    )
+    for block in range(8):
+        push(
+            from_core.at[rows_of(block * rows + row_o, part), pl.ds(0, wide_a)],
+            from_x.at[pl.ds(block * part, part)],
+            send.at[1],
+            recv.at[1],
+            place.peer(0, 2),
+        )
+    for level in range(4):
+        push(
+            from_core.at[rows_of((2 * level + 1 - place.y) * rows, rows), pl.ds(wide_a, wide_b)],
+            from_y.at[pl.ds(level * rows, rows)],
+            send.at[2],
+            recv.at[2],
+            place.peer(1, 0),
+        )
+    yield
+    await_bytes(from_x, recv.at[1])
+    await_bytes(from_y, recv.at[2])
+
+    def fold_x(block, carry):
+        add_rows(
+            lambda s, n: from_core.at[rows_of(block * rows + row_q + s, n), pl.ds(0, wide_a)],
+            lambda s, n: from_x.at[rows_of(block * part + s, n)],
+            part,
+            chunk,
+        )
+        return carry
+
+    lax.fori_loop(0, 8, fold_x, 0)
+
+    def fold_y(level, carry):
+        add_rows(
+            lambda s, n: from_core.at[rows_of((2 * level + place.y) * rows + s, n), pl.ds(wide_a, wide_b)],
+            lambda s, n: from_y.at[rows_of(level * rows + s, n)],
+            rows,
+            chunk,
+        )
+        return carry
+
+    lax.fori_loop(0, 4, fold_y, 0)
+    for level in range(4):
+        push(
+            from_core.at[rows_of((2 * level + 1 - place.y) * rows + row_q, part), pl.ds(0, wide_a)],
+            from_y2.at[pl.ds(level * part, part)],
+            send.at[3],
+            recv.at[3],
+            place.peer(1, 0),
+        )
+        push(
+            from_core.at[rows_of((2 * level + place.y) * rows + row_o, part), pl.ds(wide_a, wide_b)],
+            from_x2.at[pl.ds(level * part, part)],
+            send.at[4],
+            recv.at[4],
+            place.peer(0, 2),
+        )
+    yield
+    await_bytes(from_y2, recv.at[3])
+    await_bytes(from_x2, recv.at[4])
+
+    def fold_last(level, carry):
+        own = (2 * level + place.y) * rows + row_q
+        add_rows(
+            lambda s, n: from_core.at[rows_of(own + s, n), pl.ds(0, wide_a)],
+            lambda s, n: from_y2.at[rows_of(level * part + s, n)],
+            part,
+            chunk,
+        )
+        add_rows(
+            lambda s, n: from_core.at[rows_of(own + s, n), pl.ds(wide_a, wide_b)],
+            lambda s, n: from_x2.at[rows_of(level * part + s, n)],
+            part,
+            chunk,
+        )
+        return carry
+
+    lax.fori_loop(0, 4, fold_last, 0)
+    for slot, bits in enumerate((2, 4, 6)):
+        push(
+            from_core.at[rows_of(flip(place.f, bits) * rows + row_q, part)],
+            from_z.at[pl.ds(slot * part, part)],
+            send.at[5],
+            recv.at[5],
+            place.peer(bits, 0),
+        )
+    yield
+    await_bytes(from_z, recv.at[5])
+
+    def fold_z(index, carry):
+        start = pl.multiple_of(index * chunk, chunk)
+        total = from_core[rows_of(place.f * rows + row_q + start, chunk)].astype(jnp.float32)
+        for slot in range(3):
+            total = total + from_z[rows_of(slot * part + start, chunk)].astype(jnp.float32)
+        out[rows_of(row_q + start, chunk), cols_of(col_0, half)] = total.astype(out.dtype)
+        return carry
+
+    lax.fori_loop(0, part // chunk, fold_z, 0)
+    block = out.at[rows_of(row_q, part), cols_of(col_0, half)]
+    push(block, block, send.at[6], recv.at[6], place.peer(0, 2))
+    yield
+    await_bytes(out.at[pl.ds(0, part), pl.ds(0, half)], recv.at[6])
+    block = out.at[:, cols_of(col_0, half)]
+    push(block, block, send.at[7], recv.at[7], place.peer(0, 1))
+    yield
+    await_bytes(out.at[:, pl.ds(0, half)], recv.at[7])
+
+
+def scatter_sent(grad, room, out, send):
+    from_core, from_x, from_y, from_y2, from_x2, from_z = room
+    half = grad.shape[1] // 2
+    for index, view in enumerate((from_core, from_x, from_y, from_y2, from_x2, from_z)):
+        await_bytes(view, send.at[index])
+    await_bytes(out.at[pl.ds(0, out.shape[0] // 2), pl.ds(0, half)], send.at[6])
+    await_bytes(out.at[:, pl.ds(0, half)], send.at[7])
+
+
+def room_shapes(total_rows, columns):
+    rows = total_rows // 8
+    half = columns // 2
+    wide_a = split_of(columns)
+    wide_b = half - wide_a
+    part = rows // 2
+    return [
+        (8 * rows, half),
+        (8 * part, wide_a),
+        (4 * rows, wide_b),
+        (4 * part, wide_a),
+        (4 * part, wide_b),
+        (3 * part, half),
+    ]
+
+
+def run_staggered(steps):
+    alive = list(steps)
+    for one in alive:
+        next(one)
+    begun = 0
+    while any(one is not None for one in alive):
+        begun += 1
+        for index in range(min(begun, len(alive))):
+            if alive[index] is not None and next(alive[index], "end") == "end":
+                alive[index] = None
+
+
+def gather_kernel(*refs):
+    shards, wholes = refs[:7], refs[7:14]
+    local_sem, send, recv = refs[14:]
+    place = Place()
+    enter(place, LINK_PEERS)
+    run_staggered(
+        [
+            gather_steps(place, shards[i], wholes[i], local_sem.at[i], send.at[i], recv.at[i])
+            for i in range(7)
+        ]
+    )
+    for i in range(7):
+        gather_sent(shards[i], wholes[i], send.at[i])
+
+
+def gather_all(shards):
+    shapes = [(8 * one.shape[0], one.shape[1]) for one in shards]
+    return pl.pallas_call(
+        gather_kernel,
+        out_shape=[jax.ShapeDtypeStruct(shape, jnp.bfloat16) for shape in shapes],
+        in_specs=[pl.BlockSpec(memory_space=pl.ANY)] * 7,
+        out_specs=[pl.BlockSpec(memory_space=pltpu.VMEM)] * 7,
+        scratch_shapes=[
+            pltpu.SemaphoreType.DMA((7,)),
+            pltpu.SemaphoreType.DMA((7, 6)),
+            pltpu.SemaphoreType.DMA((7, 6)),
+        ],
+        compiler_params=pltpu.CompilerParams(
+            collective_id=0, has_side_effects=True, vmem_limit_bytes=60 * 2**20
+        ),
+        name="gather_weights",
+    )(*shards)
+
+
+def scatter_kernel(*refs):
+    grads, outs = refs[:7], refs[7:14]
+    rooms = [refs[14 + 6 * i : 20 + 6 * i] for i in range(7)]
+    send, recv = refs[14 + 42 :]
+    place = Place()
+    enter(place, LINK_PEERS)
+    run_staggered(
+        [scatter_steps(place, grads[i], rooms[i], outs[i], send.at[i], recv.at[i]) for i in range(7)]
+    )
+    for i in range(7):
+        scatter_sent(grads[i], rooms[i], outs[i], send.at[i])
+
+
+def scatter_all(grads):
+    shapes = [(one.shape[0] // 8, one.shape[1]) for one in grads]
+    return pl.pallas_call(
+        scatter_kernel,
+        out_shape=[jax.ShapeDtypeStruct(shape, jnp.bfloat16) for shape in shapes],
+        in_specs=[pl.BlockSpec(memory_space=pltpu.VMEM)] * 7,
+        out_specs=[pl.BlockSpec(memory_space=pltpu.VMEM)] * 7,
+        scratch_shapes=[
+            pltpu.VMEM(shape, jnp.bfloat16) for one in grads for shape in room_shapes(*one.shape)
+        ]
+        + [pltpu.SemaphoreType.DMA((7, 8)), pltpu.SemaphoreType.DMA((7, 8))],
+        compiler_params=pltpu.CompilerParams(
+            collective_id=1, has_side_effects=True, vmem_limit_bytes=62 * 2**20
+        ),
+        name="scatter_grads",
+    )(*grads)
+
+
+SUM_PEERS = ((0, 1), (0, 2), (0, 3), (1, 0), (2, 0), (3, 0), (4, 0), (5, 0), (6, 0), (7, 0))
+
+
+def sum_everywhere(place, near, far, send, recv):
+    own = near.at[place.d]
+    for bits in (1, 2, 3):
+        push(own, own, send.at[0], recv.at[0], place.peer(0, bits))
+    await_bytes(near.at[pl.ds(0, 3)], recv.at[0])
+    own_far = far.at[place.f]
+    own_far[...] = (near[0] + near[1]) + (near[2] + near[3])
+    for bits in range(1, 8):
+        push(own_far, own_far, send.at[1], recv.at[1], place.peer(bits, 0))
+    await_bytes(far.at[pl.ds(0, 7)], recv.at[1])
+    total = far[0]
+    for index in range(1, 8):
+        total = total + far[index]
+    await_bytes(near.at[pl.ds(0, 3)], send.at[0])
+    await_bytes(far.at[pl.ds(0, 7)], send.at[1])
+    return total
+
+
+def sum_kernel(local, out, near, far, send, recv):
+    place = Place()
+    near[place.d] = local[...]
+    enter(place, SUM_PEERS)
+    out[...] = sum_everywhere(place, near, far, send, recv)
+
+
+def sum_call(local, index):
+    rows = local.shape[0]
+    return pl.pallas_call(
+        sum_kernel,
+        out_shape=jax.ShapeDtypeStruct(local.shape, jnp.float32),
+        in_specs=[pl.BlockSpec(memory_space=pltpu.VMEM)],
+        out_specs=pl.BlockSpec(memory_space=pltpu.VMEM),
+        scratch_shapes=[
+            pltpu.VMEM((4, rows, 128), jnp.float32),
+            pltpu.VMEM((8, rows, 128), jnp.float32),
+            pltpu.SemaphoreType.DMA((2,)),
+            pltpu.SemaphoreType.DMA((2,)),
+        ],
+        compiler_params=pltpu.CompilerParams(collective_id=2 + index, has_side_effects=True),
+        name="sum_all",
+    )(local)
+
+
+def gather_plain(shards):
+    return [lax.all_gather(one, "fsdp", axis=0, tiled=True) for one in shards]
+
+
+def scatter_plain(grads):
+    parts = [lax.psum_scatter(one, "fsdp", scatter_dimension=0, tiled=True) for one in grads]
+    return lax.psum(tuple(parts), "dp")
+
+
+MODE = {"fast": True, "calls": 0}
+
+
+def sum_pair(first, second):
+    width = first.shape[0]
+    if not MODE["fast"]:
+        return lax.psum((first, second), ("fsdp", "dp"))
+    packed = jnp.concatenate([first, second]).reshape(2 * width // 128, 128)
+    MODE["calls"] += 1
+    total = sum_call(packed, MODE["calls"] - 1).reshape(2, width)
+    return total[0], total[1]
 
 
 def silu_slope(values):
@@ -32,15 +467,11 @@
 
 
 def norm_stats(hidden, pixel_mask, local_counts, count_slot):
-    sum_values, sum_squares, totals = lax.psum(
-        (
-            jnp.sum(hidden * pixel_mask, axis=(0, 1, 2)),
-            jnp.sum(hidden * hidden * pixel_mask, axis=(0, 1, 2)),
-            local_counts,
-        ),
-        ("fsdp", "dp"),
-    )
-    pixel_total = totals[count_slot]
+    sum_values, sum_squares = sum_pair(
+        jnp.sum(hidden * pixel_mask, axis=(0, 1, 2)),
+        jnp.sum(hidden * hidden * pixel_mask, axis=(0, 1, 2)),
+    )
+    pixel_total = local_counts[count_slot]
     average = sum_values / pixel_total
     inv_std = lax.rsqrt(sum_squares / pixel_total - average * average + EPSILON)
     return (average, inv_std, pixel_total)
@@ -55,9 +486,8 @@
 
 def norm_backward(grad_norm, scaled, stats_now, params, pixel_mask):
     average, inv_std, pixel_total = stats_now
-    shift_sum, gain_sum = lax.psum(
-        (jnp.sum(grad_norm, axis=(0, 1, 2)), jnp.sum(grad_norm * scaled, axis=(0, 1, 2))),
-        ("fsdp", "dp"),
+    shift_sum, gain_sum = sum_pair(
+        jnp.sum(grad_norm, axis=(0, 1, 2)), jnp.sum(grad_norm * scaled, axis=(0, 1, 2))
     )
     gain_row = params[0].astype(jnp.float32)
     grad_hidden = (
@@ -376,83 +806,42 @@
     channel_b = (lane_ids < widths[1]).astype(jnp.float32)
     depth_gate = keep_gate.astype(jnp.float32)[:, None, None, None]
     inputs = images * mask_in.astype(jnp.bfloat16)
-    weights_a = (
-        lax.all_gather(w_in_a, "fsdp", axis=0, tiled=True),
-        lax.all_gather(w_mid_a, "fsdp", axis=0, tiled=True),
-        lax.all_gather(w_out_a, "fsdp", axis=0, tiled=True),
-        lax.all_gather(w_proj_a, "fsdp", axis=0, tiled=True),
-        lax.all_gather(norm_in_a, "fsdp", axis=1, tiled=True),
-        lax.all_gather(norm_mid_a, "fsdp", axis=1, tiled=True),
-        lax.all_gather(norm_out_a, "fsdp", axis=1, tiled=True),
-        lax.all_gather(norm_proj_a, "fsdp", axis=1, tiled=True),
-    )
-    block_out, stats_a, unused_a = block_a_forward(
-        inputs, weights_a, mask_in, mask_out, local_counts, channel_a, None
-    )
-    weights_b = (
-        lax.all_gather(w_in_b, "fsdp", axis=0, tiled=True),
-        lax.all_gather(w_mid_b, "fsdp", axis=0, tiled=True),
-        lax.all_gather(w_out_b, "fsdp", axis=0, tiled=True),
-        lax.all_gather(norm_in_b, "fsdp", axis=1, tiled=True),
-        lax.all_gather(norm_mid_b, "fsdp", axis=1, tiled=True),
-        lax.all_gather(norm_out_b, "fsdp", axis=1, tiled=True),
-    )
-    result, stats_b, unused_b = block_b_forward(
-        block_out, weights_b, mask_out, local_counts, channel_b, depth_gate, None
-    )
-    backward_b = (
-        lax.all_gather(w_in_b, "fsdp", axis=0, tiled=True),
-        lax.all_gather(w_mid_b, "fsdp", axis=0, tiled=True),
-        lax.all_gather(w_out_b, "fsdp", axis=0, tiled=True),
-        lax.all_gather(norm_in_b, "fsdp", axis=1, tiled=True),
-        lax.all_gather(norm_mid_b, "fsdp", axis=1, tiled=True),
-        lax.all_gather(norm_out_b, "fsdp", axis=1, tiled=True),
-    )
-    redone_b = block_b_forward(
-        block_out, backward_b, mask_out, local_counts, channel_b, depth_gate, stats_b
-    )[2]
+    MODE["fast"] = lax.axis_size("fsdp") == 8 and lax.axis_size("dp") == 4
+    MODE["calls"] = 0
+    gather_now = gather_all if MODE["fast"] else gather_plain
+    scatter_now = scatter_all if MODE["fast"] else scatter_plain
+    total_counts = lax.psum(local_counts, ("fsdp", "dp"))
+    gathered = gather_now((w_in_a, w_mid_a, w_out_a, w_proj_a, w_in_b, w_mid_b, w_out_b))
+    norms = lax.all_gather(
+        jnp.concatenate(
+            [norm_in_a, norm_mid_a, norm_out_a, norm_proj_a, norm_in_b, norm_mid_b, norm_out_b], axis=1
+        ),
+        "fsdp",
+        axis=0,
+    )
+    wide = []
+    place = 0
+    for one in (norm_in_a, norm_mid_a, norm_out_a, norm_proj_a, norm_in_b, norm_mid_b, norm_out_b):
+        width = one.shape[1]
+        wide.append(norms[:, :, place : place + width].transpose(1, 0, 2).reshape(2, -1))
+        place += width
+    weights_a = tuple(gathered[:4]) + tuple(wide[:4])
+    weights_b = tuple(gathered[4:]) + tuple(wide[4:])
+    block_out, stats_a, redone_a = block_a_forward(
+        inputs, weights_a, mask_in, mask_out, total_counts, channel_a, None
+    )
+    result, stats_b, redone_b = block_b_forward(
+        block_out, weights_b, mask_out, total_counts, channel_b, depth_gate, None
+    )
     grad_block, grads_b, norms_b = block_b_backward(
-        cotangent.astype(jnp.float32),
-        backward_b,
-        stats_b,
-        redone_b,
-        mask_out,
-        channel_b,
-        depth_gate,
-    )
-    backward_a = (
-        lax.all_gather(w_in_a, "fsdp", axis=0, tiled=True),
-        lax.all_gather(w_mid_a, "fsdp", axis=0, tiled=True),
-        lax.all_gather(w_out_a, "fsdp", axis=0, tiled=True),
-        lax.all_gather(w_proj_a, "fsdp", axis=0, tiled=True),
-        lax.all_gather(norm_in_a, "fsdp", axis=1, tiled=True),
-        lax.all_gather(norm_mid_a, "fsdp", axis=1, tiled=True),
-        lax.all_gather(norm_out_a, "fsdp", axis=1, tiled=True),
-        lax.all_gather(norm_proj_a, "fsdp", axis=1, tiled=True),
-    )
-    redone_a = block_a_forward(
-        inputs, backward_a, mask_in, mask_out, local_counts, channel_a, stats_a
-    )[2]
+        cotangent.astype(jnp.float32), weights_b, stats_b, redone_b, mask_out, channel_b, depth_gate
+    )
     grad_inputs, grads_a, norms_a = block_a_backward(
-        grad_block, inputs, backward_a, stats_a, redone_a, mask_in, mask_out, channel_a
-    )
-    part_in_a, part_mid_a, part_out_a, part_proj_a, part_in_b, part_mid_b, part_out_b = (
-        lax.psum_scatter(grads_a[0], "fsdp", scatter_dimension=0, tiled=True),
-        lax.psum_scatter(grads_a[1], "fsdp", scatter_dimension=0, tiled=True),
-        lax.psum_scatter(grads_a[2], "fsdp", scatter_dimension=0, tiled=True),
-        lax.psum_scatter(grads_a[3], "fsdp", scatter_dimension=0, tiled=True),
-        lax.psum_scatter(grads_b[0], "fsdp", scatter_dimension=0, tiled=True),
-        lax.psum_scatter(grads_b[1], "fsdp", scatter_dimension=0, tiled=True),
-        lax.psum_scatter(grads_b[2], "fsdp", scatter_dimension=0, tiled=True),
-    )
+        grad_block, inputs, weights_a, stats_a, redone_a, mask_in, mask_out, channel_a
+    )
+    finals = scatter_now(tuple(one.astype(jnp.bfloat16) for one in grads_a + grads_b))
     final_in_a, final_mid_a, final_out_a, final_proj_a, final_in_b, final_mid_b, final_out_b = (
-        lax.psum(part_in_a.astype(jnp.bfloat16), "dp").astype(jnp.float32),
-        lax.psum(part_mid_a.astype(jnp.bfloat16), "dp").astype(jnp.float32),
-        lax.psum(part_out_a.astype(jnp.bfloat16), "dp").astype(jnp.float32),
-        lax.psum(part_proj_a.astype(jnp.bfloat16), "dp").astype(jnp.float32),
-        lax.psum(part_in_b.astype(jnp.bfloat16), "dp").astype(jnp.float32),
-        lax.psum(part_mid_b.astype(jnp.bfloat16), "dp").astype(jnp.float32),
-        lax.psum(part_out_b.astype(jnp.bfloat16), "dp").astype(jnp.float32),
+        one.astype(jnp.float32) for one in finals
     )
     return (
         result.astype(jnp.bfloat16),

time: 1710 us -> 681 us (0.40)
  waiting for transfers between devices: 846 us -> 0 us
  blocking collectives: 609 us -> 70.3 us
  Pallas kernels: 0 us -> 391 us
    reduce_scatter x7 -> x0, waiting for transfers between devices: 749 us -> none  [the longest x1 164 us: body(): lax.psum_scatter(grads_a[1], 'fsdp', scatter_dimension=0, tiled=True)]
    psum x12 -> x1, blocking collectives: 508 us -> 45.1 us  [body(): total_counts = lax.psum(local_counts, ('fsdp', 'dp'))]
    pallas_call x0 -> x14, Pallas kernels: none -> 391 us  [the longest x12 143 us: sum_call(): pl.pallas_call(sum_kernel, out_shape=jax.ShapeDtypeStruct(local.shape, jn...]
    all_gather x7 -> x1, blocking collectives: 101 us -> 25.2 us  [body(): lax.all_gather(jnp.concatenate([norm_in_a, norm_mid_a, norm_out_a, norm_p...]
    psum x1 -> x0, waiting for transfers between devices: 53.7 us -> none  [body(): lax.psum(part_in_a.astype(jnp.bfloat16), 'dp').astype(jnp.float32)]
    all_gather x7 -> x0, waiting for transfers between devices: 38.6 us -> none  [the longest x1 28 us: body(): lax.all_gather(w_mid_b, 'fsdp', axis=0, tiled=True)]
    unnamed x146 -> x133, local copies, waits for them, and re-layouts: 29.4 us -> 10.3 us
  transfers between devices with their start and end apart: 15 -> 0, of which waited for: 11 -> 0; matrix products, arithmetic and copies ran while one was open for 8% -> 0% of each run, Pallas kernels for 0% -> 0%
where the time goes in v1:
time: 681 us; the launch traced here: 671 us
  Pallas kernels  391 us (57%)
  other arithmetic  84.7 us (12%)
  blocking collectives  70.3 us (10%)
  matrix products  69.9 us (10%)
  local copies, waits for them, and re-layouts  52.9 us (8%)
    pallas_call x12, Pallas kernels, sum_call(): pl.pallas_call(sum_kernel, out_shape=jax.ShapeDtypeStruct(local.shape, jn...  143 us
    pallas_call x1, Pallas kernels, scatter_all(): pl.pallas_call(scatter_kernel, out_shape=[jax.ShapeDtypeStruct(shape, jnp...  130 us
    pallas_call x1, Pallas kernels, gather_all(): pl.pallas_call(gather_kernel, out_shape=[jax.ShapeDtypeStruct(shape, jnp....  118 us
    psum x1, blocking collectives, body(): total_counts = lax.psum(local_counts, ('fsdp', 'dp'))  45.1 us
    all_gather x1, blocking collectives, body(): lax.all_gather(jnp.concatenate([norm_in_a, norm_mid_a, norm_out_a, norm_p...  25.2 us
    dot_general x7, matrix products, contract(): lax.dot_general(left_side, right_side, (((0, 1, 2), (0, 1, 2)), ((), ()))...  23 us
    dot_general x7, matrix products, back_project(): lax.dot_general(gradient, weight, (((3,), (1,)), ((), ())), preferred_ele...  21.1 us
    convert_element_type x6, other arithmetic, norm_backward(): return (grad_hidden.astype(jnp.bfloat16), gain_sum, shift_sum)  15.4 us

profile of v1, /device:TPU:1, one launch (start us, length us, event | category | flops | bytes accessed | tf_op | source)
XLA Modules:
  0.0 670.9 jit_solution(1424027711923056060)
XLA Ops:
  2.3 25.2 %all-gather.1 = bf16[8,2,1024]{2,1,0:T(2,128)(2,1)S(1)} all-gather(bf16[1,2,1024]{2,1,0:T(2,128)(2,1)S(1)} %bitcast.391), channel_id=2, replica_groups=mesh['fsdp'=8,'dp'=4] {'fsdp'}, dimensions={0}, use_global_device_ids=true | all-gather | bytes 36864 | tf_op jit(solution)/shard_map/all_gather | solution.py:815
  30.2 45.1 %psum.7 = f32[2]{0:T(128)S(1)} all-reduce(f32[2]{0:T(128)S(1)} %add_convert_fusion), channel_id=1, replica_groups=mesh['fsdp'=8,'dp'=4] {'fsdp','dp'}, use_global_device_ids=true, to_apply=%region_4.5 | all-reduce | flops 2 | bytes 16 | tf_op jit(solution)/shard_map/psum | solution.py:813
  76.1 117.9 %gather_weights.1 = (bf16[1024,512]{1,0:T(8,128)(2,1)}, bf16[4608,512]{1,0:T(8,128)(2,1)}, bf16[512,2048]{1,0:T(8,128)(2,1)}, bf16[1024,2048]{1,0:T(8,128)(2,1)}...) custom-call(bf16[128,512]{1,0:T(8,128)(2,1)} %refs_0_.1, ...), custom_call_target="tpu_custom_call" | custom-call | tf_op jit(solution)/shard_map/gather_weights/pallas_call | solution.py:328
  195.4 4.6 fusion.10
  204.8 18.1 %sum_all.12 = f32[8,128]{1,0:T(8,128)} custom-call(f32[8,128]{1,0:T(8,128)} %pad_maximum_fusion.7.local), custom_call_target="tpu_custom_call" | custom-call | tf_op jit(solution)/shard_map/sum_all/pallas_call | solution.py:406
  233.9 5.4 multiply_reduce_fusion.17
  240.2 9.9 %sum_all.13 = f32[8,128]{1,0:T(8,128)} custom-call(f32[8,128]{1,0:T(8,128)} %pad_maximum_fusion.8.local), custom_call_target="tpu_custom_call" | custom-call | tf_op jit(solution)/shard_map/sum_all/pallas_call | solution.py:406
  257.4 15.0 %sum_all.14 = f32[64,128]{1,0:T(8,128)} custom-call(f32[64,128]{1,0:T(8,128)} %pad_maximum_fusion.3.local), custom_call_target="tpu_custom_call" | custom-call | tf_op jit(solution)/shard_map/sum_all/pallas_call | solution.py:406
  283.1 9.8 %sum_all.15 = f32[8,128]{1,0:T(8,128)} custom-call(f32[8,128]{1,0:T(8,128)} %pad_maximum_fusion.9.local), custom_call_target="tpu_custom_call" | custom-call | tf_op jit(solution)/shard_map/sum_all/pallas_call | solution.py:406
  296.6 5.4 multiply_reduce_fusion.13
  302.9 11.0 %sum_all.16 = f32[8,128]{1,0:T(8,128)} custom-call(f32[8,128]{1,0:T(8,128)} %pad_maximum_fusion.10.local), custom_call_target="tpu_custom_call" | custom-call | tf_op jit(solution)/shard_map/sum_all/pallas_call | solution.py:406
  321.3 11.4 %sum_all.17 = f32[32,128]{1,0:T(8,128)} custom-call(f32[32,128]{1,0:T(8,128)} %pad_maximum_fusion.5.local), custom_call_target="tpu_custom_call" | custom-call | tf_op jit(solution)/shard_map/sum_all/pallas_call | solution.py:406
  335.5 5.4 multiply_reduce_fusion.8
  343.1 12.4 %sum_all.18 = f32[32,128]{1,0:T(8,128)} custom-call(f32[32,128]{1,0:T(8,128)} %pad_maximum_fusion.6.local), custom_call_target="tpu_custom_call" | custom-call | tf_op jit(solution)/shard_map/sum_all/pallas_call | solution.py:406
  364.4 9.9 %sum_all.19 = f32[8,128]{1,0:T(8,128)} custom-call(f32[8,128]{1,0:T(8,128)} %pad_maximum_fusion.11.local), custom_call_target="tpu_custom_call" | custom-call | tf_op jit(solution)/shard_map/sum_all/pallas_call | solution.py:406
  385.9 11.0 %sum_all.20 = f32[8,128]{1,0:T(8,128)} custom-call(f32[8,128]{1,0:T(8,128)} %pad_maximum_fusion.12.local), custom_call_target="tpu_custom_call" | custom-call | tf_op jit(solution)/shard_map/sum_all/pallas_call | solution.py:406
  401.1 4.7 fusion.21
  407.6 14.0 %sum_all.21 = f32[64,128]{1,0:T(8,128)} custom-call(f32[64,128]{1,0:T(8,128)} %pad_maximum_fusion.4.local), custom_call_target="tpu_custom_call" | custom-call | tf_op jit(solution)/shard_map/sum_all/pallas_call | solution.py:406
  423.0 4.4 fusion.19
  430.5 10.6 %pad.98 = f32[4,14,14,1024]{3,2,1,0:T(8,128)} pad(f32[4,7,7,1024]{3,2,1,0:T(8,128)S(1)} %fusion.8, f32[]{:T(128)} %constant.21.clone.1), padding=0_0_0x0_1_1x0_1_1x0_0_0 | pad | bytes 4014084 | tf_op jit(solution)/shard_map/pad | solution.py:689
  444.6 10.9 %sum_all.22 = f32[8,128]{1,0:T(8,128)} custom-call(f32[8,128]{1,0:T(8,128)} %pad_maximum_fusion.13.local), custom_call_target="tpu_custom_call" | custom-call | tf_op jit(solution)/shard_map/sum_all/pallas_call | solution.py:406
  477.7 9.9 %sum_all.23 = f32[8,128]{1,0:T(8,128)} custom-call(f32[8,128]{1,0:T(8,128)} %pad_maximum_fusion.14.local), custom_call_target="tpu_custom_call" | custom-call | tf_op jit(solution)/shard_map/sum_all/pallas_call | solution.py:406
  512.8 4.6 bitcast_convert_fusion.refs_5_
  520.1 129.8 %scatter_grads.1 = (bf16[128,512]{1,0:T(8,128)(2,1)}, bf16[576,512]{1,0:T(8,128)(2,1)}, bf16[64,2048]{1,0:T(8,128)(2,1)}, bf16[128,2048]{1,0:T(8,128)(2,1)}, bf1...) custom-call(bf16[1024,512]{1,0:T(8,128)(2,1)} %bitcast_convert_fusion.6.refs_0_, ...), custom_call_target="tpu_custom_call" | custom-call | tf_op jit(solution)/shard_map/scatter_grads/pallas_call | solution.py:360
  (282 shorter events, 162.4 us)
Async XLA Ops:
  0.6 193.4 %copy-start.56 = (s32[4]{0:T(128)S(1)}, s32[4]{0:T(128)}, u32[]{:S(2)}) copy-start(s32[4]{0:T(128)} %param.20) | copy-start | bytes 52
  0.7 193.7 %copy-start.17 = (bf16[4,14,14,1024]{3,0,2,1:T(4,128)(2,1)S(1)}, bf16[4,14,14,1024]{3,0,2,1:T(4,128)(2,1)}, u32[]{:S(2)}) copy-start(bf16[4,14,14,1024]{3,0,2,1:T(4,128)(2,1)} %param.19) | copy-start | bytes 4816900
  195.2 4.8 copy-start.9
  233.9 5.4 copy-start.41
  239.4 201.8 %copy-start.26 = (f32[4,7,7,512]{3,2,1,0:T(8,128)}, f32[4,7,7,512]{3,2,1,0:T(8,128)S(1)}, u32[]{:S(2)}) copy-start(f32[4,7,7,512]{3,2,1,0:T(8,128)S(1)} %get-tuple-element.209) | copy-start | bytes 1204228
  282.2 102.5 %copy-start.37 = (f32[512]{0:T(512)}, f32[512]{0:T(512)S(1)}, u32[]{:S(2)}) copy-start(f32[512]{0:T(512)S(1)} %fusion.111) | copy-start | bytes 6148
  296.6 5.4 copy-start.39
  302.0 59.6 %copy-start.28 = (f32[4,7,7,512]{3,2,1,0:T(8,128)}, f32[4,7,7,512]{3,2,1,0:T(8,128)S(1)}, u32[]{:S(2)}) copy-start(f32[4,7,7,512]{3,2,1,0:T(8,128)S(1)} %get-tuple-element.211) | copy-start | bytes 1204228
  302.1 59.5 %copy-start.51 = (f32[512]{0:T(512)}, f32[512]{0:T(512)S(1)}, u32[]{:S(2)}) copy-start(f32[512]{0:T(512)S(1)} %add.308) | copy-start | bytes 6148
  302.2 59.4 %copy-start.53 = (f32[512]{0:T(512)}, f32[512]{0:T(512)S(1)}, u32[]{:S(2)}) copy-start(f32[512]{0:T(512)S(1)} %mul.783) | copy-start | bytes 6148
  315.3 61.6 %copy-start.46 = (f32[512]{0:T(512)}, f32[512]{0:T(512)S(1)}, u32[]{:S(2)}) copy-start(f32[512]{0:T(512)S(1)} %get-tuple-element.200) | copy-start | bytes 6148
  316.6 60.3 %copy-start.43 = (f32[512]{0:T(512)}, f32[512]{0:T(512)S(1)}, u32[]{:S(2)}) copy-start(f32[512]{0:T(512)S(1)} %divide_bitcast_fusion.3) | copy-start | bytes 6148
  356.8 4.8 copy-start.36
  375.6 8.2 %copy-start.45 = (f32[512]{0:T(512)}, f32[512]{0:T(512)S(1)}, u32[]{:S(2)}) copy-start(f32[512]{0:T(512)S(1)} %get-tuple-element.190) | copy-start | bytes 6148
  398.2 7.5 %copy-start.48 = (f32[512]{0:T(512)}, f32[512]{0:T(512)S(1)}, u32[]{:S(2)}) copy-start(f32[512]{0:T(512)S(1)} %get-tuple-element.192) | copy-start | bytes 6148
  423.0 5.7 copy-start.8
  430.5 10.7 %copy-start.15 = (bf16[4,7,7,4096]{3,2,1,0:T(8,128)(2,1)S(1)}, bf16[4,7,7,4096]{3,2,1,0:T(8,128)(2,1)}, u32[]{:S(2)}) copy-start(bf16[4,7,7,4096]{3,2,1,0:T(8,128)(2,1)} %copy-done.14) | copy-start | bytes 4816900
  456.8 7.4 %copy-start.49 = (f32[512]{0:T(512)}, f32[512]{0:T(512)S(1)}, u32[]{:S(2)}) copy-start(f32[512]{0:T(512)S(1)} %get-tuple-element.194) | copy-start | bytes 6148
  472.9 20.4 %copy-start.19 = (bf16[1024,512]{1,0:T(8,128)(2,1)S(1)}, bf16[1024,512]{1,0:T(8,128)(2,1)}, u32[]{:S(2)}) copy-start(bf16[1024,512]{1,0:T(8,128)(2,1)} %get-tuple-element.30) | copy-start | bytes 3145732
  649.9 4.8 copy-start.25
  651.6 8.3 %copy-start.30 = (f32[64,128]{1,0:T(8,128)S(1)}, f32[64,128]{1,0:T(8,128)}, u32[]{:S(2)}) copy-start(f32[64,128]{1,0:T(8,128)} %sum_all.21) | copy-start | bytes 98308
  651.6 9.8 %copy-start.32 = (bf16[256,512]{1,0:T(8,128)(2,1)S(1)}, bf16[256,512]{1,0:T(8,128)(2,1)}, u32[]{:S(2)}) copy-start(bf16[256,512]{1,0:T(8,128)(2,1)} %get-tuple-element.41) | copy-start | bytes 786436
  653.8 8.4 %copy-start.24 = (bf16[576,512]{1,0:T(8,128)(2,1)S(1)}, bf16[576,512]{1,0:T(8,128)(2,1)}, u32[]{:S(2)}) copy-start(bf16[576,512]{1,0:T(8,128)(2,1)} %get-tuple-element.42) | copy-start | bytes 1769476
  654.7 8.7 %copy-start.31 = (bf16[64,2048]{1,0:T(8,128)(2,1)S(1)}, bf16[64,2048]{1,0:T(8,128)(2,1)}, u32[]{:S(2)}) copy-start(bf16[64,2048]{1,0:T(8,128)(2,1)} %get-tuple-element.43) | copy-start | bytes 786436
  (34 other events, 109.9 us)

commit v2 on v1

--- a/solution.py
+++ b/solution.py
@@ -164,6 +164,7 @@
         total_rows,
         chunk,
     )
+    await_bytes(from_core, send.at[0])
     for block in range(8):
         push(
             from_core.at[rows_of(block * rows + row_o, part), pl.ds(0, wide_a)],
@@ -274,149 +275,893 @@
 def scatter_sent(grad, room, out, send):
     from_core, from_x, from_y, from_y2, from_x2, from_z = room
     half = grad.shape[1] // 2
-    for index, view in enumerate((from_core, from_x, from_y, from_y2, from_x2, from_z)):
-        await_bytes(view, send.at[index])
+    for index, view in enumerate((from_x, from_y, from_y2, from_x2, from_z)):
+        await_bytes(view, send.at[index + 1])
     await_bytes(out.at[pl.ds(0, out.shape[0] // 2), pl.ds(0, half)], send.at[6])
     await_bytes(out.at[:, pl.ds(0, half)], send.at[7])
 
 
-def room_shapes(total_rows, columns):
-    rows = total_rows // 8
+ORDER = ("in_a", "mid_a", "proj_a", "out_a", "in_b", "mid_b", "out_b")
+BLOCK = 256
+LANES = 512
+CHUNK = 32
+TAPS = [(u, v) for u in range(3) for v in range(3)]
+EVERY_PEER = ((0, 1), (0, 2), (0, 3), (1, 0), (2, 0), (3, 0), (4, 0), (5, 0), (6, 0), (7, 0))
+F32 = jnp.float32
+BF16 = jnp.bfloat16
+
+
+def mm(left, right):
+    return jnp.dot(left, right, preferred_element_type=F32)
+
+
+def mm_nt(left, right):
+    return lax.dot_general(left, right, (((1,), (1,)), ((), ())), preferred_element_type=F32)
+
+
+def mm_tn(left, right):
+    return lax.dot_general(left, right, (((0,), (0,)), ((), ())), preferred_element_type=F32)
+
+
+def loop(count, step):
+    def body_of(index, carry):
+        step(index)
+        return carry
+
+    lax.fori_loop(0, count, body_of, 0)
+
+
+def at_block(index, size):
+    return pl.ds(pl.multiple_of(index * size, size), size)
+
+
+def slope_of(values):
+    gate = jax.nn.sigmoid(values)
+    return gate * (1.0 + values * (1.0 - gate))
+
+
+def fold(values):
+    total = values[0:8]
+    for start in range(8, values.shape[0], 8):
+        total = total + values[start : start + 8]
+    return total
+
+
+def column_sums(count, terms, chunk=CHUNK):
+    def step(index, carry):
+        start = pl.multiple_of(index * chunk, chunk)
+        return tuple(total + fold(one) for total, one in zip(carry, terms(start)))
+
+    width = len(jax.eval_shape(lambda: terms(0)))
+    zero = jnp.zeros((8, LANES), F32)
+    totals = lax.fori_loop(0, count, step, (zero,) * width)
+    return [jnp.sum(one, axis=0, keepdims=True) for one in totals]
+
+
+class Vectors:
+    def __init__(self, ref):
+        self.ref, self.used = ref, 0
+
+    def put(self, row):
+        at = self.used
+        self.used += 1
+        self.ref[at : at + 1, :] = row
+        return at
+
+    def get(self, at):
+        return self.ref[at : at + 1, :]
+
+
+class Totals:
+    def __init__(self, place, near, far, tot, send, recv):
+        self.place, self.near, self.far, self.tot, self.send, self.recv = place, near, far, tot, send, recv
+        self.turn, self.rows = 1, 0
+
+    def start(self, rows_of_values, extra=None):
+        self.turn = 1 - self.turn
+        turn, place = self.turn, self.place
+        at = 0
+        for row in rows_of_values:
+            for lane in range(0, LANES, 128):
+                self.near[turn, place.d, at : at + 1, :] = row[:, lane : lane + 128]
+                at += 1
+        if extra is not None:
+            self.near[turn, place.d, at : at + 8, :] = extra
+            at += 8
+        self.rows = at
+        own = self.near.at[turn, place.d, pl.ds(0, at)]
+        for bits in (1, 2, 3):
+            push(own, own, self.send.at[turn, 0], self.recv.at[turn, 0], place.peer(0, bits))
+
+    def middle(self):
+        turn, rows, place = self.turn, self.rows, self.place
+        await_bytes(self.near.at[turn, pl.ds(0, 3), pl.ds(0, rows)], self.recv.at[turn, 0])
+        near = self.near
+        own = self.far.at[turn, place.f, pl.ds(0, rows)]
+        own[...] = (near[turn, 0, 0:rows, :] + near[turn, 1, 0:rows, :]) + (
+            near[turn, 2, 0:rows, :] + near[turn, 3, 0:rows, :]
+        )
+        for bits in range(1, 8):
+            push(own, own, self.send.at[turn, 1], self.recv.at[turn, 1], place.peer(bits, 0))
+
+    def end(self):
+        turn, rows = self.turn, self.rows
+        await_bytes(self.far.at[turn, pl.ds(0, 7), pl.ds(0, rows)], self.recv.at[turn, 1])
+        total = self.far[turn, 0, 0:rows, :]
+        for index in range(1, 8):
+            total = total + self.far[turn, index, 0:rows, :]
+        self.tot[0:rows, :] = total
+        await_bytes(self.near.at[turn, pl.ds(0, 3), pl.ds(0, rows)], self.send.at[turn, 0])
+        await_bytes(self.far.at[turn, pl.ds(0, 7), pl.ds(0, rows)], self.send.at[turn, 1])
+
+    def whole(self, rows_of_values, extra=None):
+        self.start(rows_of_values, extra)
+        self.middle()
+        self.end()
+
+    def row(self, index):
+        at = 4 * index
+        return jnp.concatenate([self.tot[at + k : at + k + 1, :] for k in range(4)], axis=1)
+
+    def wide(self, at):
+        return jnp.concatenate([self.tot[at : at + 1, :]] * 4, axis=1)
+
+
+def room_in(whole):
+    total, columns = whole.shape
+    rows = total // 8
     half = columns // 2
     wide_a = split_of(columns)
     wide_b = half - wide_a
-    part = rows // 2
-    return [
-        (8 * rows, half),
-        (8 * part, wide_a),
-        (4 * rows, wide_b),
-        (4 * part, wide_a),
-        (4 * part, wide_b),
-        (3 * part, half),
-    ]
-
-
-def run_staggered(steps):
-    alive = list(steps)
-    for one in alive:
-        next(one)
-    begun = 0
-    while any(one is not None for one in alive):
-        begun += 1
-        for index in range(min(begun, len(alive))):
-            if alive[index] is not None and next(alive[index], "end") == "end":
-                alive[index] = None
-
-
-def gather_kernel(*refs):
-    shards, wholes = refs[:7], refs[7:14]
-    local_sem, send, recv = refs[14:]
+    return (
+        whole.at[:, pl.ds(0, half)],
+        whole.at[pl.ds(0, 4 * rows), pl.ds(half, wide_a)],
+        whole.at[pl.ds(0, 4 * rows), pl.ds(half + wide_a, wide_b)],
+        whole.at[pl.ds(4 * rows, 2 * rows), pl.ds(half, wide_a)],
+        whole.at[pl.ds(4 * rows, 2 * rows), pl.ds(half + wide_a, wide_b)],
+        whole.at[pl.ds(6 * rows, 3 * rows // 2), pl.ds(half, half)],
+    )
+
+
+def step_kernel(
+    x_hbm,
+    cot_hbm,
+    mask_ref,
+    gate_ref,
+    count_ref,
+    chan_ref,
+    norm_hbm,
+    sh_in_a,
+    sh_mid_a,
+    sh_out_a,
+    sh_proj_a,
+    sh_in_b,
+    sh_mid_b,
+    sh_out_b,
+    result_hbm,
+    images_hbm,
+    sums_out,
+    out_in_a,
+    out_mid_a,
+    out_out_a,
+    out_proj_a,
+    out_in_b,
+    out_mid_b,
+    out_out_b,
+    w_in_a,
+    w_mid_a,
+    w_out_a,
+    w_proj_a,
+    w_in_b,
+    w_mid_b,
+    w_out_b,
+    room_a,
+    x,
+    cot,
+    c1,
+    cols_a,
+    c2,
+    a2,
+    c3,
+    cp,
+    bo,
+    feed,
+    d1,
+    cols_b,
+    d2,
+    b2,
+    d3,
+    dz,
+    dm,
+    df,
+    dout,
+    dproj,
+    dfa,
+    g_mid,
+    g_out,
+    g_in,
+    g_proj,
+    norms,
+    vec_ref,
+    near,
+    far,
+    tot,
+    io_sem,
+    ag_local,
+    ag_send,
+    ag_recv,
+    rs_send,
+    rs_recv,
+    ar_send,
+    ar_recv,
+    nb_sem,
+):
     place = Place()
-    enter(place, LINK_PEERS)
-    run_staggered(
-        [
-            gather_steps(place, shards[i], wholes[i], local_sem.at[i], send.at[i], recv.at[i])
-            for i in range(7)
+    enter(place, EVERY_PEER)
+    shards = dict(in_a=sh_in_a, mid_a=sh_mid_a, out_a=sh_out_a, proj_a=sh_proj_a, in_b=sh_in_b, mid_b=sh_mid_b, out_b=sh_out_b)
+    wholes = dict(in_a=w_in_a, mid_a=w_mid_a, out_a=w_out_a, proj_a=w_proj_a, in_b=w_in_b, mid_b=w_mid_b, out_b=w_out_b)
+    outs = dict(in_a=out_in_a, mid_a=out_mid_a, out_a=out_out_a, proj_a=out_proj_a, in_b=out_in_b, mid_b=out_mid_b, out_b=out_out_b)
+
+    pltpu.make_async_copy(norm_hbm, norms.at[place.f], nb_sem.at[0]).start()
+    for bits in range(1, 8):
+        push(norm_hbm, norms.at[place.f], nb_sem.at[1], nb_sem.at[2], place.peer(bits, 0))
+    pltpu.make_async_copy(x_hbm, x, io_sem.at[0]).start()
+    legs = {}
+    for i, name in enumerate(ORDER):
+        legs[name] = gather_steps(place, shards[name], wholes[name], ag_local.at[i], ag_send.at[i], ag_recv.at[i])
+        next(legs[name])
+    pltpu.make_async_copy(cot_hbm, cot, io_sem.at[1]).start()
+    ticks = [0]
+
+    def tick():
+        ticks[0] += 1
+        now = ticks[0]
+        due = [i for i in range(7) if 0 <= now - 1 - i < 4]
+        for i in [j for j in due if now - 1 - j < 3] + [j for j in due if now - 1 - j == 3]:
+            next(legs[ORDER[i]], None)
+
+    vec = Vectors(vec_ref)
+    totals = Totals(place, near, far, tot, ar_send, ar_recv)
+
+    for _ in range(3):
+        tick()
+
+    pltpu.make_async_copy(norm_hbm, norms.at[place.f], nb_sem.at[0]).wait()
+    await_bytes(norms.at[pl.ds(0, 7)], nb_sem.at[2])
+    await_bytes(norms.at[pl.ds(0, 7)], nb_sem.at[1])
+
+    def narrow_row(at):
+        pieces = [norms[2 * k, at : at + 1, :] + norms[2 * k + 1, at : at + 1, :] for k in range(4)]
+        return vec.put(jnp.concatenate(pieces, axis=1))
+
+    def wide_rows(at):
+        return [
+            vec.put(
+                jnp.concatenate(
+                    [norms[2 * j + k // 2, at + k % 2 : at + k % 2 + 1, :] for k in range(4)], axis=1
+                )
+            )
+            for j in range(4)
         ]
-    )
-    for i in range(7):
-        gather_sent(shards[i], wholes[i], send.at[i])
-
-
-def gather_all(shards):
-    shapes = [(8 * one.shape[0], one.shape[1]) for one in shards]
-    return pl.pallas_call(
-        gather_kernel,
-        out_shape=[jax.ShapeDtypeStruct(shape, jnp.bfloat16) for shape in shapes],
-        in_specs=[pl.BlockSpec(memory_space=pl.ANY)] * 7,
-        out_specs=[pl.BlockSpec(memory_space=pltpu.VMEM)] * 7,
-        scratch_shapes=[
+
+    params = dict(
+        in_a=([narrow_row(0)], [narrow_row(10)]),
+        mid_a=([narrow_row(1)], [narrow_row(11)]),
+        out_a=(wide_rows(2), wide_rows(12)),
+        proj_a=(wide_rows(4), wide_rows(14)),
+        in_b=([narrow_row(6)], [narrow_row(16)]),
+        mid_b=([narrow_row(7)], [narrow_row(17)]),
+        out_b=(wide_rows(8), wide_rows(18)),
+    )
+    chan_a = vec.put(chan_ref[0:1, :])
+    chan_b = vec.put(chan_ref[1:2, :])
+    scales = {}
+
+    def mask_at(start, size=CHUNK):
+        return jnp.concatenate([mask_ref[pl.ds(start, size), :]] * 4, axis=1)
+
+    def gate_at(start, size=CHUNK):
+        return jnp.concatenate([gate_ref[pl.ds(start, size), :]] * 4, axis=1)
+
+    def set_norm(name, block, sums, inverse, chan):
+        total, squares = sums
+        average = total * inverse
+        rstd = lax.rsqrt(squares * inverse - average * average + EPSILON)
+        gain, shift = (vec.get(rows[block]) for rows in params[name])
+        keep = 1.0 if chan is None else vec.get(chan)
+        by = gain * rstd
+        scales[name, block] = dict(
+            rstd=vec.put(rstd),
+            off=vec.put(-average * rstd),
+            by=vec.put(by),
+            mul=vec.put(by * keep),
+            add=vec.put((shift - average * by) * keep),
+        )
+
+    def normed(name, block, values):
+        s = scales[name, block]
+        return values * vec.get(s["mul"]) + vec.get(s["add"])
+
+    def hat(name, block, values):
+        s = scales[name, block]
+        return values * vec.get(s["rstd"]) + vec.get(s["off"])
+
+    def set_back(name, block, shift_sum, gain_sum):
+        s = scales[name, block]
+        inverse = vec.get(inv_in if name == "in_a" else inv_out)
+        by = vec.get(s["by"])
+        pull = by * gain_sum * inverse
+        s["back_add"] = vec.put(by * shift_sum * inverse + pull * vec.get(s["off"]))
+        s["back_mul"] = vec.put(pull * vec.get(s["rstd"]))
+
+    def back(name, block, grad, values):
+        s = scales[name, block]
+        return grad * vec.get(s["by"]) - vec.get(s["back_add"]) - values * vec.get(s["back_mul"])
+
+    pltpu.make_async_copy(x_hbm, x, io_sem.at[0]).wait()
+    tick()
+
+    def first_a(p):
+        c1[at_block(p, BLOCK), :] = mm(x[at_block(p, BLOCK), :], w_in_a[...])
+
+    loop(4, first_a)
+
+    def square_terms(ref):
+        def terms(start):
+            values = ref[pl.ds(start, CHUNK), :]
+            return values, values * values
+
+        return terms
+
+    totals.whole(column_sums(32, square_terms(c1)), count_ref[...])
+    inv_in = vec.put(1.0 / totals.wide(8))
+    inv_out = vec.put(1.0 / totals.wide(9))
+    set_norm("in_a", 0, (totals.row(0), totals.row(1)), vec.get(inv_in), chan_a)
+
+    def lane_row(at, lane):
+        return vec_ref[at : at + 1, at_block(lane, 128)]
+
+    def act_a(lane):
+        s = scales["in_a", 0]
+        for row_par in range(2):
+            for col_par in range(2):
+                p = 2 * row_par + col_par
+                values = c1[p * BLOCK : (p + 1) * BLOCK, at_block(lane, 128)]
+                scaled = values * lane_row(s["mul"], lane) + lane_row(s["add"], lane)
+                act = scaled * jax.nn.sigmoid(scaled) * mask_ref[...]
+                for t, (u, v) in enumerate(TAPS):
+                    if (u != 1) != bool(row_par) or (v != 1) != bool(col_par):
+                        continue
+                    shift = (8 if u == 0 else 0) + (1 if v == 0 else 0)
+                    moved = pltpu.roll(act, shift, 0) if shift else act
+                    cols_a[:, pl.ds(pl.multiple_of(t * LANES + lane * 128, 128), 128)] = moved.astype(BF16)
+
+    loop(4, act_a)
+    tick()
+
+    def conv_mid(out, cols, weight):
+        out[...] = mm(cols[:, 0:1536], weight[0:1536, :])
+
+        def more(k):
+            at = at_block(k + 1, 1536)
+            out[...] += mm(cols[:, at], weight[at, :])
+
+        loop(2, more)
+
+    def masked_terms(ref):
+        def terms(start):
+            values = ref[pl.ds(start, CHUNK), :]
+            kept = values * mask_at(start)
+            return kept, kept * values
+
+        return terms
+
+    conv_mid(c2, cols_a, w_mid_a)
+    totals.start(column_sums(8, masked_terms(c2)))
+    tick()
+
+    def project(j):
+        cp[at_block(j, BLOCK), :] = mm(x[0:BLOCK, :], w_proj_a[:, at_block(j, LANES)])
+
+    loop(4, project)
+    totals.middle()
+    totals.end()
+    set_norm("mid_a", 0, (totals.row(0), totals.row(1)), vec.get(inv_out), chan_a)
+
+    def act_mid(act_ref, ref, name):
+        def step(index):
+            start = pl.multiple_of(index * CHUNK, CHUNK)
+            scaled = normed(name, 0, ref[pl.ds(start, CHUNK), :])
+            act_ref[pl.ds(start, CHUNK), :] = (scaled * jax.nn.sigmoid(scaled) * mask_at(start)).astype(BF16)
+
+        loop(BLOCK // CHUNK, step)
+
+    act_mid(a2, c2, "mid_a")
+    tick()
+
+    def expand_a(j):
+        c3[at_block(j, BLOCK), :] = mm(a2[...], w_out_a[:, at_block(j, LANES)])
+
+    loop(4, expand_a)
+
+    def blocked(ref, j, terms_of=square_terms):
+        return terms_of(ref.at[pl.ds(j * BLOCK, BLOCK)])
+
+    values = []
+    for ref in (c3, cp):
+        for j in range(4):
+            values += column_sums(8, blocked(ref, j))
+    totals.whole(values)
+    for n, name in enumerate(("out_a", "proj_a")):
+        for j in range(4):
+            at = 8 * n + 2 * j
+            set_norm(name, j, (totals.row(at), totals.row(at + 1)), vec.get(inv_out), None)
+
+    for j in range(4):
+
+        def join_a(index, j=j):
+            start = pl.multiple_of(index * CHUNK, CHUNK)
+            rows = pl.ds(j * BLOCK + start, CHUNK)
+            pre = normed("out_a", j, c3[rows, :]) + normed("proj_a", j, cp[rows, :])
+            out = pre * jax.nn.sigmoid(pre) * mask_at(start)
+            bo[rows, :] = out
+            feed[pl.ds(start, CHUNK), pl.ds(j * LANES, LANES)] = out.astype(BF16)
+
+        loop(BLOCK // CHUNK, join_a)
+
+    tick()
+    d1[...] = mm(feed[:, 0:LANES], w_in_b[0:LANES, :])
+
+    def first_b(k):
+        at = at_block(k + 1, LANES)
+        d1[...] += mm(feed[:, at], w_in_b[at, :])
+
+    loop(3, first_b)
+    totals.whole(column_sums(8, square_terms(d1)))
+    set_norm("in_b", 0, (totals.row(0), totals.row(1)), vec.get(inv_out), chan_b)
+
+    def act_b(lane):
+        s = scales["in_b", 0]
+        scaled = d1[:, at_block(lane, 128)] * lane_row(s["mul"], lane) + lane_row(s["add"], lane)
+        act = scaled * jax.nn.sigmoid(scaled) * mask_ref[...]
+        for t, (u, v) in enumerate(TAPS):
+            shift = (-(8 * (u - 1) + v - 1)) % BLOCK
+            moved = pltpu.roll(act, shift, 0) if shift else act
+            cols_b[:, pl.ds(pl.multiple_of(t * LANES + lane * 128, 128), 128)] = moved.astype(BF16)
+
+    loop(4, act_b)
+    tick()
+    conv_mid(d2, cols_b, w_mid_b)
+    totals.whole(column_sums(8, masked_terms(d2)))
+    set_norm("mid_b", 0, (totals.row(0), totals.row(1)), vec.get(inv_out), chan_b)
+    act_mid(b2, d2, "mid_b")
+    tick()
+
+    def expand_b(j):
+        d3[at_block(j, BLOCK), :] = mm(b2[...], w_out_b[:, at_block(j, LANES)])
+
+    loop(4, expand_b)
+    values = []
+    for j in range(4):
+        values += column_sums(8, blocked(d3, j))
+    totals.whole(values)
+    for j in range(4):
+        set_norm("out_b", j, (totals.row(2 * j), totals.row(2 * j + 1)), vec.get(inv_out), None)
+    for i, name in enumerate(ORDER):
+        gather_sent(shards[name], wholes[name], ag_send.at[i])
+
+    pltpu.make_async_copy(cot_hbm, cot, io_sem.at[1]).wait()
+    values = []
+    for j in range(4):
+
+        def finish(start, j=j):
+            rows = pl.ds(j * BLOCK + start, CHUNK)
+            near_rows, lanes = pl.ds(start, CHUNK), pl.ds(j * LANES, LANES)
+            mask, gate, hidden = mask_at(start), gate_at(start), d3[rows, :]
+            pre = bo[rows, :] + gate * normed("out_b", j, hidden)
+            part = jax.nn.sigmoid(pre)
+            grad = cot[near_rows, lanes].astype(F32) * mask * (part * (1.0 + pre * (1.0 - part)))
+            cot[near_rows, lanes] = (pre * part * mask).astype(BF16)
+            bo[rows, :] = grad
+            grad = grad * gate
+            return grad, grad * hat("out_b", j, hidden)
+
+        values += column_sums(8, finish)
+    result_copy = pltpu.make_async_copy(cot, result_hbm, io_sem.at[2])
+    result_copy.start()
+    totals.whole(values)
+    sums_out[0:32, :] = tot[0:32, :]
+    for j in range(4):
+        set_back("out_b", j, totals.row(2 * j), totals.row(2 * j + 1))
+    for j in range(4):
+
+        def low_out_b(index, j=j):
+            start = pl.multiple_of(index * CHUNK, CHUNK)
+            rows = pl.ds(j * BLOCK + start, CHUNK)
+            grad = back("out_b", j, bo[rows, :] * gate_at(start), d3[rows, :]) * mask_at(start)
+            dout[pl.ds(start, CHUNK), pl.ds(j * LANES, LANES)] = grad.astype(BF16)
+
+        loop(BLOCK // CHUNK, low_out_b)
+
+    def through_out(weight):
+        dz[...] = mm_nt(dout[:, 0:LANES], weight[:, 0:LANES])
+
+        def more(k):
+            at = at_block(k + 1, LANES)
+            dz[...] += mm_nt(dout[:, at], weight[:, at])
+
+        loop(3, more)
+
+    def slope_terms(grad_ref, ref, name, chan):
+        def terms(start):
+            rows = pl.ds(start, CHUNK)
+            hidden = ref[rows, :]
+            mask = mask_at(start % BLOCK) if grad_ref.shape[0] > BLOCK else mask_at(start)
+            grad = grad_ref[rows, :] * mask * vec.get(chan) * slope_of(normed(name, 0, hidden))
+            grad_ref[rows, :] = grad
+            return grad, grad * hat(name, 0, hidden)
+
+        return terms
+
+    through_out(w_out_b)
+    totals.start(column_sums(8, slope_terms(dz, d2, "mid_b", chan_b)))
+
+    def grad_out(act_ref, j):
+        g_out[:, at_block(j, LANES)] = mm_tn(act_ref[...], dout[:, at_block(j, LANES)]).astype(BF16)
+
+    loop(2, lambda j: grad_out(b2, j))
+    totals.middle()
+    loop(2, lambda j: grad_out(b2, j + 2))
+    totals.end()
+    sums_out[32:40, :] = tot[0:8, :]
+    scatters = {}
+
+    def scatter(name, grad, room):
+        i = ORDER.index(name)
+        scatters[name] = scatter_steps(place, grad, room, outs[name], rs_send.at[i], rs_recv.at[i])
+        next(scatters[name])
+
+    def go(*names):
+        for name in names:
+            next(scatters[name], None)
+
+    scatter("out_b", g_out, room_in(w_out_b))
+    set_back("mid_b", 0, totals.row(0), totals.row(1))
+
+    def low_mid(name, ref, shifts):
+        s = scales[name, 0]
+
+        def step(lane):
+            lanes = at_block(lane, 128)
+            grad = (
+                dz[:, lanes] * lane_row(s["by"], lane)
+                - lane_row(s["back_add"], lane)
+                - ref[:, lanes] * lane_row(s["back_mul"], lane)
+            ) * mask_ref[...]
+            dm[:, lanes] = grad.astype(BF16)
+            for k, shift in enumerate(shifts):
+                moved = pltpu.roll(grad, shift, 0) if shift else grad
+                g_mid[k * BLOCK : (k + 1) * BLOCK, lanes] = moved.astype(BF16)
+
+        loop(4, step)
+
+    low_mid("mid_b", d2, [(8 * (u - 1) + v - 1) % BLOCK for u, v in TAPS])
+    dz[...] = mm_nt(g_mid[0:BLOCK, :], w_mid_b[0:LANES, :])
+
+    def back_mid_b(t):
+        dz[...] += mm_nt(g_mid[at_block(t + 1, BLOCK), :], w_mid_b[at_block(t + 1, LANES), :])
+
+    loop(8, back_mid_b)
+    totals.start(column_sums(8, slope_terms(dz, d1, "in_b", chan_b)))
+    go("out_b")
+
+    def grad_mid(cols, t):
+        g_mid[at_block(t, LANES), :] = mm_tn(cols[:, at_block(t, LANES)], dm[...]).astype(BF16)
+
+    loop(3, lambda t: grad_mid(cols_b, t))
+    totals.middle()
+    loop(6, lambda t: grad_mid(cols_b, t + 3))
+    totals.end()
+    sums_out[40:48, :] = tot[0:8, :]
+    scatter("mid_b", g_mid, room_in(w_mid_b))
+    set_back("in_b", 0, totals.row(0), totals.row(1))
+
+    def low_first_b(index):
+        start = pl.multiple_of(index * CHUNK, CHUNK)
+        rows = pl.ds(start, CHUNK)
+        df[rows, :] = (back("in_b", 0, dz[rows, :], d1[rows, :]) * mask_at(start)).astype(BF16)
+
+    loop(BLOCK // CHUNK, low_first_b)
+
+    def back_in_b(j):
+        bo[at_block(j, BLOCK), :] += mm_nt(df[...], w_in_b[at_block(j, LANES), :])
+
+    loop(4, back_in_b)
+
+    values = []
+    for j in range(4):
+
+        def join_back(start, j=j):
+            rows = pl.ds(j * BLOCK + start, CHUNK)
+            left, right = c3[rows, :], cp[rows, :]
+            pre = normed("out_a", j, left) + normed("proj_a", j, right)
+            grad = bo[rows, :] * mask_at(start) * slope_of(pre)
+            bo[rows, :] = grad
+            return grad, grad * hat("out_a", j, left), grad * hat("proj_a", j, right)
+
+        values += column_sums(8, join_back)
+    totals.start(values)
+    go("out_b")
+
+    def grad_in_b(j):
+        g_in[at_block(j, LANES), :] = mm_tn(feed[:, at_block(j, LANES)], df[...]).astype(BF16)
+
+    loop(4, grad_in_b)
+    totals.middle()
+    go("mid_b")
+    totals.end()
+    sums_out[48:96, :] = tot[0:48, :]
+    scatter("in_b", g_in, room_in(w_in_b))
+    for j in range(4):
+        set_back("out_a", j, totals.row(3 * j), totals.row(3 * j + 1))
+        set_back("proj_a", j, totals.row(3 * j), totals.row(3 * j + 2))
+    for j in range(4):
+
+        def low_both(index, j=j):
+            start = pl.multiple_of(index * CHUNK, CHUNK)
+            rows = pl.ds(j * BLOCK + start, CHUNK)
+            near_rows, lanes = pl.ds(start, CHUNK), pl.ds(j * LANES, LANES)
+            grad, mask = bo[rows, :], mask_at(start)
+            dout[near_rows, lanes] = (back("out_a", j, grad, c3[rows, :]) * mask).astype(BF16)
+            dproj[near_rows, lanes] = (back("proj_a", j, grad, cp[rows, :]) * mask).astype(BF16)
+
+        loop(BLOCK // CHUNK, low_both)
+    through_out(w_out_a)
+    totals.start(column_sums(8, slope_terms(dz, c2, "mid_a", chan_a)))
+    go("out_b", "mid_b")
+    loop(4, lambda j: grad_out(a2, j))
+    totals.middle()
+
+    def grad_proj(n):
+        i, j = n // 4, n % 4
+        g_proj[at_block(i, LANES), at_block(j, LANES)] = mm_tn(
+            x[0:BLOCK, at_block(i, LANES)], dproj[:, at_block(j, LANES)]
+        ).astype(BF16)
+
+    loop(8, grad_proj)
+
+    def back_proj(n):
+        rows = at_block(n, BLOCK)
+        d3[rows, :] = mm_nt(dproj[:, 0:LANES], w_proj_a[at_block(n, LANES), 0:LANES])
+
+        def more(k):
+            at = at_block(k + 1, LANES)
+            d3[rows, :] += mm_nt(dproj[:, at], w_proj_a[at_block(n, LANES), at])
+
+        loop(3, more)
+
+    loop(2, back_proj)
+    go("in_b")
+    totals.end()
+    sums_out[96:104, :] = tot[0:8, :]
+    scatter("out_a", g_out, room_in(w_out_a))
+    set_back("mid_a", 0, totals.row(0), totals.row(1))
+    go("out_b", "mid_b", "in_b")
+    low_mid("mid_a", c2, [(-(8 * r + s)) % BLOCK for r in range(2) for s in range(2)])
+    for row_par in range(2):
+        for col_par in range(2):
+            rows = pl.ds((2 * row_par + col_par) * BLOCK, BLOCK)
+            grad = None
+            for t, (u, v) in enumerate(TAPS):
+                if (u != 1) != bool(row_par) or (v != 1) != bool(col_par):
+                    continue
+                moved = 2 * (1 if u == 0 else 0) + (1 if v == 0 else 0)
+                term = mm_nt(g_mid[moved * BLOCK : (moved + 1) * BLOCK, :], w_mid_a[t * LANES : (t + 1) * LANES, :])
+                grad = term if grad is None else grad + term
+            bo[rows, :] = grad
+    totals.start(column_sums(32, slope_terms(bo, c1, "in_a", chan_a)))
+    go("out_b", "out_a")
+    loop(3, lambda t: grad_mid(cols_a, t))
+    totals.middle()
+    loop(6, lambda t: grad_mid(cols_a, t + 3))
+    go("mid_b", "in_b")
+    totals.end()
+    sums_out[104:112, :] = tot[0:8, :]
+    scatter("mid_a", g_mid, room_in(w_mid_a))
+    scatter("proj_a", g_proj, room_in(w_proj_a))
+    go("out_b", "out_a")
+    set_back("in_a", 0, totals.row(0), totals.row(1))
+
+    def low_first_a(index):
+        start = pl.multiple_of(index * CHUNK, CHUNK)
+        rows = pl.ds(start, CHUNK)
+        dfa[rows, :] = (back("in_a", 0, bo[rows, :], c1[rows, :]) * mask_at(start % BLOCK)).astype(BF16)
+
+    loop(4 * BLOCK // CHUNK, low_first_a)
+
+    def grad_in_a(i):
+        g_in[at_block(i, 256), :] = mm_tn(x[:, at_block(i, 256)], dfa[...]).astype(BF16)
+
+    loop(4, grad_in_a)
+    scatter("in_a", g_in.at[pl.ds(0, 1024)], room_in(room_a))
+    go("mid_b", "in_b", "out_a", "mid_a", "proj_a")
+
+    def back_in_a(n):
+        p, h = n // 2, n % 2
+        grad = mm_nt(dfa[at_block(p, BLOCK), :], w_in_a[at_block(h, LANES), :])
+        spread = jnp.where(p == 0, d3[at_block(h, BLOCK), :], 0.0)
+        x[at_block(p, BLOCK), at_block(h, LANES)] = (grad + spread).astype(BF16)
+
+    loop(8, back_in_a)
+    images_copy = pltpu.make_async_copy(x, images_hbm, io_sem.at[3])
+    images_copy.start()
+    for _ in range(8):
+        go("mid_b", "in_b", "out_a", "mid_a", "proj_a", "in_a")
+    go("out_b")
+    go("out_b")
+    result_copy.wait()
+    images_copy.wait()
+    for name, grad, room in (
+        ("in_a", g_in.at[pl.ds(0, 1024)], room_in(room_a)),
+        ("mid_a", g_mid, room_in(w_mid_a)),
+        ("out_a", g_out, room_in(w_out_a)),
+        ("proj_a", g_proj, room_in(w_proj_a)),
+        ("in_b", g_in, room_in(w_in_b)),
+        ("mid_b", g_mid, room_in(w_mid_b)),
+        ("out_b", g_out, room_in(w_out_b)),
+    ):
+        scatter_sent(grad, room, outs[name], rs_send.at[ORDER.index(name)])
+
+
+def pieces_128(row, odd):
+    width = row.shape[0]
+    if width >= 128:
+        return row.reshape(width // 128, 128)
+    blank = jnp.zeros((width,), F32)
+    return jnp.where(odd, jnp.concatenate([blank, row]), jnp.concatenate([row, blank]))[None]
+
+
+def body_fast(
+    images,
+    image_sides,
+    widths,
+    keep_gate,
+    w_in_a,
+    w_mid_a,
+    w_out_a,
+    w_proj_a,
+    norm_in_a,
+    norm_mid_a,
+    norm_out_a,
+    norm_proj_a,
+    w_in_b,
+    w_mid_b,
+    w_out_b,
+    norm_in_b,
+    norm_mid_b,
+    norm_out_b,
+    cotangent,
+):
+    slots, side_in, _, width_in = images.shape
+    side, width_out = cotangent.shape[1], cotangent.shape[3]
+    grid = side + 1
+    half = image_sides // 2
+    steps = jnp.arange(grid, dtype=jnp.int32)
+    inside = (steps[None, :, None] < half[:, None, None]) & (steps[None, None, :] < half[:, None, None])
+    mask = jnp.broadcast_to(inside.reshape(BLOCK, 1), (BLOCK, 128)).astype(F32)
+    gate = jnp.broadcast_to(keep_gate[:, None, None], (slots, grid * grid, 128)).reshape(BLOCK, 128).astype(F32)
+    counts = jnp.stack([jnp.sum(image_sides * image_sides), jnp.sum(half * half)]).astype(F32)
+    counts = jnp.broadcast_to(jnp.concatenate([counts, jnp.zeros((6,), F32)])[:, None], (8, 128))
+    lane_ids = jnp.arange(LANES, dtype=jnp.int32)
+    chan = jnp.concatenate([lane_ids[None, :] < widths[:, None], jnp.zeros((6, LANES), bool)]).astype(F32)
+    planes = images.reshape(slots, side, 2, side, 2, width_in).transpose(2, 4, 0, 1, 3, 5)
+    planes = jnp.pad(planes, ((0, 0), (0, 0), (0, 0), (0, 1), (0, 1), (0, 0)))
+    planes = planes * inside[None, None, :, :, :, None].astype(planes.dtype)
+    planes = planes.reshape(4 * BLOCK, width_in)
+    cot = jnp.pad(cotangent, ((0, 0), (0, 1), (0, 1), (0, 0))).reshape(BLOCK, width_out)
+    norms = [norm_in_a, norm_mid_a, norm_out_a, norm_proj_a, norm_in_b, norm_mid_b, norm_out_b]
+    odd = lax.axis_index("fsdp") % 2 == 1
+    packed = [pieces_128(one[k].astype(F32), odd) for k in range(2) for one in norms]
+    packed = jnp.concatenate(packed + [jnp.zeros((4, 128), F32)])
+    shards = (w_in_a, w_mid_a, w_out_a, w_proj_a, w_in_b, w_mid_b, w_out_b)
+    vmem = pl.BlockSpec(memory_space=pltpu.VMEM)
+    anywhere = pl.BlockSpec(memory_space=pl.ANY)
+    wholes = [(8 * one.shape[0], one.shape[1]) for one in shards]
+    outs = pl.pallas_call(
+        step_kernel,
+        out_shape=[
+            jax.ShapeDtypeStruct((BLOCK, width_out), BF16),
+            jax.ShapeDtypeStruct((4 * BLOCK, width_in), BF16),
+            jax.ShapeDtypeStruct((112, 128), F32),
+        ]
+        + [jax.ShapeDtypeStruct(one.shape, BF16) for one in shards],
+        in_specs=[anywhere, anywhere, vmem, vmem, vmem, vmem, anywhere] + [anywhere] * 7,
+        out_specs=[anywhere, anywhere, vmem] + [vmem] * 7,
+        scratch_shapes=[pltpu.VMEM(shape, BF16) for shape in wholes]
+        + [
+            pltpu.VMEM(wholes[0], BF16),
+            pltpu.VMEM((4 * BLOCK, width_in), BF16),
+            pltpu.VMEM((BLOCK, width_out), BF16),
+            pltpu.VMEM((4 * BLOCK, LANES), F32),
+            pltpu.VMEM((BLOCK, 9 * LANES), BF16),
+            pltpu.VMEM((BLOCK, LANES), F32),
+            pltpu.VMEM((BLOCK, LANES), BF16),
+            pltpu.VMEM((4 * BLOCK, LANES), F32),
+            pltpu.VMEM((4 * BLOCK, LANES), F32),
+            pltpu.VMEM((4 * BLOCK, LANES), F32),
+            pltpu.VMEM((BLOCK, width_out), BF16),
+            pltpu.VMEM((BLOCK, LANES), F32),
+            pltpu.VMEM((BLOCK, 9 * LANES), BF16),
+            pltpu.VMEM((BLOCK, LANES), F32),
+            pltpu.VMEM((BLOCK, LANES), BF16),
+            pltpu.VMEM((4 * BLOCK, LANES), F32),
+            pltpu.VMEM((BLOCK, LANES), F32),
+            pltpu.VMEM((BLOCK, LANES), BF16),
+            pltpu.VMEM((BLOCK, LANES), BF16),
+            pltpu.VMEM((BLOCK, width_out), BF16),
+            pltpu.VMEM((BLOCK, width_out), BF16),
+            pltpu.VMEM((4 * BLOCK, LANES), BF16),
+            pltpu.VMEM(wholes[1], BF16),
+            pltpu.VMEM(wholes[2], BF16),
+            pltpu.VMEM(wholes[4], BF16),
+            pltpu.VMEM(wholes[3], BF16),
+            pltpu.VMEM((8, 24, 128), F32),
+            pltpu.VMEM((160, LANES), F32),
+            pltpu.VMEM((2, 4, 64, 128), F32),
+            pltpu.VMEM((2, 8, 64, 128), F32),
+            pltpu.VMEM((64, 128), F32),
+            pltpu.SemaphoreType.DMA((4,)),
             pltpu.SemaphoreType.DMA((7,)),
             pltpu.SemaphoreType.DMA((7, 6)),
             pltpu.SemaphoreType.DMA((7, 6)),
+            pltpu.SemaphoreType.DMA((7, 8)),
+            pltpu.SemaphoreType.DMA((7, 8)),
+            pltpu.SemaphoreType.DMA((2, 2)),
+            pltpu.SemaphoreType.DMA((2, 2)),
+            pltpu.SemaphoreType.DMA((3,)),
         ],
         compiler_params=pltpu.CompilerParams(
-            collective_id=0, has_side_effects=True, vmem_limit_bytes=60 * 2**20
+            collective_id=0, has_side_effects=True, vmem_limit_bytes=64 * 2**20
         ),
-        name="gather_weights",
-    )(*shards)
-
-
-def scatter_kernel(*refs):
-    grads, outs = refs[:7], refs[7:14]
-    rooms = [refs[14 + 6 * i : 20 + 6 * i] for i in range(7)]
-    send, recv = refs[14 + 42 :]
-    place = Place()
-    enter(place, LINK_PEERS)
-    run_staggered(
-        [scatter_steps(place, grads[i], rooms[i], outs[i], send.at[i], recv.at[i]) for i in range(7)]
-    )
-    for i in range(7):
-        scatter_sent(grads[i], rooms[i], outs[i], send.at[i])
-
-
-def scatter_all(grads):
-    shapes = [(one.shape[0] // 8, one.shape[1]) for one in grads]
-    return pl.pallas_call(
-        scatter_kernel,
-        out_shape=[jax.ShapeDtypeStruct(shape, jnp.bfloat16) for shape in shapes],
-        in_specs=[pl.BlockSpec(memory_space=pltpu.VMEM)] * 7,
-        out_specs=[pl.BlockSpec(memory_space=pltpu.VMEM)] * 7,
-        scratch_shapes=[
-            pltpu.VMEM(shape, jnp.bfloat16) for one in grads for shape in room_shapes(*one.shape)
-        ]
-        + [pltpu.SemaphoreType.DMA((7, 8)), pltpu.SemaphoreType.DMA((7, 8))],
-        compiler_params=pltpu.CompilerParams(
-            collective_id=1, has_side_effects=True, vmem_limit_bytes=62 * 2**20
-        ),
-        name="scatter_grads",
-    )(*grads)
-
-
-SUM_PEERS = ((0, 1), (0, 2), (0, 3), (1, 0), (2, 0), (3, 0), (4, 0), (5, 0), (6, 0), (7, 0))
-
-
-def sum_everywhere(place, near, far, send, recv):
-    own = near.at[place.d]
-    for bits in (1, 2, 3):
-        push(own, own, send.at[0], recv.at[0], place.peer(0, bits))
-    await_bytes(near.at[pl.ds(0, 3)], recv.at[0])
-    own_far = far.at[place.f]
-    own_far[...] = (near[0] + near[1]) + (near[2] + near[3])
-    for bits in range(1, 8):
-        push(own_far, own_far, send.at[1], recv.at[1], place.peer(bits, 0))
-    await_bytes(far.at[pl.ds(0, 7)], recv.at[1])
-    total = far[0]
-    for index in range(1, 8):
-        total = total + far[index]
-    await_bytes(near.at[pl.ds(0, 3)], send.at[0])
-    await_bytes(far.at[pl.ds(0, 7)], send.at[1])
-    return total
-
-
-def sum_kernel(local, out, near, far, send, recv):
-    place = Place()
-    near[place.d] = local[...]
-    enter(place, SUM_PEERS)
-    out[...] = sum_everywhere(place, near, far, send, recv)
-
-
-def sum_call(local, index):
-    rows = local.shape[0]
-    return pl.pallas_call(
-        sum_kernel,
-        out_shape=jax.ShapeDtypeStruct(local.shape, jnp.float32),
-        in_specs=[pl.BlockSpec(memory_space=pltpu.VMEM)],
-        out_specs=pl.BlockSpec(memory_space=pltpu.VMEM),
-        scratch_shapes=[
-            pltpu.VMEM((4, rows, 128), jnp.float32),
-            pltpu.VMEM((8, rows, 128), jnp.float32),
-            pltpu.SemaphoreType.DMA((2,)),
-            pltpu.SemaphoreType.DMA((2,)),
-        ],
-        compiler_params=pltpu.CompilerParams(collective_id=2 + index, has_side_effects=True),
-        name="sum_all",
-    )(local)
+        name="whole_step",
+    )(planes, cot, mask, gate, counts, chan, packed, *shards)
+    result, grad_planes, sums = outs[:3]
+    finals = [one.astype(F32) for one in outs[3:]]
+    result = result.reshape(slots, grid, grid, width_out)[:, :side, :side]
+    grad_images = grad_planes.reshape(2, 2, slots, grid, grid, width_in)[:, :, :, :side, :side]
+    grad_images = grad_images.transpose(2, 3, 0, 4, 1, 5).reshape(images.shape)
+    out_b = sums[0:32].reshape(4, 2, LANES)
+    both = sums[48:96].reshape(4, 3, LANES)
+
+    def narrow(at):
+        pair = sums[at : at + 8].reshape(2, LANES)
+        return own_shard((pair[1], pair[0]))
+
+    def wide(array, gain):
+        return own_shard((array[:, gain].reshape(-1), array[:, 0].reshape(-1)))
+
+    return (
+        result,
+        grad_images,
+        finals[0],
+        finals[1],
+        finals[2],
+        finals[3],
+        narrow(104),
+        narrow(96),
+        wide(both, 1),
+        wide(both, 2),
+        finals[4],
+        finals[5],
+        finals[6],
+        narrow(40),
+        narrow(32),
+        wide(out_b, 1),
+    )
+
+
+def fits(mesh):
+    return mesh.shape["fsdp"] == 8 and mesh.shape["dp"] == 4
 
 
 def gather_plain(shards):
@@ -428,17 +1173,8 @@
     return lax.psum(tuple(parts), "dp")
 
 
-MODE = {"fast": True, "calls": 0}
-
-
 def sum_pair(first, second):
-    width = first.shape[0]
-    if not MODE["fast"]:
-        return lax.psum((first, second), ("fsdp", "dp"))
-    packed = jnp.concatenate([first, second]).reshape(2 * width // 128, 128)
-    MODE["calls"] += 1
-    total = sum_call(packed, MODE["calls"] - 1).reshape(2, width)
-    return total[0], total[1]
+    return lax.psum((first, second), ("fsdp", "dp"))
 
 
 def silu_slope(values):
@@ -806,12 +1542,8 @@
     channel_b = (lane_ids < widths[1]).astype(jnp.float32)
     depth_gate = keep_gate.astype(jnp.float32)[:, None, None, None]
     inputs = images * mask_in.astype(jnp.bfloat16)
-    MODE["fast"] = lax.axis_size("fsdp") == 8 and lax.axis_size("dp") == 4
-    MODE["calls"] = 0
-    gather_now = gather_all if MODE["fast"] else gather_plain
-    scatter_now = scatter_all if MODE["fast"] else scatter_plain
     total_counts = lax.psum(local_counts, ("fsdp", "dp"))
-    gathered = gather_now((w_in_a, w_mid_a, w_out_a, w_proj_a, w_in_b, w_mid_b, w_out_b))
+    gathered = gather_plain((w_in_a, w_mid_a, w_out_a, w_proj_a, w_in_b, w_mid_b, w_out_b))
     norms = lax.all_gather(
         jnp.concatenate(
             [norm_in_a, norm_mid_a, norm_out_a, norm_proj_a, norm_in_b, norm_mid_b, norm_out_b], axis=1
@@ -839,7 +1571,7 @@
     grad_inputs, grads_a, norms_a = block_a_backward(
         grad_block, inputs, weights_a, stats_a, redone_a, mask_in, mask_out, channel_a
     )
-    finals = scatter_now(tuple(one.astype(jnp.bfloat16) for one in grads_a + grads_b))
+    finals = scatter_plain(tuple(one.astype(jnp.bfloat16) for one in grads_a + grads_b))
     final_in_a, final_mid_a, final_out_a, final_proj_a, final_in_b, final_mid_b, final_out_b = (
         one.astype(jnp.float32) for one in finals
     )
@@ -903,4 +1635,5 @@
         P(None, "fsdp"),
         P(None, "fsdp"),
     )
-    return jax.shard_map(body, mesh=mesh, in_specs=in_specs, out_specs=out_specs, check_vma=False)
+    step = body_fast if fits(mesh) else body
+    return jax.shard_map(step, mesh=mesh, in_specs=in_specs, out_specs=out_specs, check_vma=False)

time: 681 us -> 352 us (0.52); the launches traced: 671 us -> 351 us
  Pallas kernels: 391 us -> 312 us
  blocking collectives: 70.3 us -> 0 us
  matrix products: 69.9 us -> 0 us
  other arithmetic: 84.7 us -> 21 us
  local copies, waits for them, and re-layouts: 52.9 us -> 17.4 us
    pallas_call x14 -> x1, Pallas kernels: 391 us -> 312 us  [body_fast(): pl.pallas_call(step_kernel, out_shape=[jax.ShapeDtypeStruct((BLOCK, width...]
    dot_general x21 -> x0, matrix products: 69.9 us -> none  [the longest x7 23 us: contract(): lax.dot_general(left_side, right_side, (((0, 1, 2), (0, 1, 2)), ((), ()))...]
    psum x1 -> x0, blocking collectives: 45.1 us -> none  [body(): total_counts = lax.psum(local_counts, ('fsdp', 'dp'))]
    all_gather x1 -> x0, blocking collectives: 25.2 us -> none  [body(): lax.all_gather(jnp.concatenate([norm_in_a, norm_mid_a, norm_out_a, norm_p...]
    convert_element_type x26 -> x18, other arithmetic: 30.3 us -> 13.9 us  [the longest x7 6.63 us: body_fast(): finals = [one.astype(F32) for one in outs[3:]]]
    reduce_sum x6 -> x1, other arithmetic: 13.6 us -> 1.3 us  [body_fast(): jnp.sum(half * half)]
    div x9 -> x0, other arithmetic: 12.1 us -> none  [the longest x6 8.06 us: norm_backward(): shift_sum / pixel_total]
    pad x2 -> x1, local copies, waits for them, and re-layouts: 12 us -> 1.16 us  [body_fast(): jnp.pad(cotangent, ((0, 0), (0, 1), (0, 1), (0, 0)))]
where the time goes in v2:
time: 352 us; the launch traced here: 351 us
  Pallas kernels  312 us (89%)
  other arithmetic  21 us (6%)
  local copies, waits for them, and re-layouts  17.4 us (5%)
    pallas_call x1, Pallas kernels, body_fast(): pl.pallas_call(step_kernel, out_shape=[jax.ShapeDtypeStruct((BLOCK, width...  312 us

profile of v2, /device:TPU:1, one launch (start us, length us, event | category | flops | bytes accessed | tf_op | source)
XLA Modules:
  0.0 351.5 jit_solution(14413011705197088722)
XLA Ops:
  0.7 0.7 bitcast_convert_fusion.2
  3.9 0.8 slice_convert_fusion.2
  4.7 0.8 slice_convert_fusion.1
  5.4 0.8 slice_convert_fusion
  6.2 1.8 concatenate.75.norm_hbm
  8.0 1.3 multiply_reduce_fusion
  9.3 1.4 add_convert_fusion
  11.5 2.3 copy.46
  13.8 1.9 pad_multiply_fusion
  15.8 0.8 broadcast_in_dim.26.mask_ref
  17.0 1.2 pad.27.clone
  18.4 0.8 broadcast_in_dim.56.gate_ref
  19.8 312.3 %whole_step.1 = (bf16[256,2048]{1,0:T(8,128)(2,1)}, bf16[1024,1024]{1,0:T(8,128)(2,1)}, f32[112,128]{1,0:T(8,128)}, bf16[128,512]{1,0:T(8,128)(2,1)}, bf16[576,5...) custom-call(bf16[1024,1024]{1,0:T(8,128)(2,1)} %bitcast.101, ...), custom_call_target="tpu_custom_call" | custom-call | tf_op jit(solution)/shard_map/whole_step/pallas_call | solution.py:1070
  333.6 0.8 slice_bitcast_fusion.2
  335.9 0.7 slice.134
  338.9 1.7 slice_bitcast_fusion
  340.6 2.6 copy.42
  343.2 1.6 copy.43
  344.8 1.2 convert_element_type.175
  346.0 1.2 convert_element_type.179
  347.2 1.1 convert_element_type.177
  348.2 0.8 convert_element_type.176
  349.1 0.9 convert_element_type.178
  349.9 0.8 convert_element_type.180
  (67 shorter events, 10.8 us)
Async XLA Ops:
  13.8 2.8 copy-start.1
  15.7 2.5 copy-start.10
  15.7 3.4 copy-start.9
  340.6 2.6 copy-start
  343.2 1.7 copy-start.3
  343.2 2.8 copy-start.2
  344.8 2.3 copy-start.4
  346.0 2.3 copy-start.7
  346.0 3.1 copy-start.6
  346.0 3.9 %copy-start.5 = (bf16[64,2048]{1,0:T(8,128)(2,1)S(1)}, bf16[64,2048]{1,0:T(8,128)(2,1)}, u32[]{:S(2)}) copy-start(bf16[64,2048]{1,0:T(8,128)(2,1)} %get-tuple-element.35) | copy-start | bytes 786436
  347.2 3.6 %copy-start.8 = (bf16[128,512]{1,0:T(8,128)(2,1)S(1)}, bf16[128,512]{1,0:T(8,128)(2,1)}, u32[]{:S(2)}) copy-start(bf16[128,512]{1,0:T(8,128)(2,1)} %get-tuple-element.28) | copy-start | bytes 393220

commit v3 on v0

--- a/solution.py
+++ b/solution.py
@@ -1,9 +1,1493 @@
+import functools
+
 import jax
 import jax.numpy as jnp
 from jax import lax
+from jax.experimental import pallas as pl
+from jax.experimental.pallas import tpu as pltpu
 from jax.sharding import PartitionSpec as P
 
 EPSILON = 1e-05
+BY_MESH = pl.DeviceIdType.MESH
+F32 = jnp.float32
+BF16 = jnp.bfloat16
+NAMES = ("in_a", "mid_a", "out_a", "proj_a", "in_b", "mid_b", "out_b")
+BLOCK = 256
+LANES = 512
+CHUNK = 32
+SIDE = 7
+TAPS = [(u, v) for u in range(3) for v in range(3)]
+LINK_PEERS = ((1, 0), (2, 0), (4, 0), (6, 0), (0, 2), (0, 1))
+CHIP_PEERS = tuple((a, b) for a in (7, 6, 5, 4, 3, 2, 1, 0) for b in (2, 0) if a or b)
+PIECES = {
+    "in_a": [(0, 128, 4, 4)],
+    "mid_a": [(0, 96, 4, 4), (96, 96, 4, 4), (192, 96, 4, 4), (288, 96, 4, 4), (384, 96, 4, 4), (480, 96, 8, 4)],
+    "out_a": [(0, 32, 6, 5), (32, 32, 4, 5)],
+    "proj_a": [(0, 64, 6, 5), (64, 64, 4, 5)],
+    "in_b": [(0, 128, 4, 4), (128, 128, 4, 4)],
+    "mid_b": [(0, 96, 4, 4), (96, 96, 4, 4), (192, 96, 4, 4), (288, 96, 4, 4), (384, 96, 4, 4), (480, 96, 8, 4)],
+    "out_b": [(0, 32, 6, 5), (32, 32, 4, 5)],
+}
+RUN = [
+    253, 297, 300, 301, 295, 272, 273, 302, 276, 277, 278, 303, 279, 48, 304, 280, 51, 305, 281, 52, 316, 292,
+    53, 69, 54, 72, 55, 317, 73, 56, 74, 293, 90, 312, 75, 93, 67, 244, 15, 94, 14, 13, 313, 95, 298, 76, 77,
+    68, 96, 299, 288, 306, 63, 307, 88, 97, 98, 12, 289, 64, 308, 309, 246, 19, 18, 17, 89, 310, 274, 84, 311,
+    109, 275, 49, 314, 85, 50, 315, 110, 282, 16, 57, 105, 283, 58, 250, 296, 70, 106, 284, 59, 71, 248, 23,
+    22, 78, 285, 79, 60, 91, 286, 61, 92, 80, 287, 21, 62, 99, 245, 290, 100, 65, 81, 291, 20, 27, 101, 26,
+    25, 82, 83, 66, 86, 102, 103, 104, 24, 87, 247, 31, 107, 30, 29, 108, 249, 28, 35, 34, 33, 32, 39, 38, 37,
+    36, 43, 266, 267, 42, 41, 40, 47, 116, 261, 46, 45, 262, 263, 135, 136, 44, 3, 114, 256, 2, 156, 257, 157,
+    127, 1, 128, 129, 130, 131, 132, 177, 178, 148, 0, 7, 112, 251, 6, 5, 149, 150, 252, 119, 120, 151, 268,
+    152, 269, 198, 199, 153, 117, 169, 264, 265, 170, 4, 11, 219, 115, 258, 10, 9, 140, 137, 138, 141, 133,
+    220, 134, 171, 172, 190, 191, 259, 173, 260, 174, 240, 241, 161, 8, 113, 254, 255, 270, 158, 121, 122,
+    123, 124, 125, 126, 271, 111, 294, 162, 159, 118, 154, 179, 155, 192, 193, 211, 212, 194, 195, 232, 182,
+    233, 142, 143, 144, 145, 146, 147, 183, 180, 139, 200, 213, 214, 175, 215, 234, 216, 235, 236, 203, 237,
+    176, 204, 224, 163, 225, 201, 164, 221, 165, 242, 166, 167, 222, 168, 196, 243, 160, 197, 184, 217, 185,
+    238, 218, 186, 205, 239, 187, 206, 226, 188, 207, 227, 189, 208, 228, 181, 209, 229, 210, 230, 231, 202,
+    223,
+]
+
+
+def flip(index, bits):
+    out = index
+    for bit in (1, 2, 4):
+        if bits & bit:
+            out = out + bit - 2 * bit * ((index // bit) % 2)
+    return out
+
+
+class Place:
+    def __init__(self):
+        self.f = lax.axis_index("fsdp")
+        self.d = lax.axis_index("dp")
+        self.y = self.f % 2
+        self.z = self.f // 2
+        self.c = self.d % 2
+        self.x = self.d // 2
+
+    def peer(self, f_bits, d_bits):
+        return (flip(self.f, f_bits), flip(self.d, d_bits))
+
+
+def enter(place, peers):
+    barrier = pltpu.get_barrier_semaphore()
+    for f_bits, d_bits in peers:
+        pl.semaphore_signal(barrier, inc=1, device_id=place.peer(f_bits, d_bits), device_id_type=BY_MESH)
+    pl.semaphore_wait(barrier, len(peers))
+
+
+def push(source, target, send_sem, recv_sem, device):
+    pltpu.make_async_remote_copy(
+        src_ref=source,
+        dst_ref=target,
+        send_sem=send_sem,
+        recv_sem=recv_sem,
+        device_id=device,
+        device_id_type=BY_MESH,
+    ).start()
+
+
+def await_bytes(view, sem):
+    pltpu.make_async_copy(view, view, sem).wait()
+
+
+def await_count(ref, count, sem):
+    if not count:
+        return
+    rows_most, columns_most = ref.shape
+    for columns in range(columns_most, 0, -128):
+        rows = count // columns
+        if count % columns == 0 and rows % 16 == 0 and rows <= rows_most:
+            await_bytes(ref.at[pl.ds(0, rows), pl.ds(0, columns)], sem)
+            return
+    raise ValueError(count)
+
+
+def rows_of(start, size):
+    return pl.ds(pl.multiple_of(start, 16), size)
+
+
+def cols_of(start, size):
+    return pl.ds(pl.multiple_of(start, 128), size)
+
+
+class Gather:
+    def __init__(self, place, shard, whole, start, rows, wide_a, send, recv):
+        self.place, self.shard, self.whole = place, shard, whole
+        self.start, self.rows, self.wide_a = start, rows, wide_a
+        self.local, self.send, self.recv = recv.at[6], send, recv
+        self.total, columns = shard.shape
+        self.half = columns // 2
+        self.wide_b = self.half - wide_a
+        self.part = rows // 2
+        self.col_0 = place.c * self.half
+        self.row_q = start + place.x * self.part
+        self.row_o = start + self.part - place.x * self.part
+        self.near_count = self.part * wide_a + rows * self.wide_b + 3 * self.part * self.half
+
+    def view(self, bits, row, rows, from_col, columns):
+        block = flip(self.place.f, bits) * self.total
+        return self.whole.at[rows_of(block + row, rows), cols_of(self.col_0 + from_col, columns)]
+
+    def pass_on(self, bits, row, rows, from_col, columns, leg, device):
+        view = self.view(bits, row, rows, from_col, columns)
+        push(view, view, self.send, self.recv.at[leg], device)
+
+    def first(self):
+        half, part, place = self.half, self.part, self.place
+        pltpu.make_async_copy(
+            self.shard.at[pl.ds(self.start, self.rows), cols_of(self.col_0, half)],
+            self.view(0, self.start, self.rows, 0, half),
+            self.local,
+        ).start()
+        for bits in (6, 4, 2):
+            push(
+                self.shard.at[rows_of(self.row_q, part), cols_of(self.col_0, half)],
+                self.view(0, self.row_q, part, 0, half),
+                self.send,
+                self.recv.at[0],
+                place.peer(bits, 0),
+            )
+
+    def own(self):
+        place = self.place
+        for row, rows, col, columns in (
+            (self.row_q, self.part, 0, self.wide_a),
+            (self.start, self.rows, self.wide_a, self.wide_b),
+        ):
+            if columns:
+                push(
+                    self.shard.at[rows_of(row, rows), cols_of(self.col_0 + col, columns)],
+                    self.view(0, row, rows, col, columns),
+                    self.send,
+                    self.recv.at[1],
+                    place.peer(1, 0),
+                )
+
+    def one(self):
+        place = self.place
+        await_count(self.whole, self.rows * self.half, self.local)
+        await_count(self.whole, 3 * self.part * self.half, self.recv.at[0])
+        for bits in (2, 4, 6):
+            self.pass_on(bits, self.row_q, self.part, 0, self.half, 1, place.peer(1, 0))
+            self.pass_on(bits, self.row_q, self.part, 0, self.half, 2, place.peer(0, 2))
+
+    def two(self):
+        place = self.place
+        await_count(self.whole, self.near_count, self.recv.at[1])
+        await_count(self.whole, 3 * self.part * self.half, self.recv.at[2])
+        if self.wide_a:
+            for bits in (1, 3, 5, 7):
+                self.pass_on(bits, self.row_q, self.part, 0, self.wide_a, 3, place.peer(0, 2))
+        if self.wide_b:
+            for bits in (2, 4, 6):
+                self.pass_on(bits, self.row_o, self.part, self.wide_a, self.wide_b, 4, place.peer(1, 0))
+
+    def three(self):
+        place = self.place
+        await_count(self.whole, 4 * self.part * self.wide_a, self.recv.at[3])
+        await_count(self.whole, 3 * self.part * self.wide_b, self.recv.at[4])
+        for bits in range(8):
+            self.pass_on(bits, self.start, self.rows, 0, self.half, 5, place.peer(0, 1))
+
+    def four(self):
+        await_count(self.whole, 8 * self.rows * self.half, self.recv.at[5])
+
+    def sent(self):
+        count = 6 * self.part * self.half + self.near_count + 8 * self.rows * self.half
+        count += 4 * self.part * self.wide_a + 3 * self.part * self.wide_b
+        await_count(self.whole, count, self.send)
+
+
+def chunk_of(rows, columns):
+    best = 16
+    for chunk in range(16, rows + 1, 16):
+        if rows % chunk == 0 and chunk * columns <= 16384:
+            best = chunk
+    return best
+
+
+def add_blocks(blocks, rows, columns, target, source):
+    chunk = chunk_of(rows, columns)
+    each = rows // chunk
+
+    def step(index, carry):
+        block, start = index // each, pl.multiple_of((index % each) * chunk, 16)
+        into, more = target(block, start, chunk), source(block, start, chunk)
+        into[...] = (into[...].astype(F32) + more[...].astype(F32)).astype(BF16)
+        return carry
+
+    lax.fori_loop(0, blocks * each, step, 0)
+
+
+class Scatter:
+    def __init__(self, place, grad, room, out, start, rows, wide_a, first, send, recv):
+        self.place, self.grad, self.out = place, grad, out
+        self.start, self.rows, self.wide_a = start, rows, wide_a
+        self.first, self.send, self.recv = first, send, recv
+        total, columns = room.shape
+        self.total = total = total // 8
+        self.half = half = columns // 2
+        self.wide_b = wide_b = half - wide_a
+        self.part = part = rows // 2
+        self.room = room
+        self.from_core = room.at[:, pl.ds(0, half)]
+
+        def landing(row, count, col, width):
+            return room.at[pl.ds(row, count), pl.ds(half + col, width)] if width else None
+
+        self.a_x = landing(4 * start, 4 * rows, 0, wide_a)
+        self.a_y = landing(4 * total + 2 * start, 2 * rows, 0, wide_a)
+        self.a_z = landing(6 * total + 3 * start // 2, 3 * part, 0, wide_a)
+        self.b_y = landing(4 * start, 4 * rows, wide_a, wide_b)
+        self.b_z = landing(4 * total + 3 * start, 3 * rows, wide_a, wide_b)
+        self.b_x = landing(7 * total + start // 2, part, wide_a, wide_b)
+        self.col_0 = place.c * half
+        self.row_q = start + place.x * part
+        self.row_o = start + part - place.x * part
+
+    def push(self, source, target, leg, device):
+        push(source, target, self.send, self.recv.at[leg - 1], device)
+
+    def zero(self):
+        other = self.half - self.col_0
+        source = self.grad.at[:, cols_of(other, self.half)]
+        push(source, self.from_core, self.first.at[0], self.first.at[1], self.place.peer(0, 1))
+
+    def core(self, row, rows, from_col, columns):
+        return self.from_core.at[rows_of(row, rows), pl.ds(from_col, columns)]
+
+    def mine(self, row, rows, from_col, columns):
+        return self.core(self.place.f * self.total + row, rows, from_col, columns)
+
+    def one(self, first, last):
+        place, total, part, rows = self.place, self.total, self.part, self.rows
+        if first:
+            await_bytes(self.from_core, self.first.at[1])
+        add_blocks(
+            8,
+            rows,
+            self.half,
+            lambda b, s, n: self.core(b * total + self.start + s, n, 0, self.half),
+            lambda b, s, n: self.grad.at[rows_of(b * total + self.start + s, n), cols_of(self.col_0, self.half)],
+        )
+        if last:
+            await_bytes(self.from_core, self.first.at[0])
+        if self.wide_a:
+            for block in range(8):
+                self.push(
+                    self.core(block * total + self.row_o, part, 0, self.wide_a),
+                    self.a_x.at[pl.ds(block * part, part)],
+                    1,
+                    place.peer(0, 2),
+                )
+        if self.wide_b:
+            for level in range(4):
+                self.push(
+                    self.core((2 * level + 1 - place.y) * total + self.start, rows, self.wide_a, self.wide_b),
+                    self.b_y.at[pl.ds(level * rows, rows)],
+                    2,
+                    place.peer(1, 0),
+                )
+
+    def two(self):
+        place, total, part, rows = self.place, self.total, self.part, self.rows
+        if self.wide_a:
+            await_bytes(self.a_x, self.recv.at[0])
+            add_blocks(
+                8,
+                part,
+                self.wide_a,
+                lambda b, s, n: self.core(b * total + self.row_q + s, n, 0, self.wide_a),
+                lambda b, s, n: self.a_x.at[rows_of(b * part + s, n)],
+            )
+            for level in range(4):
+                self.push(
+                    self.core((2 * level + 1 - place.y) * total + self.row_q, part, 0, self.wide_a),
+                    self.a_y.at[pl.ds(level * part, part)],
+                    3,
+                    place.peer(1, 0),
+                )
+        if self.wide_b:
+            await_bytes(self.b_y, self.recv.at[1])
+            add_blocks(
+                4,
+                rows,
+                self.wide_b,
+                lambda b, s, n: self.core((2 * b + place.y) * total + self.start + s, n, self.wide_a, self.wide_b),
+                lambda b, s, n: self.b_y.at[rows_of(b * rows + s, n)],
+            )
+            for slot, bits in enumerate((6, 4, 2)):
+                self.push(
+                    self.core(flip(place.f, bits) * total + self.start, rows, self.wide_a, self.wide_b),
+                    self.b_z.at[pl.ds(slot * rows, rows)],
+                    4,
+                    place.peer(bits, 0),
+                )
+
+    def sum_four(self, row, rows, col, wide, landed, store):
+        chunk = chunk_of(rows, wide)
+
+        def step(index, carry):
+            start = pl.multiple_of(index * chunk, 16)
+            total = self.mine(row + start, chunk, col, wide)[...].astype(F32)
+            for slot in range(3):
+                total = total + landed[rows_of(slot * rows + start, chunk)].astype(F32)
+            store(start, chunk, total.astype(BF16))
+            return carry
+
+        lax.fori_loop(0, rows // chunk, step, 0)
+
+    def three(self):
+        place, total, part, rows = self.place, self.total, self.part, self.rows
+        if self.wide_a:
+            await_bytes(self.a_y, self.recv.at[2])
+            add_blocks(
+                4,
+                part,
+                self.wide_a,
+                lambda b, s, n: self.core((2 * b + place.y) * total + self.row_q + s, n, 0, self.wide_a),
+                lambda b, s, n: self.a_y.at[rows_of(b * part + s, n)],
+            )
+            for slot, bits in enumerate((6, 4, 2)):
+                self.push(
+                    self.core(flip(place.f, bits) * total + self.row_q, part, 0, self.wide_a),
+                    self.a_z.at[pl.ds(slot * part, part)],
+                    5,
+                    place.peer(bits, 0),
+                )
+        if self.wide_b:
+            await_bytes(self.b_z, self.recv.at[3])
+
+            def keep(start, chunk, value):
+                self.mine(self.start + start, chunk, self.wide_a, self.wide_b)[...] = value
+
+            self.sum_four(self.start, rows, self.wide_a, self.wide_b, self.b_z, keep)
+            self.push(self.mine(self.row_o, part, self.wide_a, self.wide_b), self.b_x, 6, place.peer(0, 2))
+
+    def four(self):
+        place, part = self.place, self.part
+        if self.wide_a:
+            await_bytes(self.a_z, self.recv.at[4])
+
+            def keep(start, chunk, value):
+                self.out[rows_of(self.row_q + start, chunk), cols_of(self.col_0, self.wide_a)] = value
+
+            self.sum_four(self.row_q, part, 0, self.wide_a, self.a_z, keep)
+        if self.wide_b:
+            await_bytes(self.b_x, self.recv.at[5])
+            chunk = chunk_of(part, self.wide_b)
+
+            def step(index, carry):
+                start = pl.multiple_of(index * chunk, 16)
+                total = self.mine(self.row_q + start, chunk, self.wide_a, self.wide_b)[...].astype(F32)
+                total = total + self.b_x[rows_of(start, chunk)].astype(F32)
+                columns = cols_of(self.col_0 + self.wide_a, self.wide_b)
+                self.out[rows_of(self.row_q + start, chunk), columns] = total.astype(BF16)
+                return carry
+
+            lax.fori_loop(0, part // chunk, step, 0)
+        block = self.out.at[rows_of(self.row_q, part), cols_of(self.col_0, self.half)]
+        self.push(block, block, 7, place.peer(0, 2))
+
+    def five(self):
+        await_bytes(self.out.at[pl.ds(0, self.part), pl.ds(0, self.half)], self.recv.at[6])
+        block = self.out.at[pl.ds(self.start, self.rows), cols_of(self.col_0, self.half)]
+        self.push(block, block, 8, self.place.peer(0, 1))
+
+    def six(self):
+        await_bytes(self.out.at[pl.ds(0, self.rows), pl.ds(0, self.half)], self.recv.at[7])
+
+    def sent(self):
+        await_count(self.room, 18 * self.part * self.half, self.send)
+
+
+def mm(left, right):
+    return jnp.dot(left, right, preferred_element_type=F32)
+
+
+def mm_nt(left, right):
+    return lax.dot_general(left, right, (((1,), (1,)), ((), ())), preferred_element_type=F32)
+
+
+def mm_tn(left, right):
+    return lax.dot_general(left, right, (((0,), (0,)), ((), ())), preferred_element_type=F32)
+
+
+def loop(count, step):
+    def body_of(index, carry):
+        step(index)
+        return carry
+
+    lax.fori_loop(0, count, body_of, 0)
+
+
+def at_block(index, size):
+    return pl.ds(pl.multiple_of(index * size, size), size)
+
+
+def slope_of(values):
+    gate = jax.nn.sigmoid(values)
+    return gate * (1.0 + values * (1.0 - gate))
+
+
+def fold(values):
+    total = values[0:8]
+    for start in range(8, values.shape[0], 8):
+        total = total + values[start : start + 8]
+    return total
+
+
+def column_sums(count, width, terms):
+    def step(index, carry):
+        start = pl.multiple_of(index * CHUNK, CHUNK)
+        return tuple(total + fold(one) for total, one in zip(carry, terms(start)))
+
+    zero = jnp.zeros((8, LANES), F32)
+    totals = lax.fori_loop(0, count, step, (zero,) * width)
+    return [jnp.sum(one, axis=0, keepdims=True) for one in totals]
+
+
+class Vectors:
+    def __init__(self, ref):
+        self.ref, self.used = ref, 0
+
+    def put(self, row):
+        at = self.used
+        self.used += 1
+        self.ref[at : at + 1, :] = row
+        return at
+
+    def get(self, at):
+        return self.ref[at : at + 1, :]
+
+
+class Totals:
+    def __init__(self, place, short, long, tot, send, recv):
+        self.place, self.short, self.long, self.tot, self.send, self.recv = place, short, long, tot, send, recv
+        self.turns, self.is_long, self.rows = [1, 1], 0, 0
+
+    def slot(self, at):
+        ref = self.long if self.is_long else self.short
+        return ref.at[self.turn, at, pl.ds(0, self.rows)]
+
+    def slots(self, at, count):
+        ref = self.long if self.is_long else self.short
+        return ref.at[self.turn, pl.ds(at, count), pl.ds(0, self.rows)]
+
+    def spread(self, at, peers, phase):
+        own = self.slot(at)
+        for bits in peers:
+            push(own, own, self.sem(self.send, phase), self.sem(self.recv, phase), self.place.peer(*bits))
+
+    def sem(self, sems, phase):
+        return sems.at[self.is_long, self.turn, phase]
+
+    def gather(self, at, count, peers, phase):
+        await_bytes(self.slots(at, peers), self.sem(self.recv, phase))
+        ref = self.long if self.is_long else self.short
+        total = ref[self.turn, at, 0 : self.rows, :]
+        for index in range(at + 1, at + count):
+            total = total + ref[self.turn, index, 0 : self.rows, :]
+        return total
+
+    def start(self, rows_of_values, extra=None):
+        count = 4 * len(rows_of_values) + (8 if extra is not None else 0)
+        self.is_long = 1 if count > 16 else 0
+        self.turns[self.is_long] = self.turn = 1 - self.turns[self.is_long]
+        self.rows = count
+        own = self.slot(self.place.c)
+        at = 0
+        for row in rows_of_values:
+            for lane in range(0, LANES, 128):
+                own[at : at + 1, :] = row[:, lane : lane + 128]
+                at += 1
+        if extra is not None:
+            own[at : at + 8, :] = extra
+        self.spread(self.place.c, ((0, 1),), 0)
+
+    def middle(self):
+        place = self.place
+        total = self.gather(0, 2, 1, 0)
+        if self.is_long:
+            self.slot(2 + 2 * place.y + place.x)[...] = total
+            self.spread(2 + 2 * place.y + place.x, ((1, 2), (1, 0), (0, 2)), 1)
+        else:
+            self.slot(2 + 2 * place.f + place.x)[...] = total
+            self.spread(2 + 2 * place.f + place.x, CHIP_PEERS, 1)
+
+    def late(self):
+        if self.is_long:
+            self.slot(6 + self.place.z)[...] = self.gather(2, 4, 3, 1)
+            self.spread(6 + self.place.z, ((6, 0), (4, 0), (2, 0)), 2)
+
+    def end(self):
+        if self.is_long:
+            self.tot[0 : self.rows, :] = self.gather(6, 4, 3, 2)
+        else:
+            self.tot[0 : self.rows, :] = self.gather(2, 16, 15, 1)
+        for phase, count in enumerate((1, 3, 3) if self.is_long else (1, 15)):
+            await_bytes(self.slots(0, count), self.sem(self.send, phase))
+
+    def row(self, index):
+        at = 4 * index
+        return jnp.concatenate([self.tot[at + k : at + k + 1, :] for k in range(4)], axis=1)
+
+    def wide(self, at):
+        return jnp.concatenate([self.tot[at : at + 1, :]] * 4, axis=1)
+
+
+def step_kernel(
+    img_hbm,
+    cot_hbm,
+    sides,
+    keep,
+    widths,
+    norm_in_a,
+    norm_mid_a,
+    norm_out_a,
+    norm_proj_a,
+    norm_in_b,
+    norm_mid_b,
+    norm_out_b,
+    sh_in_a,
+    sh_mid_a,
+    sh_out_a,
+    sh_proj_a,
+    sh_in_b,
+    sh_mid_b,
+    sh_out_b,
+    result_hbm,
+    images_hbm,
+    own_hbm_in_a,
+    own_hbm_mid_a,
+    own_hbm_out_a,
+    own_hbm_proj_a,
+    own_hbm_in_b,
+    own_hbm_mid_b,
+    own_hbm_out_b,
+    out_hbm_in_a,
+    out_hbm_mid_a,
+    out_hbm_out_a,
+    out_hbm_proj_a,
+    out_hbm_in_b,
+    out_hbm_mid_b,
+    out_hbm_out_b,
+    own_in_a,
+    own_mid_a,
+    own_out_a,
+    own_proj_a,
+    own_in_b,
+    own_mid_b,
+    own_out_b,
+    out_in_a,
+    out_mid_a,
+    out_out_a,
+    out_proj_a,
+    out_in_b,
+    out_mid_b,
+    out_out_b,
+    w_in_a,
+    w_mid_a,
+    w_out_a,
+    w_proj_a,
+    w_in_b,
+    w_mid_b,
+    w_out_b,
+    raw,
+    cot,
+    x,
+    c1,
+    cols_a,
+    c2,
+    a2,
+    c3,
+    cp,
+    bo,
+    feed,
+    d1,
+    cols_b,
+    d2,
+    b2,
+    d3,
+    dz,
+    dm,
+    df,
+    dout,
+    dproj,
+    g_mid,
+    g_out,
+    g_in,
+    g_proj,
+    mask_ref,
+    gate_ref,
+    move,
+    norms,
+    block_ref,
+    vec_ref,
+    short,
+    long,
+    tot,
+    sums,
+    io_sem,
+    link_send,
+    link_recv,
+    core_sem,
+    ar_send,
+    ar_recv,
+    nb_sem,
+    out_sem,
+    free_sem,
+):
+    place = Place()
+    shards = dict(zip(NAMES, (sh_in_a, sh_mid_a, sh_out_a, sh_proj_a, sh_in_b, sh_mid_b, sh_out_b)))
+    wholes = dict(zip(NAMES, (w_in_a, w_mid_a, w_out_a, w_proj_a, w_in_b, w_mid_b, w_out_b)))
+    outs = dict(zip(NAMES, (out_in_a, out_mid_a, out_out_a, out_proj_a, out_in_b, out_mid_b, out_out_b)))
+    owned = dict(zip(NAMES, (own_in_a, own_mid_a, own_out_a, own_proj_a, own_in_b, own_mid_b, own_out_b)))
+    own_hbm = (own_hbm_in_a, own_hbm_mid_a, own_hbm_out_a, own_hbm_proj_a, own_hbm_in_b, own_hbm_mid_b, own_hbm_out_b)
+    out_hbm = (out_hbm_in_a, out_hbm_mid_a, out_hbm_out_a, out_hbm_proj_a, out_hbm_in_b, out_hbm_mid_b, out_hbm_out_b)
+    own_copies = [pltpu.make_async_copy(owned[n], own_hbm[i], out_sem.at[0, i]) for i, n in enumerate(NAMES)]
+    out_copies = [pltpu.make_async_copy(outs[n], out_hbm[i], out_sem.at[1, i]) for i, n in enumerate(NAMES)]
+    small = dict(zip(NAMES, (norm_in_a, norm_mid_a, norm_out_a, norm_proj_a, norm_in_b, norm_mid_b, norm_out_b)))
+    grads = dict(mid_a=g_mid, mid_b=g_mid, out_a=g_out, out_b=g_out, in_b=g_in, proj_a=g_proj)
+    grads["in_a"] = g_in.at[pl.ds(0, wholes["in_a"].shape[0])]
+    todo = {}
+
+    def token(name):
+        def keep_it(function):
+            todo[name] = function
+            return function
+
+        return keep_it
+
+    def tokens(name, count, each, step):
+        for part in range(count):
+            todo[f"{name}.{part}"] = functools.partial(loop, each, lambda k, first=part * each: step(first + k))
+
+    gathers, scatters, at = {}, {}, 0
+    left = {name: len(PIECES[name]) for name in NAMES}
+
+    def finish_piece(name, piece):
+        piece.six()
+        left[name] -= 1
+        if not left[name]:
+            out_copies[NAMES.index(name)].start()
+
+    for name in NAMES:
+        eighth = shards[name].shape[1] // 16
+        for n, (start, rows, way_in, way_out) in enumerate(PIECES[name]):
+            sems = link_send.at[at], link_recv.at[at]
+            g = Gather(place, shards[name], wholes[name], start, rows, way_in * eighth, *sems)
+            first_sem = core_sem.at[NAMES.index(name)]
+            s = Scatter(
+                place, grads[name], wholes[name], outs[name], start, rows, way_out * eighth, first_sem, *sems
+            )
+            gathers[name, n], scatters[name, n] = g, s
+            at += 1
+            key = f"{name}.{n}"
+            todo["z." + key], todo["o." + key], todo["L1." + key] = g.first, g.own, g.one
+            todo["L2." + key], todo["L3." + key] = g.two, g.three
+            if n == 0:
+                todo["S0." + name] = s.zero
+            todo["S1." + key] = functools.partial(s.one, n == 0, n == len(PIECES[name]) - 1)
+            todo["S2." + key], todo["S3." + key], todo["S4." + key] = s.two, s.three, s.four
+            todo["S5." + key] = s.five
+            todo["S6." + key] = functools.partial(finish_piece, name, s)
+
+        def arrived(name=name):
+            for n in range(len(PIECES[name])):
+                gathers[name, n].four()
+
+        todo["W." + name] = arrived
+
+    vec = Vectors(vec_ref)
+    totals = Totals(place, short, long, tot, ar_send, ar_recv)
+    state, scales, params = {}, {}, {}
+    for n in range(1, 13):
+        todo[f"A{n}m"] = totals.middle
+        todo[f"A{n}l"] = totals.late
+
+    image_copy = pltpu.make_async_copy(img_hbm, raw, io_sem.at[0])
+    cot_copy = pltpu.make_async_copy(cot_hbm, cot, io_sem.at[1])
+    result_copy = pltpu.make_async_copy(cot, result_hbm, io_sem.at[2])
+    grad_copy = pltpu.make_async_copy(raw, images_hbm, io_sem.at[3])
+
+    @token("enter")
+    def _():
+        image_copy.start()
+        cot_copy.start()
+        odd = (place.f % 2).astype(F32)
+        block_ref[...] = jnp.zeros_like(block_ref)
+        at = 0
+        for name in NAMES:
+            values = small[name][...].astype(F32)
+            if values.shape[1] < 128:
+                move[0:8, 0:128] = jnp.zeros((8, 128), F32)
+                move[0:2, 0 : values.shape[1]] = values
+                plain = move[0:8, 0:128]
+                values = (plain + (pltpu.roll(plain, 64, 1) - plain) * odd)[0:2]
+            for lane in range(0, values.shape[1], 128):
+                block_ref[at : at + 1, :] = values[0:1, lane : lane + 128]
+                block_ref[at + 10 : at + 11, :] = values[1:2, lane : lane + 128]
+                at += 1
+        norms[place.f] = block_ref[...]
+        enter(place, ((0, 1),) + CHIP_PEERS)
+        for bits in (7, 6, 5, 4, 3, 2, 1):
+            push(block_ref, norms.at[place.f], nb_sem.at[0], nb_sem.at[1], place.peer(bits, 0))
+
+    @token("prep")
+    def _():
+        pixel = lax.broadcasted_iota(jnp.int32, (BLOCK, 128), 0)
+        slot = pixel % 4
+
+        def by_slot(values):
+            return jnp.where(slot == 0, values[0], jnp.where(slot == 1, values[1], jnp.where(slot == 2, values[2], values[3])))
+
+        half = by_slot([sides[i] // 2 for i in range(4)])
+        inside = ((pixel // 4) % 8 < half) & (pixel // 32 < half)
+        mask_ref[...] = jnp.where(inside, 1.0, 0.0).astype(F32)
+        gate_ref[...] = by_slot([keep[i] for i in range(4)]).astype(F32)
+        move[...] = jnp.zeros_like(move)
+        image_copy.wait()
+
+        def plane_rows(row):
+            mask = jnp.concatenate([mask_ref[at_block(row, CHUNK), :]] * (x.shape[1] // 128), axis=1)
+            for row_par in range(2):
+                for col_par in range(2):
+                    for col in range(SIDE):
+                        move[4 * col : 4 * col + 4, :] = raw[2 * row + row_par, 2 * col + col_par].astype(F32)
+                    start = (2 * row_par + col_par) * BLOCK + row * CHUNK
+                    x[pl.ds(pl.multiple_of(start, CHUNK), CHUNK), :] = (move[...] * mask).astype(BF16)
+
+        loop(SIDE, plane_rows)
+        for p in range(4):
+            x[(p + 1) * BLOCK - CHUNK : (p + 1) * BLOCK, :] = jnp.zeros((CHUNK, x.shape[1]), BF16)
+
+    @token("norms")
+    def _():
+        await_bytes(norms.at[pl.ds(0, 7)], nb_sem.at[1])
+        await_bytes(norms.at[pl.ds(0, 7)], nb_sem.at[0])
+
+        def narrow_row(at):
+            pieces = [norms[2 * k, at : at + 1, :] + norms[2 * k + 1, at : at + 1, :] for k in range(4)]
+            return vec.put(jnp.concatenate(pieces, axis=1))
+
+        def wide_rows(at):
+            return [
+                vec.put(
+                    jnp.concatenate(
+                        [norms[2 * j + k // 2, at + k % 2 : at + k % 2 + 1, :] for k in range(4)], axis=1
+                    )
+                )
+                for j in range(4)
+            ]
+
+        params["in_a"] = ([narrow_row(0)], [narrow_row(10)])
+        params["mid_a"] = ([narrow_row(1)], [narrow_row(11)])
+        params["out_a"] = (wide_rows(2), wide_rows(12))
+        params["proj_a"] = (wide_rows(4), wide_rows(14))
+        params["in_b"] = ([narrow_row(6)], [narrow_row(16)])
+        params["mid_b"] = ([narrow_row(7)], [narrow_row(17)])
+        params["out_b"] = (wide_rows(8), wide_rows(18))
+        lanes = lax.broadcasted_iota(jnp.int32, (1, LANES), 1)
+        state["chan_a"] = vec.put(jnp.where(lanes < widths[0], 1.0, 0.0).astype(F32))
+        state["chan_b"] = vec.put(jnp.where(lanes < widths[1], 1.0, 0.0).astype(F32))
+
+    def wide_of(ref, start, size=CHUNK):
+        return jnp.concatenate([ref[pl.ds(start, size), :]] * 4, axis=1)
+
+    def mask_at(start):
+        return wide_of(mask_ref, start)
+
+    def gate_at(start):
+        return wide_of(gate_ref, start)
+
+    def set_norm(name, block, first_row, inverse, chan):
+        inverse = vec.get(state[inverse])
+        average = totals.row(first_row) * inverse
+        rstd = lax.rsqrt(totals.row(first_row + 1) * inverse - average * average + EPSILON)
+        gain, shift = (vec.get(rows[block]) for rows in params[name])
+        keep_lanes = 1.0 if chan is None else vec.get(state[chan])
+        by = gain * rstd
+        scales[name, block] = dict(
+            rstd=vec.put(rstd),
+            off=vec.put(-average * rstd),
+            by=vec.put(by),
+            mul=vec.put(by * keep_lanes),
+            add=vec.put((shift - average * by) * keep_lanes),
+        )
+
+    def normed(name, block, values):
+        s = scales[name, block]
+        return values * vec.get(s["mul"]) + vec.get(s["add"])
+
+    def hat(name, block, values):
+        s = scales[name, block]
+        return values * vec.get(s["rstd"]) + vec.get(s["off"])
+
+    def set_back(name, block, shift_row, gain_row):
+        s = scales[name, block]
+        inverse = vec.get(state["inv_in" if name == "in_a" else "inv_out"])
+        by = vec.get(s["by"])
+        pull = by * totals.row(gain_row) * inverse
+        s["back_add"] = vec.put(by * totals.row(shift_row) * inverse + pull * vec.get(s["off"]))
+        s["back_mul"] = vec.put(pull * vec.get(s["rstd"]))
+
+    def back(name, block, grad, values):
+        s = scales[name, block]
+        return grad * vec.get(s["by"]) - vec.get(s["back_add"]) - values * vec.get(s["back_mul"])
+
+    def square_terms(ref):
+        def terms(start):
+            values = ref[pl.ds(start, CHUNK), :]
+            return values, values * values
+
+        return terms
+
+    def masked_terms(ref):
+        def terms(start):
+            values = ref[pl.ds(start, CHUNK), :]
+            kept = values * mask_at(start)
+            return kept, kept * values
+
+        return terms
+
+    def lane_row(at, lane):
+        return vec_ref[at : at + 1, at_block(lane, 128)]
+
+    def add_up(out, count, left, right, product=mm):
+        out[...] = product(left(0), right(0))
+
+        def more(k):
+            out[...] += product(left(k + 1), right(k + 1))
+
+        loop(count - 1, more)
+
+    @token("A1s")
+    def _():
+        def first_a(p):
+            c1[at_block(p, BLOCK), :] = mm(x[at_block(p, BLOCK), :], w_in_a[...])
+
+        loop(4, first_a)
+        side = [sides[i] for i in range(4)]
+        count_in = sum(s * s for s in side).astype(F32)
+        count_out = sum((s // 2) * (s // 2) for s in side).astype(F32)
+        at = lax.broadcasted_iota(jnp.int32, (8, 128), 0)
+        counts = jnp.where(at == 0, count_in, jnp.where(at == 1, count_out, 0.0))
+        totals.start(column_sums(32, 2, square_terms(c1)), counts)
+
+    @token("A1e")
+    def _():
+        totals.end()
+        state["inv_in"] = vec.put(1.0 / totals.wide(8))
+        state["inv_out"] = vec.put(1.0 / totals.wide(9))
+        set_norm("in_a", 0, 0, "inv_in", "chan_a")
+        s = scales["in_a", 0]
+
+        def act_a(lane):
+            for row_par in range(2):
+                for col_par in range(2):
+                    p = 2 * row_par + col_par
+                    values = c1[p * BLOCK : (p + 1) * BLOCK, at_block(lane, 128)]
+                    scaled = values * lane_row(s["mul"], lane) + lane_row(s["add"], lane)
+                    act = scaled * jax.nn.sigmoid(scaled) * mask_ref[...]
+                    for t, (u, v) in enumerate(TAPS):
+                        if (u != 1) != bool(row_par) or (v != 1) != bool(col_par):
+                            continue
+                        shift = (32 if u == 0 else 0) + (4 if v == 0 else 0)
+                        moved = pltpu.roll(act, shift, 0) if shift else act
+                        cols_a[:, pl.ds(pl.multiple_of(t * LANES + lane * 128, 128), 128)] = moved.astype(BF16)
+
+        loop(4, act_a)
+
+    def conv_mid(out, cols, weight):
+        def at(k):
+            return pl.ds(pl.multiple_of(k * 1536, 512), 1536)
+
+        add_up(out, 3, lambda k: cols[:, at(k)], lambda k: weight[at(k), :])
+
+    def act_mid(act_ref, ref, name):
+        def step(index):
+            start = pl.multiple_of(index * CHUNK, CHUNK)
+            scaled = normed(name, 0, ref[pl.ds(start, CHUNK), :])
+            act_ref[pl.ds(start, CHUNK), :] = (scaled * jax.nn.sigmoid(scaled) * mask_at(start)).astype(BF16)
+
+        loop(BLOCK // CHUNK, step)
+
+    @token("A2s")
+    def _():
+        conv_mid(c2, cols_a, w_mid_a)
+        totals.start(column_sums(8, 2, masked_terms(c2)))
+
+    @token("A2e")
+    def _():
+        totals.end()
+        set_norm("mid_a", 0, 0, "inv_out", "chan_a")
+        act_mid(a2, c2, "mid_a")
+
+    @token("proj")
+    def _():
+        def project(j):
+            cp[at_block(j, BLOCK), :] = mm(x[0:BLOCK, :], w_proj_a[:, at_block(j, LANES)])
+
+        loop(4, project)
+
+    def blocked(ref, j):
+        return square_terms(ref.at[pl.ds(j * BLOCK, BLOCK)])
+
+    @token("A3s")
+    def _():
+        def expand_a(j):
+            c3[at_block(j, BLOCK), :] = mm(a2[...], w_out_a[:, at_block(j, LANES)])
+
+        loop(4, expand_a)
+        totals.start([row for ref in (c3, cp) for j in range(4) for row in column_sums(8, 2, blocked(ref, j))])
+
+    @token("A3e")
+    def _():
+        totals.end()
+        for j in range(4):
+            set_norm("out_a", j, 2 * j, "inv_out", None)
+            set_norm("proj_a", j, 8 + 2 * j, "inv_out", None)
+        for j in range(4):
+
+            def join_a(index, j=j):
+                start = pl.multiple_of(index * CHUNK, CHUNK)
+                rows = pl.ds(j * BLOCK + start, CHUNK)
+                pre = normed("out_a", j, c3[rows, :]) + normed("proj_a", j, cp[rows, :])
+                out = pre * jax.nn.sigmoid(pre) * mask_at(start)
+                bo[rows, :] = out
+                feed[pl.ds(start, CHUNK), pl.ds(j * LANES, LANES)] = out.astype(BF16)
+
+            loop(BLOCK // CHUNK, join_a)
+
+    @token("A4s")
+    def _():
+        add_up(d1, 4, lambda k: feed[:, at_block(k, LANES)], lambda k: w_in_b[at_block(k, LANES), :])
+        totals.start(column_sums(8, 2, square_terms(d1)))
+
+    @token("A4e")
+    def _():
+        totals.end()
+        set_norm("in_b", 0, 0, "inv_out", "chan_b")
+        s = scales["in_b", 0]
+
+        def act_b(lane):
+            scaled = d1[:, at_block(lane, 128)] * lane_row(s["mul"], lane) + lane_row(s["add"], lane)
+            act = scaled * jax.nn.sigmoid(scaled) * mask_ref[...]
+            for t, (u, v) in enumerate(TAPS):
+                shift = (-(32 * (u - 1) + 4 * (v - 1))) % BLOCK
+                moved = pltpu.roll(act, shift, 0) if shift else act
+                cols_b[:, pl.ds(pl.multiple_of(t * LANES + lane * 128, 128), 128)] = moved.astype(BF16)
+
+        loop(4, act_b)
+
+    @token("A5s")
+    def _():
+        conv_mid(d2, cols_b, w_mid_b)
+        totals.start(column_sums(8, 2, masked_terms(d2)))
+
+    @token("A5e")
+    def _():
+        totals.end()
+        set_norm("mid_b", 0, 0, "inv_out", "chan_b")
+        act_mid(b2, d2, "mid_b")
+
+    @token("A6s")
+    def _():
+        def expand_b(j):
+            d3[at_block(j, BLOCK), :] = mm(b2[...], w_out_b[:, at_block(j, LANES)])
+
+        loop(4, expand_b)
+        totals.start([row for j in range(4) for row in column_sums(8, 2, blocked(d3, j))])
+
+    @token("A6e")
+    def _():
+        totals.end()
+        for j in range(4):
+            set_norm("out_b", j, 2 * j, "inv_out", None)
+
+    @token("A7s")
+    def _():
+        for one in gathers.values():
+            one.sent()
+        cot_copy.wait()
+        values = []
+        for j in range(4):
+            lanes = pl.ds(j * LANES, LANES)
+
+            def finish(start, j=j, lanes=lanes):
+                rows = pl.ds(j * BLOCK + start, CHUNK)
+                row = start // CHUNK
+                for col in range(SIDE):
+                    move[4 * col : 4 * col + 4, 0:LANES] = cot[row, col, :, lanes].astype(F32)
+                mask, gate, hidden = mask_at(start), gate_at(start), d3[rows, :]
+                pre = bo[rows, :] + gate * normed("out_b", j, hidden)
+                part = jax.nn.sigmoid(pre)
+                grad = move[:, 0:LANES] * mask * (part * (1.0 + pre * (1.0 - part)))
+                move[:, LANES : 2 * LANES] = pre * part * mask
+                for col in range(SIDE):
+                    cot[row, col, :, lanes] = move[4 * col : 4 * col + 4, LANES : 2 * LANES].astype(BF16)
+                bo[rows, :] = grad
+                grad = grad * gate
+                return grad, grad * hat("out_b", j, hidden)
+
+            values += column_sums(SIDE, 2, finish)
+            bo[(j + 1) * BLOCK - CHUNK : (j + 1) * BLOCK, :] = jnp.zeros((CHUNK, LANES), F32)
+        result_copy.start()
+        totals.start(values)
+
+    def keep_sums(at):
+        rows = totals.rows
+        sums[at : at + rows, :] = tot[0:rows, :]
+
+    @token("A7e")
+    def _():
+        totals.end()
+        keep_sums(0)
+        for j in range(4):
+            set_back("out_b", j, 2 * j, 2 * j + 1)
+
+    def through_out(weight):
+        add_up(dz, 4, lambda k: dout[:, at_block(k, LANES)], lambda k: weight[:, at_block(k, LANES)], mm_nt)
+
+    def slope_terms(grad_ref, ref, name, chan):
+        def terms(start):
+            rows = pl.ds(start, CHUNK)
+            hidden = ref[rows, :]
+            mask = mask_at(pl.multiple_of(start % BLOCK, CHUNK) if grad_ref.shape[0] > BLOCK else start)
+            grad = grad_ref[rows, :] * mask * vec.get(state[chan]) * slope_of(normed(name, 0, hidden))
+            grad_ref[rows, :] = grad
+            return grad, grad * hat(name, 0, hidden)
+
+        return terms
+
+    @token("A8s")
+    def _():
+        for j in range(4):
+
+            def low_out_b(index, j=j):
+                start = pl.multiple_of(index * CHUNK, CHUNK)
+                rows = pl.ds(j * BLOCK + start, CHUNK)
+                grad = back("out_b", j, bo[rows, :] * gate_at(start), d3[rows, :]) * mask_at(start)
+                dout[pl.ds(start, CHUNK), pl.ds(j * LANES, LANES)] = grad.astype(BF16)
+
+            loop(BLOCK // CHUNK, low_out_b)
+        through_out(w_out_b)
+        totals.start(column_sums(8, 2, slope_terms(dz, d2, "mid_b", "chan_b")))
+
+    def grad_out(act_ref, j):
+        g_out[:, at_block(j, LANES)] = mm_tn(act_ref[...], dout[:, at_block(j, LANES)]).astype(BF16)
+
+    tokens("g.out_b", 2, 2, lambda j: grad_out(b2, j))
+
+    @token("A8e")
+    def _():
+        totals.end()
+        keep_sums(32)
+        set_back("mid_b", 0, 0, 1)
+
+    def low_mid(name, ref, shifts):
+        s = scales[name, 0]
+
+        def step(lane):
+            lanes = at_block(lane, 128)
+            grad = (
+                dz[:, lanes] * lane_row(s["by"], lane)
+                - lane_row(s["back_add"], lane)
+                - ref[:, lanes] * lane_row(s["back_mul"], lane)
+            ) * mask_ref[...]
+            dm[:, lanes] = grad.astype(BF16)
+            for k, shift in enumerate(shifts):
+                moved = pltpu.roll(grad, shift, 0) if shift else grad
+                g_mid[k * BLOCK : (k + 1) * BLOCK, lanes] = moved.astype(BF16)
+
+        loop(4, step)
+
+    @token("A9s")
+    def _():
+        low_mid("mid_b", d2, [(32 * (u - 1) + 4 * (v - 1)) % BLOCK for u, v in TAPS])
+        add_up(dz, 9, lambda t: g_mid[at_block(t, BLOCK), :], lambda t: w_mid_b[at_block(t, LANES), :], mm_nt)
+        totals.start(column_sums(8, 2, slope_terms(dz, d1, "in_b", "chan_b")))
+
+    def grad_mid(cols, t):
+        g_mid[at_block(t, LANES), :] = mm_tn(cols[:, at_block(t, LANES)], dm[...]).astype(BF16)
+
+    tokens("g.mid_b", 3, 3, lambda t: grad_mid(cols_b, t))
+
+    @token("A9e")
+    def _():
+        totals.end()
+        keep_sums(40)
+        set_back("in_b", 0, 0, 1)
+
+    @token("A10s")
+    def _():
+        def low_first_b(index):
+            start = pl.multiple_of(index * CHUNK, CHUNK)
+            rows = pl.ds(start, CHUNK)
+            df[rows, :] = (back("in_b", 0, dz[rows, :], d1[rows, :]) * mask_at(start)).astype(BF16)
+
+        loop(BLOCK // CHUNK, low_first_b)
+
+        def back_in_b(j):
+            bo[at_block(j, BLOCK), :] += mm_nt(df[...], w_in_b[at_block(j, LANES), :])
+
+        loop(4, back_in_b)
+        values = []
+        for j in range(4):
+
+            def join_back(start, j=j):
+                rows = pl.ds(j * BLOCK + start, CHUNK)
+                left, right = c3[rows, :], cp[rows, :]
+                pre = normed("out_a", j, left) + normed("proj_a", j, right)
+                grad = bo[rows, :] * mask_at(start) * slope_of(pre)
+                bo[rows, :] = grad
+                return grad, grad * hat("out_a", j, left), grad * hat("proj_a", j, right)
+
+            values += column_sums(8, 3, join_back)
+        totals.start(values)
+
+    def grad_in_b(j):
+        g_in[at_block(j, LANES), :] = mm_tn(feed[:, at_block(j, LANES)], df[...]).astype(BF16)
+
+    tokens("g.in_b", 2, 2, grad_in_b)
+
+    @token("A10e")
+    def _():
+        totals.end()
+        keep_sums(48)
+        for j in range(4):
+            set_back("out_a", j, 3 * j, 3 * j + 1)
+            set_back("proj_a", j, 3 * j, 3 * j + 2)
+
+    @token("A11s")
+    def _():
+        for j in range(4):
+
+            def low_both(index, j=j):
+                start = pl.multiple_of(index * CHUNK, CHUNK)
+                rows = pl.ds(j * BLOCK + start, CHUNK)
+                near_rows, lanes = pl.ds(start, CHUNK), pl.ds(j * LANES, LANES)
+                grad, mask = bo[rows, :], mask_at(start)
+                dout[near_rows, lanes] = (back("out_a", j, grad, c3[rows, :]) * mask).astype(BF16)
+                dproj[near_rows, lanes] = (back("proj_a", j, grad, cp[rows, :]) * mask).astype(BF16)
+
+            loop(BLOCK // CHUNK, low_both)
+        through_out(w_out_a)
+        totals.start(column_sums(8, 2, slope_terms(dz, c2, "mid_a", "chan_a")))
+
+    tokens("g.out_a", 2, 2, lambda j: grad_out(a2, j))
+
+    def grad_proj(n):
+        i, j = n // 4, n % 4
+        g_proj[at_block(i, LANES), at_block(j, LANES)] = mm_tn(
+            x[0:BLOCK, at_block(i, LANES)], dproj[:, at_block(j, LANES)]
+        ).astype(BF16)
+
+    tokens("g.proj_a", 2, 4, grad_proj)
+
+    def tell(at):
+        for bits in LINK_PEERS:
+            pl.semaphore_signal(free_sem.at[at], inc=1, device_id=place.peer(*bits), device_id_type=BY_MESH)
+
+    def told(at, name):
+        def go():
+            pl.semaphore_wait(free_sem.at[at], len(LINK_PEERS))
+            scatters[name, 0].zero()
+
+        todo["S0." + name] = go
+
+    def back_proj(n):
+        out, rows = d3.at[pl.ds(n * BLOCK, BLOCK)], pl.ds(n * LANES, LANES)
+        add_up(out, 4, lambda k: dproj[:, at_block(k, LANES)], lambda k: w_proj_a[rows, at_block(k, LANES)], mm_nt)
+
+    @token("dproj.0")
+    def _():
+        back_proj(0)
+
+    @token("dproj.1")
+    def _():
+        back_proj(1)
+        tell(0)
+
+    told(0, "proj_a")
+
+    @token("A11e")
+    def _():
+        totals.end()
+        keep_sums(96)
+        set_back("mid_a", 0, 0, 1)
+
+    @token("A12s")
+    def _():
+        low_mid("mid_a", c2, [(-(32 * r + 4 * s)) % BLOCK for r in range(2) for s in range(2)])
+        for row_par in range(2):
+            for col_par in range(2):
+                grad = None
+                for t, (u, v) in enumerate(TAPS):
+                    if (u != 1) != bool(row_par) or (v != 1) != bool(col_par):
+                        continue
+                    moved = 2 * (1 if u == 0 else 0) + (1 if v == 0 else 0)
+                    term = mm_nt(g_mid[moved * BLOCK : (moved + 1) * BLOCK, :], w_mid_a[t * LANES : (t + 1) * LANES, :])
+                    grad = term if grad is None else grad + term
+                bo[pl.ds((2 * row_par + col_par) * BLOCK, BLOCK), :] = grad
+        totals.start(column_sums(32, 2, slope_terms(bo, c1, "in_a", "chan_a")))
+
+    tokens("g.mid_a", 3, 3, lambda t: grad_mid(cols_a, t))
+
+    @token("A12e")
+    def _():
+        totals.end()
+        keep_sums(104)
+        set_back("in_a", 0, 0, 1)
+        for p in range(4):
+
+            def low_first_a(index, p=p):
+                start = pl.multiple_of(index * CHUNK, CHUNK)
+                rows = pl.ds(p * BLOCK + start, CHUNK)
+                grad = back("in_a", 0, bo[rows, :], c1[rows, :]) * mask_at(start)
+                cols_b[pl.ds(start, CHUNK), p * LANES : (p + 1) * LANES] = grad.astype(BF16)
+
+            loop(BLOCK // CHUNK, low_first_a)
+
+    def first_grad(p):
+        return cols_b[:, p * LANES : (p + 1) * LANES]
+
+    def grad_in_a(i):
+        lanes = at_block(i, 256)
+        total = mm_tn(x[0:BLOCK, lanes], first_grad(0))
+        for p in range(1, 4):
+            total = total + mm_tn(x[p * BLOCK : (p + 1) * BLOCK, lanes], first_grad(p))
+        g_in[at_block(i, 256), :] = total.astype(BF16)
+
+    tokens("g.in_a", 2, 2, grad_in_a)
+
+    def image_grad(planes):
+        for p in planes:
+            for h in range(2):
+                lanes = pl.ds(h * LANES, LANES)
+                grad = mm_nt(first_grad(p), w_in_a[h * LANES : (h + 1) * LANES, :])
+                dz[...] = grad + d3[h * BLOCK : (h + 1) * BLOCK, :] if p == 0 else grad
+
+                def pixels(row, p=p, lanes=lanes):
+                    move[:, 0:LANES] = dz[at_block(row, CHUNK), :]
+                    for col in range(SIDE):
+                        raw[2 * row + p // 2, 2 * col + p % 2, :, lanes] = move[4 * col : 4 * col + 4, 0:LANES].astype(BF16)
+
+                loop(SIDE, pixels)
+
+    @token("img.0")
+    def _():
+        image_grad((0, 1))
+
+    @token("img.1")
+    def _():
+        image_grad((2, 3))
+        grad_copy.start()
+        tell(1)
+
+    told(1, "in_a")
+
+    @token("own")
+    def _():
+        def own_row(at, out, k):
+            if out.shape[1] >= 128:
+                for lane in range(2):
+                    line = sums[pl.ds(at + 2 * (place.f % 2) + lane, 1), :]
+                    out[k : k + 1, lane * 128 : (lane + 1) * 128] = line
+            else:
+                odd = (place.f % 2).astype(F32)
+                move[0:1, 0:128] = sums[pl.ds(at + place.f // 2, 1), :]
+                line = move[0:8, 0:128]
+                line = line + (pltpu.roll(line, 64, 1) - line) * odd
+                out[k : k + 1, :] = line[0:1, 0 : out.shape[1]]
+
+        for name, at in (("mid_b", 32), ("in_b", 40), ("mid_a", 96), ("in_a", 104)):
+            own_row(at + 4, owned[name], 0)
+            own_row(at, owned[name], 1)
+        block = place.f // 2
+        for name, at, step, gain in (("out_b", 0, 8, 4), ("out_a", 48, 12, 4), ("proj_a", 48, 12, 8)):
+            own_row(at + step * block + gain, owned[name], 0)
+            own_row(at + step * block, owned[name], 1)
+        for one in own_copies:
+            one.start()
+
+    steps = sorted(todo)
+    if sorted(RUN) != list(range(len(steps))):
+        raise ValueError(len(steps))
+    for index in RUN:
+        todo[steps[index]]()
+    result_copy.wait()
+    grad_copy.wait()
+    for one in scatters.values():
+        one.sent()
+    for one in own_copies + out_copies:
+        one.wait()
+
+
+def finish_kernel(*refs):
+    arrays_in, arrays_out, held, wide = refs[:16], refs[16:32], refs[32:48], refs[48:55]
+    in_sem, out_sem = refs[55:]
+    loads = [pltpu.make_async_copy(a, b, in_sem.at[i]) for i, (a, b) in enumerate(zip(arrays_in, held))]
+    leaving = held[:9] + wide
+    stores = [pltpu.make_async_copy(a, b, out_sem.at[i]) for i, (a, b) in enumerate(zip(leaving, arrays_out))]
+    order = list(range(9, 16)) + list(range(9))
+    for i in order:
+        loads[i].start()
+    for i in order:
+        loads[i].wait()
+        if i >= 9:
+            narrow, target = held[i], wide[i - 9]
+            rows, columns = narrow.shape
+            chunk = chunk_of(rows, columns)
+
+            def step(index, carry, narrow=narrow, target=target, chunk=chunk):
+                at = pl.ds(pl.multiple_of(index * chunk, 16), chunk)
+                target[at, :] = narrow[at, :].astype(F32)
+                return carry
+
+            lax.fori_loop(0, rows // chunk, step, 0)
+        stores[i].start()
+    for i in order:
+        stores[i].wait()
+
+
+def finish_call(plain, grads):
+    anywhere = pl.BlockSpec(memory_space=pl.ANY)
+    return pl.pallas_call(
+        finish_kernel,
+        out_shape=[jax.ShapeDtypeStruct(one.shape, one.dtype) for one in plain]
+        + [jax.ShapeDtypeStruct(one.shape, F32) for one in grads],
+        in_specs=[anywhere] * 16,
+        out_specs=[anywhere] * 16,
+        scratch_shapes=[pltpu.VMEM(one.shape, one.dtype) for one in (*plain, *grads)]
+        + [pltpu.VMEM(one.shape, F32) for one in grads]
+        + [pltpu.SemaphoreType.DMA((16,)), pltpu.SemaphoreType.DMA((16,))],
+        compiler_params=pltpu.CompilerParams(vmem_limit_bytes=64 * 2**20),
+        name="finish_step",
+    )(*plain, *grads)
+
+
+def body_fast(
+    images,
+    image_sides,
+    widths,
+    keep_gate,
+    w_in_a,
+    w_mid_a,
+    w_out_a,
+    w_proj_a,
+    norm_in_a,
+    norm_mid_a,
+    norm_out_a,
+    norm_proj_a,
+    w_in_b,
+    w_mid_b,
+    w_out_b,
+    norm_in_b,
+    norm_mid_b,
+    norm_out_b,
+    cotangent,
+):
+    width_in, width_out = images.shape[3], cotangent.shape[3]
+    turned = (1, 2, 0, 3)
+    images, cotangent = images.transpose(turned), cotangent.transpose(turned)
+    norms = (norm_in_a, norm_mid_a, norm_out_a, norm_proj_a, norm_in_b, norm_mid_b, norm_out_b)
+    shards = (w_in_a, w_mid_a, w_out_a, w_proj_a, w_in_b, w_mid_b, w_out_b)
+    vmem = pl.BlockSpec(memory_space=pltpu.VMEM)
+    smem = pl.BlockSpec(memory_space=pltpu.SMEM)
+    anywhere = pl.BlockSpec(memory_space=pl.ANY)
+    wholes = [(8 * one.shape[0], one.shape[1]) for one in shards]
+    pieces = sum(len(one) for one in PIECES.values())
+    outs = pl.pallas_call(
+        step_kernel,
+        out_shape=[jax.ShapeDtypeStruct(cotangent.shape, BF16), jax.ShapeDtypeStruct(images.shape, BF16)]
+        + [jax.ShapeDtypeStruct(one.shape, F32) for one in norms]
+        + [jax.ShapeDtypeStruct(one.shape, BF16) for one in shards],
+        in_specs=[anywhere, anywhere, smem, smem, smem] + [vmem] * 7 + [anywhere] * 7,
+        out_specs=[anywhere] * 16,
+        scratch_shapes=[pltpu.VMEM(one.shape, F32) for one in norms]
+        + [pltpu.VMEM(one.shape, BF16) for one in shards]
+        + [pltpu.VMEM(shape, BF16) for shape in wholes]
+        + [
+            pltpu.VMEM(images.shape, BF16),
+            pltpu.VMEM(cotangent.shape, BF16),
+            pltpu.VMEM((4 * BLOCK, width_in), BF16),
+            pltpu.VMEM((4 * BLOCK, LANES), F32),
+            pltpu.VMEM((BLOCK, 9 * LANES), BF16),
+            pltpu.VMEM((BLOCK, LANES), F32),
+            pltpu.VMEM((BLOCK, LANES), BF16),
+            pltpu.VMEM((4 * BLOCK, LANES), F32),
+            pltpu.VMEM((4 * BLOCK, LANES), F32),
+            pltpu.VMEM((4 * BLOCK, LANES), F32),
+            pltpu.VMEM((BLOCK, width_out), BF16),
+            pltpu.VMEM((BLOCK, LANES), F32),
+            pltpu.VMEM((BLOCK, 9 * LANES), BF16),
+            pltpu.VMEM((BLOCK, LANES), F32),
+            pltpu.VMEM((BLOCK, LANES), BF16),
+            pltpu.VMEM((4 * BLOCK, LANES), F32),
+            pltpu.VMEM((BLOCK, LANES), F32),
+            pltpu.VMEM((BLOCK, LANES), BF16),
+            pltpu.VMEM((BLOCK, LANES), BF16),
+            pltpu.VMEM((BLOCK, width_out), BF16),
+            pltpu.VMEM((BLOCK, width_out), BF16),
+            pltpu.VMEM(wholes[1], BF16),
+            pltpu.VMEM(wholes[2], BF16),
+            pltpu.VMEM(wholes[4], BF16),
+            pltpu.VMEM(wholes[3], BF16),
+            pltpu.VMEM((BLOCK, 128), F32),
+            pltpu.VMEM((BLOCK, 128), F32),
+            pltpu.VMEM((CHUNK, width_in), F32),
+            pltpu.VMEM((8, 24, 128), F32),
+            pltpu.VMEM((24, 128), F32),
+            pltpu.VMEM((160, LANES), F32),
+            pltpu.VMEM((2, 18, 16, 128), F32),
+            pltpu.VMEM((2, 10, 64, 128), F32),
+            pltpu.VMEM((64, 128), F32),
+            pltpu.VMEM((112, 128), F32),
+            pltpu.SemaphoreType.DMA((4,)),
+            pltpu.SemaphoreType.DMA((pieces,)),
+            pltpu.SemaphoreType.DMA((pieces, 8)),
+            pltpu.SemaphoreType.DMA((7, 2)),
+            pltpu.SemaphoreType.DMA((2, 2, 3)),
+            pltpu.SemaphoreType.DMA((2, 2, 3)),
+            pltpu.SemaphoreType.DMA((2,)),
+            pltpu.SemaphoreType.DMA((2, 7)),
+            pltpu.SemaphoreType.REGULAR((2,)),
+        ],
+        compiler_params=pltpu.CompilerParams(
+            collective_id=0, has_side_effects=True, vmem_limit_bytes=64 * 2**20
+        ),
+        name="whole_step",
+    )(images, cotangent, image_sides, keep_gate, widths, *norms, *shards)
+    back_turned = (2, 0, 1, 3)
+    outs = finish_call(outs[:9], outs[9:])
+    own, finals = outs[2:9], outs[9:]
+    return (
+        outs[0].transpose(back_turned),
+        outs[1].transpose(back_turned),
+        *finals[:4],
+        *own[:4],
+        *finals[4:],
+        *own[4:],
+    )
+
+
+def fits(mesh):
+    return mesh.shape["fsdp"] == 8 and mesh.shape["dp"] == 4
+
+
+def gather_plain(shards):
+    return [lax.all_gather(one, "fsdp", axis=0, tiled=True) for one in shards]
+
+
+def scatter_plain(grads):
+    parts = [lax.psum_scatter(one, "fsdp", scatter_dimension=0, tiled=True) for one in grads]
+    return lax.psum(tuple(parts), "dp")
+
+
+def sum_pair(first, second):
+    return lax.psum((first, second), ("fsdp", "dp"))
 
 
 def silu_slope(values):
@@ -32,15 +1516,11 @@
 
 
 def norm_stats(hidden, pixel_mask, local_counts, count_slot):
-    sum_values, sum_squares, totals = lax.psum(
-        (
-            jnp.sum(hidden * pixel_mask, axis=(0, 1, 2)),
-            jnp.sum(hidden * hidden * pixel_mask, axis=(0, 1, 2)),
-            local_counts,
-        ),
-        ("fsdp", "dp"),
-    )
-    pixel_total = totals[count_slot]
+    sum_values, sum_squares = sum_pair(
+        jnp.sum(hidden * pixel_mask, axis=(0, 1, 2)),
+        jnp.sum(hidden * hidden * pixel_mask, axis=(0, 1, 2)),
+    )
+    pixel_total = local_counts[count_slot]
     average = sum_values / pixel_total
     inv_std = lax.rsqrt(sum_squares / pixel_total - average * average + EPSILON)
     return (average, inv_std, pixel_total)
@@ -55,9 +1535,8 @@
 
 def norm_backward(grad_norm, scaled, stats_now, params, pixel_mask):
     average, inv_std, pixel_total = stats_now
-    shift_sum, gain_sum = lax.psum(
-        (jnp.sum(grad_norm, axis=(0, 1, 2)), jnp.sum(grad_norm * scaled, axis=(0, 1, 2))),
-        ("fsdp", "dp"),
+    shift_sum, gain_sum = sum_pair(
+        jnp.sum(grad_norm, axis=(0, 1, 2)), jnp.sum(grad_norm * scaled, axis=(0, 1, 2))
     )
     gain_row = params[0].astype(jnp.float32)
     grad_hidden = (
@@ -376,83 +1855,38 @@
     channel_b = (lane_ids < widths[1]).astype(jnp.float32)
     depth_gate = keep_gate.astype(jnp.float32)[:, None, None, None]
     inputs = images * mask_in.astype(jnp.bfloat16)
-    weights_a = (
-        lax.all_gather(w_in_a, "fsdp", axis=0, tiled=True),
-        lax.all_gather(w_mid_a, "fsdp", axis=0, tiled=True),
-        lax.all_gather(w_out_a, "fsdp", axis=0, tiled=True),
-        lax.all_gather(w_proj_a, "fsdp", axis=0, tiled=True),
-        lax.all_gather(norm_in_a, "fsdp", axis=1, tiled=True),
-        lax.all_gather(norm_mid_a, "fsdp", axis=1, tiled=True),
-        lax.all_gather(norm_out_a, "fsdp", axis=1, tiled=True),
-        lax.all_gather(norm_proj_a, "fsdp", axis=1, tiled=True),
-    )
-    block_out, stats_a, unused_a = block_a_forward(
-        inputs, weights_a, mask_in, mask_out, local_counts, channel_a, None
-    )
-    weights_b = (
-        lax.all_gather(w_in_b, "fsdp", axis=0, tiled=True),
-        lax.all_gather(w_mid_b, "fsdp", axis=0, tiled=True),
-        lax.all_gather(w_out_b, "fsdp", axis=0, tiled=True),
-        lax.all_gather(norm_in_b, "fsdp", axis=1, tiled=True),
-        lax.all_gather(norm_mid_b, "fsdp", axis=1, tiled=True),
-        lax.all_gather(norm_out_b, "fsdp", axis=1, tiled=True),
-    )
-    result, stats_b, unused_b = block_b_forward(
-        block_out, weights_b, mask_out, local_counts, channel_b, depth_gate, None
-    )
-    backward_b = (
-        lax.all_gather(w_in_b, "fsdp", axis=0, tiled=True),
-        lax.all_gather(w_mid_b, "fsdp", axis=0, tiled=True),
-        lax.all_gather(w_out_b, "fsdp", axis=0, tiled=True),
-        lax.all_gather(norm_in_b, "fsdp", axis=1, tiled=True),
-        lax.all_gather(norm_mid_b, "fsdp", axis=1, tiled=True),
-        lax.all_gather(norm_out_b, "fsdp", axis=1, tiled=True),
-    )
-    redone_b = block_b_forward(
-        block_out, backward_b, mask_out, local_counts, channel_b, depth_gate, stats_b
-    )[2]
+    total_counts = lax.psum(local_counts, ("fsdp", "dp"))
+    gathered = gather_plain((w_in_a, w_mid_a, w_out_a, w_proj_a, w_in_b, w_mid_b, w_out_b))
+    norms = lax.all_gather(
+        jnp.concatenate(
+            [norm_in_a, norm_mid_a, norm_out_a, norm_proj_a, norm_in_b, norm_mid_b, norm_out_b], axis=1
+        ),
+        "fsdp",
+        axis=0,
+    )
+    wide = []
+    place = 0
+    for one in (norm_in_a, norm_mid_a, norm_out_a, norm_proj_a, norm_in_b, norm_mid_b, norm_out_b):
+        width = one.shape[1]
+        wide.append(norms[:, :, place : place + width].transpose(1, 0, 2).reshape(2, -1))
+        place += width
+    weights_a = tuple(gathered[:4]) + tuple(wide[:4])
+    weights_b = tuple(gathered[4:]) + tuple(wide[4:])
+    block_out, stats_a, redone_a = block_a_forward(
+        inputs, weights_a, mask_in, mask_out, total_counts, channel_a, None
+    )
+    result, stats_b, redone_b = block_b_forward(
+        block_out, weights_b, mask_out, total_counts, channel_b, depth_gate, None
+    )
     grad_block, grads_b, norms_b = block_b_backward(
-        cotangent.astype(jnp.float32),
-        backward_b,
-        stats_b,
-        redone_b,
-        mask_out,
-        channel_b,
-        depth_gate,
-    )
-    backward_a = (
-        lax.all_gather(w_in_a, "fsdp", axis=0, tiled=True),
-        lax.all_gather(w_mid_a, "fsdp", axis=0, tiled=True),
-        lax.all_gather(w_out_a, "fsdp", axis=0, tiled=True),
-        lax.all_gather(w_proj_a, "fsdp", axis=0, tiled=True),
-        lax.all_gather(norm_in_a, "fsdp", axis=1, tiled=True),
-        lax.all_gather(norm_mid_a, "fsdp", axis=1, tiled=True),
-        lax.all_gather(norm_out_a, "fsdp", axis=1, tiled=True),
-        lax.all_gather(norm_proj_a, "fsdp", axis=1, tiled=True),
-    )
-    redone_a = block_a_forward(
-        inputs, backward_a, mask_in, mask_out, local_counts, channel_a, stats_a
-    )[2]
+        cotangent.astype(jnp.float32), weights_b, stats_b, redone_b, mask_out, channel_b, depth_gate
+    )
     grad_inputs, grads_a, norms_a = block_a_backward(
-        grad_block, inputs, backward_a, stats_a, redone_a, mask_in, mask_out, channel_a
-    )
-    part_in_a, part_mid_a, part_out_a, part_proj_a, part_in_b, part_mid_b, part_out_b = (
-        lax.psum_scatter(grads_a[0], "fsdp", scatter_dimension=0, tiled=True),
-        lax.psum_scatter(grads_a[1], "fsdp", scatter_dimension=0, tiled=True),
-        lax.psum_scatter(grads_a[2], "fsdp", scatter_dimension=0, tiled=True),
-        lax.psum_scatter(grads_a[3], "fsdp", scatter_dimension=0, tiled=True),
-        lax.psum_scatter(grads_b[0], "fsdp", scatter_dimension=0, tiled=True),
-        lax.psum_scatter(grads_b[1], "fsdp", scatter_dimension=0, tiled=True),
-        lax.psum_scatter(grads_b[2], "fsdp", scatter_dimension=0, tiled=True),
-    )
+        grad_block, inputs, weights_a, stats_a, redone_a, mask_in, mask_out, channel_a
+    )
+    finals = scatter_plain(tuple(one.astype(jnp.bfloat16) for one in grads_a + grads_b))
     final_in_a, final_mid_a, final_out_a, final_proj_a, final_in_b, final_mid_b, final_out_b = (
-        lax.psum(part_in_a.astype(jnp.bfloat16), "dp").astype(jnp.float32),
-        lax.psum(part_mid_a.astype(jnp.bfloat16), "dp").astype(jnp.float32),
-        lax.psum(part_out_a.astype(jnp.bfloat16), "dp").astype(jnp.float32),
-        lax.psum(part_proj_a.astype(jnp.bfloat16), "dp").astype(jnp.float32),
-        lax.psum(part_in_b.astype(jnp.bfloat16), "dp").astype(jnp.float32),
-        lax.psum(part_mid_b.astype(jnp.bfloat16), "dp").astype(jnp.float32),
-        lax.psum(part_out_b.astype(jnp.bfloat16), "dp").astype(jnp.float32),
+        one.astype(jnp.float32) for one in finals
     )
     return (
         result.astype(jnp.bfloat16),
@@ -514,4 +1948,5 @@
         P(None, "fsdp"),
         P(None, "fsdp"),
     )
-    return jax.shard_map(body, mesh=mesh, in_specs=in_specs, out_specs=out_specs, check_vma=False)
+    step = body_fast if fits(mesh) else body
+    return jax.shard_map(step, mesh=mesh, in_specs=in_specs, out_specs=out_specs, check_vma=False)

time: 1710 us -> 252 us (0.15)
  waiting for transfers between devices: 846 us -> 0 us
  blocking collectives: 609 us -> 0 us
  Pallas kernels: 0 us -> 251 us
  matrix products: 84.6 us -> 0 us
  other arithmetic: 72 us -> 0 us
  local copies, waits for them, and re-layouts: 65.7 us -> 0 us
    reduce_scatter x7 -> x0, waiting for transfers between devices: 749 us -> none  [the longest x1 164 us: body(): lax.psum_scatter(grads_a[1], 'fsdp', scatter_dimension=0, tiled=True)]
    psum x12 -> x0, blocking collectives: 508 us -> none  [the longest x6 267 us: norm_stats(): lax.psum((jnp.sum(hidden * pixel_mask, axis=(0, 1, 2)), jnp.sum(hidden *...]
    pallas_call x0 -> x2, Pallas kernels: none -> 251 us  [the longest x1 246 us: body_fast(): pl.pallas_call(step_kernel, out_shape=[jax.ShapeDtypeStruct(cotangent.sha...]
    all_gather x7 -> x0, blocking collectives: 101 us -> none  [the longest x1 17.9 us: body(): lax.all_gather(norm_out_a, 'fsdp', axis=1, tiled=True)]
    dot_general x21 -> x0, matrix products: 84.6 us -> none  [the longest x7 32.3 us: contract(): lax.dot_general(left_side, right_side, (((0, 1, 2), (0, 1, 2)), ((), ()))...]
    psum x1 -> x0, waiting for transfers between devices: 53.7 us -> none  [body(): lax.psum(part_in_a.astype(jnp.bfloat16), 'dp').astype(jnp.float32)]
    convert_element_type x38 -> x0, other arithmetic: 39.9 us -> none  [the longest x6 14 us: norm_backward(): return (grad_hidden.astype(jnp.bfloat16), gain_sum, shift_sum)]
    all_gather x7 -> x0, waiting for transfers between devices: 38.6 us -> none  [the longest x1 28 us: body(): lax.all_gather(w_mid_b, 'fsdp', axis=0, tiled=True)]
  transfers between devices with their start and end apart: 15 -> 0, of which waited for: 11 -> 0; matrix products, arithmetic and copies ran while one was open for 8% -> 0% of each run, Pallas kernels for 0% -> 0%
where the time goes in v3:
time: 252 us
  Pallas kernels  251 us (100%)
    pallas_call x1, Pallas kernels, body_fast(): pl.pallas_call(step_kernel, out_shape=[jax.ShapeDtypeStruct(cotangent.sha...  246 us

profile of v3, /device:TPU:1, one launch (start us, length us, event | category | flops | bytes accessed | tf_op | source)
XLA Modules:
  0.0 251.9 jit_solution(15834618834898248544)
XLA Ops:
  0.7 246.2 %whole_step.1 = (bf16[7,7,4,2048]{3,2,1,0:T(4,128)(2,1)}, bf16[14,14,4,1024]{3,2,1,0:T(4,128)(2,1)}, f32[2,64]{1,0:T(2,128)}, f32[2,64]{1,0:T(2,128)}, f32[2,256...) custom-call(bf16[14,14,4,1024]{3,2,1,0:T(4,128)(2,1)} %bitcast.4, ...), custom_call_target="tpu_custom_call" | custom-call | tf_op jit(solution)/shard_map/whole_step/pallas_call | solution.py:1402
  246.9 4.9 %finish_step.1 = (bf16[7,7,4,2048]{3,2,1,0:T(4,128)(2,1)}, bf16[14,14,4,1024]{3,2,1,0:T(4,128)(2,1)}, f32[2,64]{1,0:T(2,128)}, f32[2,64]{1,0:T(2,128)}, f32[2,25...) custom-call(bf16[7,7,4,2048]{3,2,1,0:T(4,128)(2,1)} %get-tuple-eleme, ...), custom_call_target="tpu_custom_call" | custom-call | tf_op jit(solution)/shard_map/finish_step/pallas_call | solution.py:1357

commit v4 on v3

--- a/solution.py
+++ b/solution.py
@@ -9,6 +9,7 @@
 
 EPSILON = 1e-05
 BY_MESH = pl.DeviceIdType.MESH
+FSDP, DP = "fsdp", "dp"
 F32 = jnp.float32
 BF16 = jnp.bfloat16
 NAMES = ("in_a", "mid_a", "out_a", "proj_a", "in_b", "mid_b", "out_b")
@@ -16,34 +17,44 @@
 LANES = 512
 CHUNK = 32
 SIDE = 7
+ZYX, ZXY, YZX = range(3)
 TAPS = [(u, v) for u in range(3) for v in range(3)]
 LINK_PEERS = ((1, 0), (2, 0), (4, 0), (6, 0), (0, 2), (0, 1))
 CHIP_PEERS = tuple((a, b) for a in (7, 6, 5, 4, 3, 2, 1, 0) for b in (2, 0) if a or b)
-PIECES = {
-    "in_a": [(0, 128, 4, 4)],
-    "mid_a": [(0, 96, 4, 4), (96, 96, 4, 4), (192, 96, 4, 4), (288, 96, 4, 4), (384, 96, 4, 4), (480, 96, 8, 4)],
-    "out_a": [(0, 32, 6, 5), (32, 32, 4, 5)],
-    "proj_a": [(0, 64, 6, 5), (64, 64, 4, 5)],
-    "in_b": [(0, 128, 4, 4), (128, 128, 4, 4)],
-    "mid_b": [(0, 96, 4, 4), (96, 96, 4, 4), (192, 96, 4, 4), (288, 96, 4, 4), (384, 96, 4, 4), (480, 96, 8, 4)],
-    "out_b": [(0, 32, 6, 5), (32, 32, 4, 5)],
+WAYS_IN = {
+    "in_a": ((0, 64, ((ZYX, 4), (ZXY, 4))), (64, 64, ((YZX, 4), (ZXY, 4)))),
+    "mid_a": ((0, 192, ((ZYX, 4), (ZXY, 4))), (192, 192, ((YZX, 4), (ZXY, 4))), (384, 192, ((ZYX, 4), (ZXY, 4)))),
+    "out_a": ((0, 32, ((ZYX, 2), (ZXY, 4), (YZX, 2))), (32, 32, ((ZYX, 2), (ZXY, 4), (YZX, 2)))),
+    "proj_a": ((0, 64, ((ZYX, 2), (ZXY, 4), (YZX, 2))), (64, 64, ((ZYX, 2), (ZXY, 4), (YZX, 2)))),
+    "in_b": ((0, 256, ((ZYX, 4), (ZXY, 4))),),
+    "mid_b": ((0, 96, ((ZYX, 4), (ZXY, 4))), (96, 96, ((YZX, 4), (ZXY, 4))), (192, 96, ((ZYX, 4), (ZXY, 4))), (288, 96, ((YZX, 4), (ZXY, 4))), (384, 96, ((ZYX, 4), (ZXY, 4))), (480, 96, ((YZX, 4), (ZXY, 4)))),
+    "out_b": ((0, 32, ((ZYX, 2), (ZXY, 4), (YZX, 2))), (32, 32, ((ZYX, 2), (ZXY, 4), (YZX, 2)))),
+}
+WAYS_OUT = {
+    "in_a": ((0, 64, 4), (64, 64, 4)),
+    "mid_a": ((0, 96, 4), (96, 96, 4), (192, 96, 4), (288, 96, 4), (384, 96, 4), (480, 96, 4)),
+    "out_a": ((0, 32, 5), (32, 32, 5)),
+    "proj_a": ((0, 32, 5), (32, 32, 5), (64, 32, 5), (96, 32, 5)),
+    "in_b": ((0, 128, 4), (128, 128, 4)),
+    "mid_b": ((0, 96, 4), (96, 96, 4), (192, 96, 4), (288, 96, 4), (384, 96, 4), (480, 96, 4)),
+    "out_b": ((0, 32, 5), (32, 32, 5)),
 }
 RUN = [
-    253, 297, 300, 301, 295, 272, 273, 302, 276, 277, 278, 303, 279, 48, 304, 280, 51, 305, 281, 52, 316, 292,
-    53, 69, 54, 72, 55, 317, 73, 56, 74, 293, 90, 312, 75, 93, 67, 244, 15, 94, 14, 13, 313, 95, 298, 76, 77,
-    68, 96, 299, 288, 306, 63, 307, 88, 97, 98, 12, 289, 64, 308, 309, 246, 19, 18, 17, 89, 310, 274, 84, 311,
-    109, 275, 49, 314, 85, 50, 315, 110, 282, 16, 57, 105, 283, 58, 250, 296, 70, 106, 284, 59, 71, 248, 23,
-    22, 78, 285, 79, 60, 91, 286, 61, 92, 80, 287, 21, 62, 99, 245, 290, 100, 65, 81, 291, 20, 27, 101, 26,
-    25, 82, 83, 66, 86, 102, 103, 104, 24, 87, 247, 31, 107, 30, 29, 108, 249, 28, 35, 34, 33, 32, 39, 38, 37,
-    36, 43, 266, 267, 42, 41, 40, 47, 116, 261, 46, 45, 262, 263, 135, 136, 44, 3, 114, 256, 2, 156, 257, 157,
-    127, 1, 128, 129, 130, 131, 132, 177, 178, 148, 0, 7, 112, 251, 6, 5, 149, 150, 252, 119, 120, 151, 268,
-    152, 269, 198, 199, 153, 117, 169, 264, 265, 170, 4, 11, 219, 115, 258, 10, 9, 140, 137, 138, 141, 133,
-    220, 134, 171, 172, 190, 191, 259, 173, 260, 174, 240, 241, 161, 8, 113, 254, 255, 270, 158, 121, 122,
-    123, 124, 125, 126, 271, 111, 294, 162, 159, 118, 154, 179, 155, 192, 193, 211, 212, 194, 195, 232, 182,
-    233, 142, 143, 144, 145, 146, 147, 183, 180, 139, 200, 213, 214, 175, 215, 234, 216, 235, 236, 203, 237,
-    176, 204, 224, 163, 225, 201, 164, 221, 165, 242, 166, 167, 222, 168, 196, 243, 160, 197, 184, 217, 185,
-    238, 218, 186, 205, 239, 187, 206, 226, 188, 207, 227, 189, 208, 228, 181, 209, 229, 210, 230, 231, 202,
-    223,
+    262, 303, 282, 304, 306, 283, 301, 285, 48, 49, 307, 308, 319, 320, 299, 286, 66, 67, 51, 287, 52, 298,
+    85, 315, 294, 84, 253, 69, 316, 53, 295, 15, 14, 64, 71, 65, 70, 60, 61, 305, 13, 89, 284, 281, 87, 88,
+    82, 83, 12, 255, 309, 19, 18, 310, 288, 79, 311, 100, 312, 78, 313, 291, 289, 290, 101, 50, 97, 314, 17,
+    292, 54, 259, 96, 302, 16, 257, 55, 23, 317, 22, 293, 68, 58, 73, 21, 57, 56, 296, 72, 86, 59, 318, 91,
+    76, 20, 254, 75, 27, 297, 74, 26, 77, 25, 62, 93, 94, 63, 90, 92, 95, 24, 80, 256, 31, 81, 30, 29, 98, 99,
+    28, 258, 35, 34, 33, 32, 39, 38, 37, 36, 43, 275, 42, 41, 276, 107, 127, 128, 40, 47, 270, 271, 46, 272,
+    105, 151, 152, 45, 119, 120, 44, 175, 3, 176, 143, 2, 121, 122, 265, 144, 266, 1, 123, 145, 200, 199, 124,
+    146, 103, 167, 0, 111, 147, 168, 7, 169, 273, 274, 6, 260, 148, 106, 170, 112, 277, 125, 171, 5, 135, 126,
+    261, 278, 172, 191, 136, 108, 4, 193, 11, 149, 10, 9, 159, 129, 194, 267, 223, 268, 150, 269, 160, 104,
+    173, 130, 153, 113, 174, 183, 114, 218, 247, 8, 300, 154, 131, 192, 177, 137, 196, 263, 115, 138, 132,
+    178, 264, 155, 279, 161, 198, 116, 139, 162, 280, 117, 156, 102, 220, 197, 118, 179, 207, 163, 109, 222,
+    140, 180, 186, 184, 110, 244, 246, 202, 216, 141, 221, 142, 195, 201, 240, 185, 133, 203, 134, 217, 226,
+    204, 209, 165, 225, 210, 166, 187, 227, 157, 224, 164, 158, 215, 189, 219, 190, 181, 188, 208, 249, 233,
+    211, 234, 228, 182, 232, 239, 213, 245, 214, 205, 212, 206, 248, 229, 235, 242, 237, 252, 250, 241, 251,
+    231, 238, 236, 243, 230,
 ]
 
 
@@ -57,8 +68,8 @@
 
 class Place:
     def __init__(self):
-        self.f = lax.axis_index("fsdp")
-        self.d = lax.axis_index("dp")
+        self.f = lax.axis_index(FSDP)
+        self.d = lax.axis_index(DP)
         self.y = self.f % 2
         self.z = self.f // 2
         self.c = self.d % 2
@@ -111,91 +122,92 @@
 
 
 class Gather:
-    def __init__(self, place, shard, whole, start, rows, wide_a, send, recv):
+    def __init__(self, place, shard, whole, start, rows, groups, send, recv):
         self.place, self.shard, self.whole = place, shard, whole
-        self.start, self.rows, self.wide_a = start, rows, wide_a
-        self.local, self.send, self.recv = recv.at[6], send, recv
+        self.start, self.rows, self.send, self.recv = start, rows, send, recv
         self.total, columns = shard.shape
-        self.half = columns // 2
-        self.wide_b = self.half - wide_a
-        self.part = rows // 2
-        self.col_0 = place.c * self.half
-        self.row_q = start + place.x * self.part
-        self.row_o = start + self.part - place.x * self.part
-        self.near_count = self.part * wide_a + rows * self.wide_b + 3 * self.part * self.half
+        self.half = half = columns // 2
+        self.part = part = rows // 2
+        self.col_0 = place.c * half
+        self.row_q = start + place.x * part
+        self.row_o = start + part - place.x * part
+        self.arriving, self.leaving = [0] * 4, 0
+        self.groups, at = {}, 0
+        for way, eighths in groups:
+            self.groups[way] = (at, half * eighths // 8)
+            at += half * eighths // 8
 
     def view(self, bits, row, rows, from_col, columns):
         block = flip(self.place.f, bits) * self.total
         return self.whole.at[rows_of(block + row, rows), cols_of(self.col_0 + from_col, columns)]
 
-    def pass_on(self, bits, row, rows, from_col, columns, leg, device):
+    def pass_on(self, bits, row, rows, group, leg, peer):
+        from_col, columns = group
         view = self.view(bits, row, rows, from_col, columns)
-        push(view, view, self.send, self.recv.at[leg], device)
+        push(view, view, self.send, self.recv.at[leg], self.place.peer(*peer))
+        self.arriving[leg] += rows * columns
+        self.leaving += rows * columns
+
+    def pass_own(self, row, rows, group, leg, peer):
+        from_col, columns = group
+        source = self.shard.at[rows_of(row, rows), cols_of(self.col_0 + from_col, columns)]
+        push(source, self.view(0, row, rows, from_col, columns), self.send, self.recv.at[leg], self.place.peer(*peer))
+        self.arriving[leg] += rows * columns
+        self.leaving += rows * columns
+
+    def arrive(self, leg):
+        await_count(self.whole, self.arriving[leg], self.recv.at[leg])
 
     def first(self):
-        half, part, place = self.half, self.part, self.place
         pltpu.make_async_copy(
-            self.shard.at[pl.ds(self.start, self.rows), cols_of(self.col_0, half)],
-            self.view(0, self.start, self.rows, 0, half),
-            self.local,
+            self.shard.at[pl.ds(self.start, self.rows), cols_of(self.col_0, self.half)],
+            self.view(0, self.start, self.rows, 0, self.half),
+            self.recv.at[0],
         ).start()
+        self.arriving[0] += self.rows * self.half
         for bits in (6, 4, 2):
-            push(
-                self.shard.at[rows_of(self.row_q, part), cols_of(self.col_0, half)],
-                self.view(0, self.row_q, part, 0, half),
-                self.send,
-                self.recv.at[0],
-                place.peer(bits, 0),
-            )
+            self.pass_own(self.row_q, self.part, (0, self.half), 0, (bits, 0))
 
     def own(self):
-        place = self.place
-        for row, rows, col, columns in (
-            (self.row_q, self.part, 0, self.wide_a),
-            (self.start, self.rows, self.wide_a, self.wide_b),
-        ):
-            if columns:
-                push(
-                    self.shard.at[rows_of(row, rows), cols_of(self.col_0 + col, columns)],
-                    self.view(0, row, rows, col, columns),
-                    self.send,
-                    self.recv.at[1],
-                    place.peer(1, 0),
-                )
+        for way, group in self.groups.items():
+            if way == ZXY:
+                self.pass_own(self.start, self.rows, group, 0, (1, 0))
+            else:
+                self.pass_own(self.row_q, self.part, group, 0, (1, 0))
 
     def one(self):
-        place = self.place
-        await_count(self.whole, self.rows * self.half, self.local)
-        await_count(self.whole, 3 * self.part * self.half, self.recv.at[0])
-        for bits in (2, 4, 6):
-            self.pass_on(bits, self.row_q, self.part, 0, self.half, 1, place.peer(1, 0))
-            self.pass_on(bits, self.row_q, self.part, 0, self.half, 2, place.peer(0, 2))
+        self.arrive(0)
+        if YZX in self.groups:
+            for bits in (6, 4, 2):
+                self.pass_on(1, self.row_q, self.part, self.groups[YZX], 1, (bits, 0))
+        for way, group in self.groups.items():
+            for bits in (2, 4, 6):
+                if way != YZX:
+                    self.pass_on(bits, self.row_q, self.part, group, 1, (1, 0))
+                self.pass_on(bits, self.row_q, self.part, group, 1, (0, 2))
+            if way == YZX:
+                self.pass_on(1, self.row_q, self.part, group, 1, (0, 2))
 
     def two(self):
-        place = self.place
-        await_count(self.whole, self.near_count, self.recv.at[1])
-        await_count(self.whole, 3 * self.part * self.half, self.recv.at[2])
-        if self.wide_a:
-            for bits in (1, 3, 5, 7):
-                self.pass_on(bits, self.row_q, self.part, 0, self.wide_a, 3, place.peer(0, 2))
-        if self.wide_b:
-            for bits in (2, 4, 6):
-                self.pass_on(bits, self.row_o, self.part, self.wide_a, self.wide_b, 4, place.peer(1, 0))
+        self.arrive(1)
+        for way, group in self.groups.items():
+            if way == ZXY:
+                for bits in (2, 4, 6):
+                    self.pass_on(bits, self.row_o, self.part, group, 2, (1, 0))
+            else:
+                for bits in (1, 3, 5, 7) if way == ZYX else (3, 5, 7):
+                    self.pass_on(bits, self.row_q, self.part, group, 2, (0, 2))
 
     def three(self):
-        place = self.place
-        await_count(self.whole, 4 * self.part * self.wide_a, self.recv.at[3])
-        await_count(self.whole, 3 * self.part * self.wide_b, self.recv.at[4])
+        self.arrive(2)
         for bits in range(8):
-            self.pass_on(bits, self.start, self.rows, 0, self.half, 5, place.peer(0, 1))
+            self.pass_on(bits, self.start, self.rows, (0, self.half), 3, (0, 1))
 
     def four(self):
-        await_count(self.whole, 8 * self.rows * self.half, self.recv.at[5])
+        self.arrive(3)
 
     def sent(self):
-        count = 6 * self.part * self.half + self.near_count + 8 * self.rows * self.half
-        count += 4 * self.part * self.wide_a + 3 * self.part * self.wide_b
-        await_count(self.whole, count, self.send)
+        await_count(self.whole, self.leaving, self.send)
 
 
 def chunk_of(rows, columns):
@@ -246,7 +258,7 @@
         self.row_o = start + part - place.x * part
 
     def push(self, source, target, leg, device):
-        push(source, target, self.send, self.recv.at[leg - 1], device)
+        push(source, target, self.send, self.recv.at[leg], device)
 
     def zero(self):
         other = self.half - self.col_0
@@ -277,7 +289,7 @@
                 self.push(
                     self.core(block * total + self.row_o, part, 0, self.wide_a),
                     self.a_x.at[pl.ds(block * part, part)],
-                    1,
+                    0,
                     place.peer(0, 2),
                 )
         if self.wide_b:
@@ -285,14 +297,14 @@
                 self.push(
                     self.core((2 * level + 1 - place.y) * total + self.start, rows, self.wide_a, self.wide_b),
                     self.b_y.at[pl.ds(level * rows, rows)],
-                    2,
+                    0,
                     place.peer(1, 0),
                 )
 
     def two(self):
         place, total, part, rows = self.place, self.total, self.part, self.rows
+        await_count(self.room, 4 * rows * self.half, self.recv.at[0])
         if self.wide_a:
-            await_bytes(self.a_x, self.recv.at[0])
             add_blocks(
                 8,
                 part,
@@ -304,11 +316,10 @@
                 self.push(
                     self.core((2 * level + 1 - place.y) * total + self.row_q, part, 0, self.wide_a),
                     self.a_y.at[pl.ds(level * part, part)],
-                    3,
+                    1,
                     place.peer(1, 0),
                 )
         if self.wide_b:
-            await_bytes(self.b_y, self.recv.at[1])
             add_blocks(
                 4,
                 rows,
@@ -320,7 +331,7 @@
                 self.push(
                     self.core(flip(place.f, bits) * total + self.start, rows, self.wide_a, self.wide_b),
                     self.b_z.at[pl.ds(slot * rows, rows)],
-                    4,
+                    1,
                     place.peer(bits, 0),
                 )
 
@@ -339,8 +350,8 @@
 
     def three(self):
         place, total, part, rows = self.place, self.total, self.part, self.rows
+        await_count(self.room, 2 * rows * self.wide_a + 3 * rows * self.wide_b, self.recv.at[1])
         if self.wide_a:
-            await_bytes(self.a_y, self.recv.at[2])
             add_blocks(
                 4,
                 part,
@@ -352,29 +363,27 @@
                 self.push(
                     self.core(flip(place.f, bits) * total + self.row_q, part, 0, self.wide_a),
                     self.a_z.at[pl.ds(slot * part, part)],
-                    5,
+                    2,
                     place.peer(bits, 0),
                 )
         if self.wide_b:
-            await_bytes(self.b_z, self.recv.at[3])
 
             def keep(start, chunk, value):
                 self.mine(self.start + start, chunk, self.wide_a, self.wide_b)[...] = value
 
             self.sum_four(self.start, rows, self.wide_a, self.wide_b, self.b_z, keep)
-            self.push(self.mine(self.row_o, part, self.wide_a, self.wide_b), self.b_x, 6, place.peer(0, 2))
+            self.push(self.mine(self.row_o, part, self.wide_a, self.wide_b), self.b_x, 2, place.peer(0, 2))
 
     def four(self):
         place, part = self.place, self.part
+        await_count(self.room, 3 * part * self.wide_a + part * self.wide_b, self.recv.at[2])
         if self.wide_a:
-            await_bytes(self.a_z, self.recv.at[4])
 
             def keep(start, chunk, value):
                 self.out[rows_of(self.row_q + start, chunk), cols_of(self.col_0, self.wide_a)] = value
 
             self.sum_four(self.row_q, part, 0, self.wide_a, self.a_z, keep)
         if self.wide_b:
-            await_bytes(self.b_x, self.recv.at[5])
             chunk = chunk_of(part, self.wide_b)
 
             def step(index, carry):
@@ -387,15 +396,15 @@
 
             lax.fori_loop(0, part // chunk, step, 0)
         block = self.out.at[rows_of(self.row_q, part), cols_of(self.col_0, self.half)]
-        self.push(block, block, 7, place.peer(0, 2))
+        self.push(block, block, 3, place.peer(0, 2))
 
     def five(self):
-        await_bytes(self.out.at[pl.ds(0, self.part), pl.ds(0, self.half)], self.recv.at[6])
+        await_bytes(self.out.at[pl.ds(0, self.part), pl.ds(0, self.half)], self.recv.at[3])
         block = self.out.at[pl.ds(self.start, self.rows), cols_of(self.col_0, self.half)]
-        self.push(block, block, 8, self.place.peer(0, 1))
+        self.push(block, block, 4, self.place.peer(0, 1))
 
     def six(self):
-        await_bytes(self.out.at[pl.ds(0, self.rows), pl.ds(0, self.half)], self.recv.at[7])
+        await_bytes(self.out.at[pl.ds(0, self.rows), pl.ds(0, self.half)], self.recv.at[4])
 
     def sent(self):
         await_count(self.room, 18 * self.part * self.half, self.send)
@@ -422,6 +431,8 @@
 
 
 def at_block(index, size):
+    if isinstance(index, int):
+        return pl.ds(index * size, size)
     return pl.ds(pl.multiple_of(index * size, size), size)
 
 
@@ -663,8 +674,8 @@
         for part in range(count):
             todo[f"{name}.{part}"] = functools.partial(loop, each, lambda k, first=part * each: step(first + k))
 
-    gathers, scatters, at = {}, {}, 0
-    left = {name: len(PIECES[name]) for name in NAMES}
+    gathers, scatters, at, going = {}, {}, 0, 0
+    left = {name: len(WAYS_OUT[name]) for name in NAMES}
 
     def finish_piece(name, piece):
         piece.six()
@@ -672,29 +683,38 @@
         if not left[name]:
             out_copies[NAMES.index(name)].start()
 
+    def tell(name):
+        for bits in LINK_PEERS:
+            sem = free_sem.at[NAMES.index(name)]
+            pl.semaphore_signal(sem, inc=1, device_id=place.peer(*bits), device_id_type=BY_MESH)
+
+    def send_core(name):
+        pl.semaphore_wait(free_sem.at[NAMES.index(name)], len(LINK_PEERS))
+        scatters[name, 0].zero()
+
     for name in NAMES:
-        eighth = shards[name].shape[1] // 16
-        for n, (start, rows, way_in, way_out) in enumerate(PIECES[name]):
+        for n, (start, rows, ways) in enumerate(WAYS_IN[name]):
             sems = link_send.at[at], link_recv.at[at]
-            g = Gather(place, shards[name], wholes[name], start, rows, way_in * eighth, *sems)
-            first_sem = core_sem.at[NAMES.index(name)]
-            s = Scatter(
-                place, grads[name], wholes[name], outs[name], start, rows, way_out * eighth, first_sem, *sems
-            )
-            gathers[name, n], scatters[name, n] = g, s
+            g = gathers[name, n] = Gather(place, shards[name], wholes[name], start, rows, ways, *sems)
             at += 1
             key = f"{name}.{n}"
             todo["z." + key], todo["o." + key], todo["L1." + key] = g.first, g.own, g.one
             todo["L2." + key], todo["L3." + key] = g.two, g.three
-            if n == 0:
-                todo["S0." + name] = s.zero
-            todo["S1." + key] = functools.partial(s.one, n == 0, n == len(PIECES[name]) - 1)
+        eighth = shards[name].shape[1] // 16
+        for n, (start, rows, wide) in enumerate(WAYS_OUT[name]):
+            sems = core_sem.at[NAMES.index(name)], link_send.at[going], link_recv.at[going]
+            s = Scatter(place, grads[name], wholes[name], outs[name], start, rows, wide * eighth, *sems)
+            scatters[name, n] = s
+            going += 1
+            key = f"{name}.{n}"
+            todo["S1." + key] = functools.partial(s.one, n == 0, n == len(WAYS_OUT[name]) - 1)
             todo["S2." + key], todo["S3." + key], todo["S4." + key] = s.two, s.three, s.four
             todo["S5." + key] = s.five
             todo["S6." + key] = functools.partial(finish_piece, name, s)
+        todo["S0." + name] = functools.partial(send_core, name)
 
         def arrived(name=name):
-            for n in range(len(PIECES[name])):
+            for n in range(len(WAYS_IN[name])):
                 gathers[name, n].four()
 
         todo["W." + name] = arrived
@@ -855,19 +875,15 @@
         return vec_ref[at : at + 1, at_block(lane, 128)]
 
     def add_up(out, count, left, right, product=mm):
-        out[...] = product(left(0), right(0))
-
-        def more(k):
-            out[...] += product(left(k + 1), right(k + 1))
-
-        loop(count - 1, more)
+        total = product(left(0), right(0))
+        for k in range(1, count):
+            total = total + product(left(k), right(k))
+        out[...] = total
 
     @token("A1s")
     def _():
-        def first_a(p):
+        for p in range(4):
             c1[at_block(p, BLOCK), :] = mm(x[at_block(p, BLOCK), :], w_in_a[...])
-
-        loop(4, first_a)
         side = [sides[i] for i in range(4)]
         count_in = sum(s * s for s in side).astype(F32)
         count_out = sum((s // 2) * (s // 2) for s in side).astype(F32)
@@ -900,10 +916,7 @@
         loop(4, act_a)
 
     def conv_mid(out, cols, weight):
-        def at(k):
-            return pl.ds(pl.multiple_of(k * 1536, 512), 1536)
-
-        add_up(out, 3, lambda k: cols[:, at(k)], lambda k: weight[at(k), :])
+        add_up(out, 3, lambda k: cols[:, at_block(k, 1536)], lambda k: weight[at_block(k, 1536), :])
 
     def act_mid(act_ref, ref, name):
         def step(index):
@@ -936,10 +949,8 @@
 
     @token("A3s")
     def _():
-        def expand_a(j):
+        for j in range(4):
             c3[at_block(j, BLOCK), :] = mm(a2[...], w_out_a[:, at_block(j, LANES)])
-
-        loop(4, expand_a)
         totals.start([row for ref in (c3, cp) for j in range(4) for row in column_sums(8, 2, blocked(ref, j))])
 
     @token("A3e")
@@ -994,10 +1005,8 @@
 
     @token("A6s")
     def _():
-        def expand_b(j):
+        for j in range(4):
             d3[at_block(j, BLOCK), :] = mm(b2[...], w_out_b[:, at_block(j, LANES)])
-
-        loop(4, expand_b)
         totals.start([row for j in range(4) for row in column_sums(8, 2, blocked(d3, j))])
 
     @token("A6e")
@@ -1073,6 +1082,7 @@
 
             loop(BLOCK // CHUNK, low_out_b)
         through_out(w_out_b)
+        tell("out_b")
         totals.start(column_sums(8, 2, slope_terms(dz, d2, "mid_b", "chan_b")))
 
     def grad_out(act_ref, j):
@@ -1107,6 +1117,7 @@
     def _():
         low_mid("mid_b", d2, [(32 * (u - 1) + 4 * (v - 1)) % BLOCK for u, v in TAPS])
         add_up(dz, 9, lambda t: g_mid[at_block(t, BLOCK), :], lambda t: w_mid_b[at_block(t, LANES), :], mm_nt)
+        tell("mid_b")
         totals.start(column_sums(8, 2, slope_terms(dz, d1, "in_b", "chan_b")))
 
     def grad_mid(cols, t):
@@ -1129,10 +1140,9 @@
 
         loop(BLOCK // CHUNK, low_first_b)
 
-        def back_in_b(j):
+        for j in range(4):
             bo[at_block(j, BLOCK), :] += mm_nt(df[...], w_in_b[at_block(j, LANES), :])
-
-        loop(4, back_in_b)
+        tell("in_b")
         values = []
         for j in range(4):
 
@@ -1174,6 +1184,7 @@
 
             loop(BLOCK // CHUNK, low_both)
         through_out(w_out_a)
+        tell("out_a")
         totals.start(column_sums(8, 2, slope_terms(dz, c2, "mid_a", "chan_a")))
 
     tokens("g.out_a", 2, 2, lambda j: grad_out(a2, j))
@@ -1186,17 +1197,6 @@
 
     tokens("g.proj_a", 2, 4, grad_proj)
 
-    def tell(at):
-        for bits in LINK_PEERS:
-            pl.semaphore_signal(free_sem.at[at], inc=1, device_id=place.peer(*bits), device_id_type=BY_MESH)
-
-    def told(at, name):
-        def go():
-            pl.semaphore_wait(free_sem.at[at], len(LINK_PEERS))
-            scatters[name, 0].zero()
-
-        todo["S0." + name] = go
-
     def back_proj(n):
         out, rows = d3.at[pl.ds(n * BLOCK, BLOCK)], pl.ds(n * LANES, LANES)
         add_up(out, 4, lambda k: dproj[:, at_block(k, LANES)], lambda k: w_proj_a[rows, at_block(k, LANES)], mm_nt)
@@ -1208,9 +1208,7 @@
     @token("dproj.1")
     def _():
         back_proj(1)
-        tell(0)
-
-    told(0, "proj_a")
+        tell("proj_a")
 
     @token("A11e")
     def _():
@@ -1231,6 +1229,7 @@
                     term = mm_nt(g_mid[moved * BLOCK : (moved + 1) * BLOCK, :], w_mid_a[t * LANES : (t + 1) * LANES, :])
                     grad = term if grad is None else grad + term
                 bo[pl.ds((2 * row_par + col_par) * BLOCK, BLOCK), :] = grad
+        tell("mid_a")
         totals.start(column_sums(32, 2, slope_terms(bo, c1, "in_a", "chan_a")))
 
     tokens("g.mid_a", 3, 3, lambda t: grad_mid(cols_a, t))
@@ -1284,9 +1283,7 @@
     def _():
         image_grad((2, 3))
         grad_copy.start()
-        tell(1)
-
-    told(1, "in_a")
+        tell("in_a")
 
     @token("own")
     def _():
@@ -1398,7 +1395,7 @@
     smem = pl.BlockSpec(memory_space=pltpu.SMEM)
     anywhere = pl.BlockSpec(memory_space=pl.ANY)
     wholes = [(8 * one.shape[0], one.shape[1]) for one in shards]
-    pieces = sum(len(one) for one in PIECES.values())
+    pieces = max(sum(len(one) for one in ways.values()) for ways in (WAYS_IN, WAYS_OUT))
     outs = pl.pallas_call(
         step_kernel,
         out_shape=[jax.ShapeDtypeStruct(cotangent.shape, BF16), jax.ShapeDtypeStruct(images.shape, BF16)]
@@ -1447,13 +1444,13 @@
             pltpu.VMEM((112, 128), F32),
             pltpu.SemaphoreType.DMA((4,)),
             pltpu.SemaphoreType.DMA((pieces,)),
-            pltpu.SemaphoreType.DMA((pieces, 8)),
+            pltpu.SemaphoreType.DMA((pieces, 5)),
             pltpu.SemaphoreType.DMA((7, 2)),
             pltpu.SemaphoreType.DMA((2, 2, 3)),
             pltpu.SemaphoreType.DMA((2, 2, 3)),
             pltpu.SemaphoreType.DMA((2,)),
             pltpu.SemaphoreType.DMA((2, 7)),
-            pltpu.SemaphoreType.REGULAR((2,)),
+            pltpu.SemaphoreType.REGULAR((7,)),
         ],
         compiler_params=pltpu.CompilerParams(
             collective_id=0, has_side_effects=True, vmem_limit_bytes=64 * 2**20
@@ -1474,20 +1471,20 @@
 
 
 def fits(mesh):
-    return mesh.shape["fsdp"] == 8 and mesh.shape["dp"] == 4
+    return mesh.shape[FSDP] == 8 and mesh.shape[DP] == 4
 
 
 def gather_plain(shards):
-    return [lax.all_gather(one, "fsdp", axis=0, tiled=True) for one in shards]
+    return [lax.all_gather(one, FSDP, axis=0, tiled=True) for one in shards]
 
 
 def scatter_plain(grads):
-    parts = [lax.psum_scatter(one, "fsdp", scatter_dimension=0, tiled=True) for one in grads]
-    return lax.psum(tuple(parts), "dp")
+    parts = [lax.psum_scatter(one, FSDP, scatter_dimension=0, tiled=True) for one in grads]
+    return lax.psum(tuple(parts), DP)
 
 
 def sum_pair(first, second):
-    return lax.psum((first, second), ("fsdp", "dp"))
+    return lax.psum((first, second), (FSDP, DP))
 
 
 def silu_slope(values):
@@ -1641,8 +1638,8 @@
 
 def own_shard(pair_sums):
     gain_sum, shift_sum = pair_sums
-    shard_width = gain_sum.shape[0] // lax.axis_size("fsdp")
-    offset = lax.axis_index("fsdp") * shard_width
+    shard_width = gain_sum.shape[0] // lax.axis_size(FSDP)
+    offset = lax.axis_index(FSDP) * shard_width
     return jnp.stack(
         [
             lax.dynamic_slice_in_dim(gain_sum, offset, shard_width, 0),
@@ -1855,13 +1852,13 @@
     channel_b = (lane_ids < widths[1]).astype(jnp.float32)
     depth_gate = keep_gate.astype(jnp.float32)[:, None, None, None]
     inputs = images * mask_in.astype(jnp.bfloat16)
-    total_counts = lax.psum(local_counts, ("fsdp", "dp"))
+    total_counts = lax.psum(local_counts, (FSDP, DP))
     gathered = gather_plain((w_in_a, w_mid_a, w_out_a, w_proj_a, w_in_b, w_mid_b, w_out_b))
     norms = lax.all_gather(
         jnp.concatenate(
             [norm_in_a, norm_mid_a, norm_out_a, norm_proj_a, norm_in_b, norm_mid_b, norm_out_b], axis=1
         ),
-        "fsdp",
+        FSDP,
         axis=0,
     )
     wide = []
@@ -1910,43 +1907,43 @@
 
 def solution(mesh):
     in_specs = (
-        P(("fsdp", "dp"), None, None, None),
-        P(("fsdp", "dp")),
+        P((FSDP, DP), None, None, None),
+        P((FSDP, DP)),
         P(),
-        P(("fsdp", "dp")),
-        P("fsdp", None),
-        P("fsdp", None),
-        P("fsdp", None),
-        P("fsdp", None),
-        P(None, "fsdp"),
-        P(None, "fsdp"),
-        P(None, "fsdp"),
-        P(None, "fsdp"),
-        P("fsdp", None),
-        P("fsdp", None),
-        P("fsdp", None),
-        P(None, "fsdp"),
-        P(None, "fsdp"),
-        P(None, "fsdp"),
-        P(("fsdp", "dp"), None, None, None),
+        P((FSDP, DP)),
+        P(FSDP, None),
+        P(FSDP, None),
+        P(FSDP, None),
+        P(FSDP, None),
+        P(None, FSDP),
+        P(None, FSDP),
+        P(None, FSDP),
+        P(None, FSDP),
+        P(FSDP, None),
+        P(FSDP, None),
+        P(FSDP, None),
+        P(None, FSDP),
+        P(None, FSDP),
+        P(None, FSDP),
+        P((FSDP, DP), None, None, None),
     )
     out_specs = (
-        P(("fsdp", "dp"), None, None, None),
-        P(("fsdp", "dp"), None, None, None),
-        P("fsdp", None),
-        P("fsdp", None),
-        P("fsdp", None),
-        P("fsdp", None),
-        P(None, "fsdp"),
-        P(None, "fsdp"),
-        P(None, "fsdp"),
-        P(None, "fsdp"),
-        P("fsdp", None),
-        P("fsdp", None),
-        P("fsdp", None),
-        P(None, "fsdp"),
-        P(None, "fsdp"),
-        P(None, "fsdp"),
+        P((FSDP, DP), None, None, None),
+        P((FSDP, DP), None, None, None),
+        P(FSDP, None),
+        P(FSDP, None),
+        P(FSDP, None),
+        P(FSDP, None),
+        P(None, FSDP),
+        P(None, FSDP),
+        P(None, FSDP),
+        P(None, FSDP),
+        P(FSDP, None),
+        P(FSDP, None),
+        P(FSDP, None),
+        P(None, FSDP),
+        P(None, FSDP),
+        P(None, FSDP),
     )
     step = body_fast if fits(mesh) else body
     return jax.shard_map(step, mesh=mesh, in_specs=in_specs, out_specs=out_specs, check_vma=False)

time: 252 us -> 236 us (0.937)
  Pallas kernels: 251 us -> 235 us
    pallas_call x1, Pallas kernels: 246 us -> 230 us  [body_fast(): pl.pallas_call(step_kernel, out_shape=[jax.ShapeDtypeStruct(cotangent.sha...]
where the time goes in v4:
time: 236 us
  Pallas kernels  235 us (100%)
    pallas_call x1, Pallas kernels, body_fast(): pl.pallas_call(step_kernel, out_shape=[jax.ShapeDtypeStruct(cotangent.sha...  230 us
    pallas_call x1, Pallas kernels, finish_call(): pl.pallas_call(finish_kernel, out_shape=[jax.ShapeDtypeStruct(one.shape,...  4.89 us

profile of v4, /device:TPU:1, one launch (start us, length us, event | category | flops | bytes accessed | tf_op | source)
XLA Modules:
  0.0 235.9 jit_solution(17285828962454459437)
XLA Ops:
  0.7 230.1 %whole_step.1 = (bf16[7,7,4,2048]{3,2,1,0:T(4,128)(2,1)}, bf16[14,14,4,1024]{3,2,1,0:T(4,128)(2,1)}, f32[2,64]{1,0:T(2,128)}, f32[2,64]{1,0:T(2,128)}, f32[2,256...) custom-call(bf16[14,14,4,1024]{3,2,1,0:T(4,128)(2,1)} %bitcast.4, ...), custom_call_target="tpu_custom_call" | custom-call | tf_op jit(solution)/shard_map/whole_step/pallas_call | solution.py:1399
  230.8 4.9 %finish_step.1 = (bf16[7,7,4,2048]{3,2,1,0:T(4,128)(2,1)}, bf16[14,14,4,1024]{3,2,1,0:T(4,128)(2,1)}, f32[2,64]{1,0:T(2,128)}, f32[2,64]{1,0:T(2,128)}, f32[2,25...) custom-call(bf16[7,7,4,2048]{3,2,1,0:T(4,128)(2,1)} %get-tuple-eleme, ...), custom_call_target="tpu_custom_call" | custom-call | tf_op jit(solution)/shard_map/finish_step/pallas_call | solution.py:1354

commit v5 on v4

--- a/solution.py
+++ b/solution.py
@@ -18,17 +18,18 @@
 CHUNK = 32
 SIDE = 7
 ZYX, ZXY, YZX = range(3)
+SHORT_SETS = 4
 TAPS = [(u, v) for u in range(3) for v in range(3)]
 LINK_PEERS = ((1, 0), (2, 0), (4, 0), (6, 0), (0, 2), (0, 1))
 CHIP_PEERS = tuple((a, b) for a in (7, 6, 5, 4, 3, 2, 1, 0) for b in (2, 0) if a or b)
 WAYS_IN = {
-    "in_a": ((0, 64, ((ZYX, 4), (ZXY, 4))), (64, 64, ((YZX, 4), (ZXY, 4)))),
-    "mid_a": ((0, 192, ((ZYX, 4), (ZXY, 4))), (192, 192, ((YZX, 4), (ZXY, 4))), (384, 192, ((ZYX, 4), (ZXY, 4)))),
-    "out_a": ((0, 32, ((ZYX, 2), (ZXY, 4), (YZX, 2))), (32, 32, ((ZYX, 2), (ZXY, 4), (YZX, 2)))),
-    "proj_a": ((0, 64, ((ZYX, 2), (ZXY, 4), (YZX, 2))), (64, 64, ((ZYX, 2), (ZXY, 4), (YZX, 2)))),
-    "in_b": ((0, 256, ((ZYX, 4), (ZXY, 4))),),
-    "mid_b": ((0, 96, ((ZYX, 4), (ZXY, 4))), (96, 96, ((YZX, 4), (ZXY, 4))), (192, 96, ((ZYX, 4), (ZXY, 4))), (288, 96, ((YZX, 4), (ZXY, 4))), (384, 96, ((ZYX, 4), (ZXY, 4))), (480, 96, ((YZX, 4), (ZXY, 4)))),
-    "out_b": ((0, 32, ((ZYX, 2), (ZXY, 4), (YZX, 2))), (32, 32, ((ZYX, 2), (ZXY, 4), (YZX, 2)))),
+    "in_a": ((0, 64, 0, ((YZX, 4), (ZXY, 4))), (64, 64, 0, ((YZX, 4), (ZXY, 4)))),
+    "mid_a": ((0, 96, 0, ((YZX, 4), (ZXY, 4))), (96, 96, 0, ((YZX, 4), (ZXY, 4))), (192, 96, 0, ((ZYX, 4), (ZXY, 4))), (288, 96, 0, ((YZX, 4), (ZXY, 4))), (384, 96, 0, ((YZX, 4), (ZXY, 4))), (480, 96, 0, ((ZYX, 4), (ZXY, 4)))),
+    "out_a": ((0, 32, 0, ((ZXY, 5), (YZX, 3))), (32, 32, 0, ((ZXY, 5), (YZX, 3)))),
+    "proj_a": ((0, 64, 0, ((ZXY, 5), (YZX, 3))), (64, 64, 0, ((ZXY, 5), (YZX, 3)))),
+    "in_b": ((0, 64, 0, ((YZX, 4), (ZXY, 4))), (64, 64, 0, ((YZX, 4), (ZXY, 4))), (128, 64, 0, ((ZYX, 4), (ZXY, 4))), (192, 64, 0, ((YZX, 4), (ZXY, 4)))),
+    "mid_b": ((0, 96, 0, ((YZX, 4), (ZXY, 4))), (96, 96, 0, ((YZX, 4), (ZXY, 4))), (192, 96, 0, ((ZYX, 4), (ZXY, 4))), (288, 96, 0, ((YZX, 4), (ZXY, 4))), (384, 96, 0, ((YZX, 4), (ZXY, 4))), (480, 96, 0, ((ZYX, 4), (ZXY, 4)))),
+    "out_b": ((0, 64, 0, ((ZXY, 2), (YZX, 2))), (0, 64, 4, ((ZXY, 2), (YZX, 2)))),
 }
 WAYS_OUT = {
     "in_a": ((0, 64, 4), (64, 64, 4)),
@@ -40,21 +41,25 @@
     "out_b": ((0, 32, 5), (32, 32, 5)),
 }
 RUN = [
-    262, 303, 282, 304, 306, 283, 301, 285, 48, 49, 307, 308, 319, 320, 299, 286, 66, 67, 51, 287, 52, 298,
-    85, 315, 294, 84, 253, 69, 316, 53, 295, 15, 14, 64, 71, 65, 70, 60, 61, 305, 13, 89, 284, 281, 87, 88,
-    82, 83, 12, 255, 309, 19, 18, 310, 288, 79, 311, 100, 312, 78, 313, 291, 289, 290, 101, 50, 97, 314, 17,
-    292, 54, 259, 96, 302, 16, 257, 55, 23, 317, 22, 293, 68, 58, 73, 21, 57, 56, 296, 72, 86, 59, 318, 91,
-    76, 20, 254, 75, 27, 297, 74, 26, 77, 25, 62, 93, 94, 63, 90, 92, 95, 24, 80, 256, 31, 81, 30, 29, 98, 99,
-    28, 258, 35, 34, 33, 32, 39, 38, 37, 36, 43, 275, 42, 41, 276, 107, 127, 128, 40, 47, 270, 271, 46, 272,
-    105, 151, 152, 45, 119, 120, 44, 175, 3, 176, 143, 2, 121, 122, 265, 144, 266, 1, 123, 145, 200, 199, 124,
-    146, 103, 167, 0, 111, 147, 168, 7, 169, 273, 274, 6, 260, 148, 106, 170, 112, 277, 125, 171, 5, 135, 126,
-    261, 278, 172, 191, 136, 108, 4, 193, 11, 149, 10, 9, 159, 129, 194, 267, 223, 268, 150, 269, 160, 104,
-    173, 130, 153, 113, 174, 183, 114, 218, 247, 8, 300, 154, 131, 192, 177, 137, 196, 263, 115, 138, 132,
-    178, 264, 155, 279, 161, 198, 116, 139, 162, 280, 117, 156, 102, 220, 197, 118, 179, 207, 163, 109, 222,
-    140, 180, 186, 184, 110, 244, 246, 202, 216, 141, 221, 142, 195, 201, 240, 185, 133, 203, 134, 217, 226,
-    204, 209, 165, 225, 210, 166, 187, 227, 157, 224, 164, 158, 215, 189, 219, 190, 181, 188, 208, 249, 233,
-    211, 234, 228, 182, 232, 239, 213, 245, 214, 205, 212, 206, 248, 229, 235, 242, 237, 252, 250, 241, 251,
-    231, 238, 236, 243, 230,
+    331, 379, 380, 385, 386, 357, 358, 351, 129, 387, 130, 352, 388, 360, 359, 135, 389, 361, 57, 137, 390,
+    362, 58, 138, 136, 401, 373, 63, 139, 81, 65, 140, 82, 66, 64, 402, 374, 376, 89, 106, 151, 397, 87, 68,
+    105, 67, 398, 88, 321, 90, 23, 369, 111, 152, 22, 92, 350, 79, 91, 370, 114, 147, 148, 21, 381, 382, 80,
+    383, 354, 384, 353, 391, 356, 75, 20, 76, 115, 116, 103, 113, 132, 112, 355, 392, 393, 104, 134, 323, 27,
+    26, 99, 133, 394, 364, 100, 395, 142, 363, 366, 131, 127, 60, 61, 128, 141, 25, 62, 123, 143, 396, 24, 70,
+    59, 124, 145, 328, 367, 377, 365, 69, 325, 31, 368, 85, 146, 30, 86, 84, 144, 83, 399, 73, 74, 93, 109,
+    29, 72, 371, 108, 110, 71, 107, 94, 322, 149, 97, 98, 400, 28, 35, 96, 34, 95, 372, 150, 118, 122, 121,
+    33, 77, 117, 120, 119, 78, 32, 324, 39, 101, 38, 102, 125, 326, 126, 37, 36, 43, 327, 15, 42, 14, 41, 13,
+    40, 47, 12, 19, 46, 378, 18, 17, 45, 44, 56, 16, 51, 344, 345, 50, 171, 195, 49, 172, 196, 48, 55, 339,
+    54, 340, 219, 53, 341, 163, 164, 165, 166, 220, 188, 187, 189, 243, 52, 3, 244, 167, 2, 212, 334, 190,
+    211, 168, 335, 191, 192, 1, 155, 156, 213, 179, 214, 180, 215, 0, 236, 267, 235, 7, 237, 329, 330, 6, 216,
+    346, 347, 173, 342, 203, 174, 268, 259, 238, 198, 5, 239, 204, 343, 169, 193, 197, 227, 261, 240, 175, 4,
+    11, 222, 336, 170, 10, 228, 217, 337, 338, 199, 157, 158, 159, 160, 246, 221, 184, 194, 241, 9, 223, 8,
+    260, 161, 245, 183, 262, 332, 333, 208, 348, 218, 182, 162, 247, 265, 181, 349, 207, 291, 286, 292, 185,
+    242, 176, 153, 232, 270, 206, 263, 154, 178, 205, 200, 209, 177, 230, 271, 229, 231, 186, 252, 287, 266,
+    264, 315, 251, 224, 295, 202, 269, 375, 201, 210, 233, 255, 294, 254, 288, 256, 283, 248, 275, 276, 226,
+    316, 289, 253, 280, 225, 319, 285, 234, 310, 311, 312, 284, 293, 299, 257, 272, 309, 300, 318, 290, 250,
+    281, 279, 278, 307, 249, 277, 317, 258, 302, 305, 304, 274, 313, 296, 273, 282, 320, 308, 297, 301, 303,
+    298, 314, 306,
 ]
 
 
@@ -74,6 +79,7 @@
         self.z = self.f // 2
         self.c = self.d % 2
         self.x = self.d // 2
+        self.inner = self.z * (3 - self.z) > 0
 
     def peer(self, f_bits, d_bits):
         return (flip(self.f, f_bits), flip(self.d, d_bits))
@@ -122,20 +128,21 @@
 
 
 class Gather:
-    def __init__(self, place, shard, whole, start, rows, groups, send, recv):
+    def __init__(self, place, shard, whole, start, rows, from_eighth, groups, send, recv):
         self.place, self.shard, self.whole = place, shard, whole
         self.start, self.rows, self.send, self.recv = start, rows, send, recv
         self.total, columns = shard.shape
-        self.half = half = columns // 2
+        half = columns // 2
         self.part = part = rows // 2
-        self.col_0 = place.c * half
+        self.col_0 = place.c * half + half * from_eighth // 8
         self.row_q = start + place.x * part
         self.row_o = start + part - place.x * part
-        self.arriving, self.leaving = [0] * 4, 0
+        self.arriving, self.leaving = [0] * 5, 0
         self.groups, at = {}, 0
         for way, eighths in groups:
             self.groups[way] = (at, half * eighths // 8)
             at += half * eighths // 8
+        self.wide = at
 
     def view(self, bits, row, rows, from_col, columns):
         block = flip(self.place.f, bits) * self.total
@@ -144,9 +151,10 @@
     def pass_on(self, bits, row, rows, group, leg, peer):
         from_col, columns = group
         view = self.view(bits, row, rows, from_col, columns)
-        push(view, view, self.send, self.recv.at[leg], self.place.peer(*peer))
-        self.arriving[leg] += rows * columns
-        self.leaving += rows * columns
+        push(view, view, self.send, self.recv.at[leg or 0], self.place.peer(*peer))
+        if leg is not None:
+            self.arriving[leg] += rows * columns
+            self.leaving += rows * columns
 
     def pass_own(self, row, rows, group, leg, peer):
         from_col, columns = group
@@ -160,13 +168,26 @@
 
     def first(self):
         pltpu.make_async_copy(
-            self.shard.at[pl.ds(self.start, self.rows), cols_of(self.col_0, self.half)],
-            self.view(0, self.start, self.rows, 0, self.half),
+            self.shard.at[pl.ds(self.start, self.rows), cols_of(self.col_0, self.wide)],
+            self.view(0, self.start, self.rows, 0, self.wide),
             self.recv.at[0],
         ).start()
-        self.arriving[0] += self.rows * self.half
-        for bits in (6, 4, 2):
-            self.pass_own(self.row_q, self.part, (0, self.half), 0, (bits, 0))
+        self.arriving[0] += self.rows * self.wide
+        everything = (0, self.wide)
+
+        @pl.when(self.place.inner)
+        def _():
+            self.pass_own(self.row_q, self.part, everything, 0, (6, 0))
+
+        self.pass_own(self.row_q, self.part, everything, 4, (4, 0))
+        self.pass_own(self.row_q, self.part, everything, 0, (2, 0))
+
+    def relay(self):
+        self.arrive(4)
+
+        @pl.when(self.place.inner)
+        def _():
+            self.pass_on(4, self.row_q, self.part, (0, self.wide), None, (2, 0))
 
     def own(self):
         for way, group in self.groups.items():
@@ -201,13 +222,21 @@
     def three(self):
         self.arrive(2)
         for bits in range(8):
-            self.pass_on(bits, self.start, self.rows, (0, self.half), 3, (0, 1))
+            self.pass_on(bits, self.start, self.rows, (0, self.wide), 3, (0, 1))
 
     def four(self):
         self.arrive(3)
 
     def sent(self):
-        await_count(self.whole, self.leaving, self.send)
+        block = self.part * self.wide
+
+        @pl.when(self.place.inner)
+        def _():
+            await_count(self.whole, self.leaving + block, self.send)
+
+        @pl.when(jnp.logical_not(self.place.inner))
+        def _():
+            await_count(self.whole, self.leaving - block, self.send)
 
 
 def chunk_of(rows, columns):
@@ -225,17 +254,17 @@
     def step(index, carry):
         block, start = index // each, pl.multiple_of((index % each) * chunk, 16)
         into, more = target(block, start, chunk), source(block, start, chunk)
-        into[...] = (into[...].astype(F32) + more[...].astype(F32)).astype(BF16)
+        into[...] = into[...] + more[...]
         return carry
 
     lax.fori_loop(0, blocks * each, step, 0)
 
 
 class Scatter:
-    def __init__(self, place, grad, room, out, start, rows, wide_a, first, send, recv):
+    def __init__(self, place, grad, room, out, start, rows, wide_a, send, recv):
         self.place, self.grad, self.out = place, grad, out
         self.start, self.rows, self.wide_a = start, rows, wide_a
-        self.first, self.send, self.recv = first, send, recv
+        self.send, self.recv = send, recv
         total, columns = room.shape
         self.total = total = total // 8
         self.half = half = columns // 2
@@ -261,9 +290,10 @@
         push(source, target, self.send, self.recv.at[leg], device)
 
     def zero(self):
-        other = self.half - self.col_0
-        source = self.grad.at[:, cols_of(other, self.half)]
-        push(source, self.from_core, self.first.at[0], self.first.at[1], self.place.peer(0, 1))
+        other = cols_of(self.half - self.col_0, self.half)
+        for block in range(8):
+            rows = pl.ds(block * self.total + self.start, self.rows)
+            self.push(self.grad.at[rows, other], self.from_core.at[rows], 5, self.place.peer(0, 1))
 
     def core(self, row, rows, from_col, columns):
         return self.from_core.at[rows_of(row, rows), pl.ds(from_col, columns)]
@@ -271,10 +301,9 @@
     def mine(self, row, rows, from_col, columns):
         return self.core(self.place.f * self.total + row, rows, from_col, columns)
 
-    def one(self, first, last):
+    def one(self):
         place, total, part, rows = self.place, self.total, self.part, self.rows
-        if first:
-            await_bytes(self.from_core, self.first.at[1])
+        await_count(self.room, 8 * rows * self.half, self.recv.at[5])
         add_blocks(
             8,
             rows,
@@ -282,8 +311,7 @@
             lambda b, s, n: self.core(b * total + self.start + s, n, 0, self.half),
             lambda b, s, n: self.grad.at[rows_of(b * total + self.start + s, n), cols_of(self.col_0, self.half)],
         )
-        if last:
-            await_bytes(self.from_core, self.first.at[0])
+        await_count(self.room, 8 * rows * self.half, self.send)
         if self.wide_a:
             for block in range(8):
                 self.push(
@@ -475,38 +503,11 @@
 class Totals:
     def __init__(self, place, short, long, tot, send, recv):
         self.place, self.short, self.long, self.tot, self.send, self.recv = place, short, long, tot, send, recv
-        self.turns, self.is_long, self.rows = [1, 1], 0, 0
-
-    def slot(self, at):
-        ref = self.long if self.is_long else self.short
-        return ref.at[self.turn, at, pl.ds(0, self.rows)]
-
-    def slots(self, at, count):
-        ref = self.long if self.is_long else self.short
-        return ref.at[self.turn, pl.ds(at, count), pl.ds(0, self.rows)]
-
-    def spread(self, at, peers, phase):
-        own = self.slot(at)
-        for bits in peers:
-            push(own, own, self.sem(self.send, phase), self.sem(self.recv, phase), self.place.peer(*bits))
-
-    def sem(self, sems, phase):
-        return sems.at[self.is_long, self.turn, phase]
-
-    def gather(self, at, count, peers, phase):
-        await_bytes(self.slots(at, peers), self.sem(self.recv, phase))
-        ref = self.long if self.is_long else self.short
-        total = ref[self.turn, at, 0 : self.rows, :]
-        for index in range(at + 1, at + count):
-            total = total + ref[self.turn, index, 0 : self.rows, :]
-        return total
+        self.began = 0
 
     def start(self, rows_of_values, extra=None):
-        count = 4 * len(rows_of_values) + (8 if extra is not None else 0)
-        self.is_long = 1 if count > 16 else 0
-        self.turns[self.is_long] = self.turn = 1 - self.turns[self.is_long]
-        self.rows = count
-        own = self.slot(self.place.c)
+        one = Total(self, 4 * len(rows_of_values) + (8 if extra is not None else 0))
+        own = one.slot(self.place.c)
         at = 0
         for row in rows_of_values:
             for lane in range(0, LANES, 128):
@@ -514,7 +515,47 @@
                 at += 1
         if extra is not None:
             own[at : at + 8, :] = extra
-        self.spread(self.place.c, ((0, 1),), 0)
+        one.spread(self.place.c, ((0, 1),), 0)
+        return one
+
+    def row(self, index):
+        at = 4 * index
+        return jnp.concatenate([self.tot[at + k : at + k + 1, :] for k in range(4)], axis=1)
+
+    def wide(self, at):
+        return jnp.concatenate([self.tot[at : at + 1, :]] * 4, axis=1)
+
+
+class Total:
+    def __init__(self, all_of_them, rows):
+        self.all, self.place, self.rows = all_of_them, all_of_them.place, rows
+        self.is_long = rows > 16
+        self.set = SHORT_SETS
+        if not self.is_long:
+            self.set = all_of_them.began % SHORT_SETS
+            all_of_them.began += 1
+
+    def slots(self, at, count):
+        if self.is_long:
+            return self.all.long.at[pl.ds(at, count), pl.ds(0, self.rows)]
+        return self.all.short.at[self.set, pl.ds(at, count), pl.ds(0, self.rows)]
+
+    def slot(self, at):
+        if self.is_long:
+            return self.all.long.at[at, pl.ds(0, self.rows)]
+        return self.all.short.at[self.set, at, pl.ds(0, self.rows)]
+
+    def spread(self, at, peers, phase):
+        own = self.slot(at)
+        for bits in peers:
+            push(own, own, self.all.send.at[self.set, phase], self.all.recv.at[self.set, phase], self.place.peer(*bits))
+
+    def gather(self, at, count, peers, phase):
+        await_bytes(self.slots(at, peers), self.all.recv.at[self.set, phase])
+        total = self.slot(at)[...]
+        for index in range(at + 1, at + count):
+            total = total + self.slot(index)[...]
+        return total
 
     def middle(self):
         place = self.place
@@ -533,18 +574,11 @@
 
     def end(self):
         if self.is_long:
-            self.tot[0 : self.rows, :] = self.gather(6, 4, 3, 2)
+            self.all.tot[0 : self.rows, :] = self.gather(6, 4, 3, 2)
         else:
-            self.tot[0 : self.rows, :] = self.gather(2, 16, 15, 1)
+            self.all.tot[0 : self.rows, :] = self.gather(2, 16, 15, 1)
         for phase, count in enumerate((1, 3, 3) if self.is_long else (1, 15)):
-            await_bytes(self.slots(0, count), self.sem(self.send, phase))
-
-    def row(self, index):
-        at = 4 * index
-        return jnp.concatenate([self.tot[at + k : at + k + 1, :] for k in range(4)], axis=1)
-
-    def wide(self, at):
-        return jnp.concatenate([self.tot[at : at + 1, :]] * 4, axis=1)
+            await_bytes(self.slots(0, count), self.all.send.at[self.set, phase])
 
 
 def step_kernel(
@@ -642,7 +676,6 @@
     io_sem,
     link_send,
     link_recv,
-    core_sem,
     ar_send,
     ar_recv,
     nb_sem,
@@ -671,8 +704,12 @@
         return keep_it
 
     def tokens(name, count, each, step):
+        def some(first):
+            for k in range(each):
+                step(first + k)
+
         for part in range(count):
-            todo[f"{name}.{part}"] = functools.partial(loop, each, lambda k, first=part * each: step(first + k))
+            todo[f"{name}.{part}"] = functools.partial(some, part * each)
 
     gathers, scatters, at, going = {}, {}, 0, 0
     left = {name: len(WAYS_OUT[name]) for name in NAMES}
@@ -688,43 +725,55 @@
             sem = free_sem.at[NAMES.index(name)]
             pl.semaphore_signal(sem, inc=1, device_id=place.peer(*bits), device_id_type=BY_MESH)
 
-    def send_core(name):
-        pl.semaphore_wait(free_sem.at[NAMES.index(name)], len(LINK_PEERS))
-        scatters[name, 0].zero()
+    def send_core(name, n):
+        if n == 0:
+            pl.semaphore_wait(free_sem.at[NAMES.index(name)], len(LINK_PEERS))
+        scatters[name, n].zero()
 
     for name in NAMES:
-        for n, (start, rows, ways) in enumerate(WAYS_IN[name]):
+        for n, (start, rows, from_eighth, ways) in enumerate(WAYS_IN[name]):
             sems = link_send.at[at], link_recv.at[at]
-            g = gathers[name, n] = Gather(place, shards[name], wholes[name], start, rows, ways, *sems)
+            g = gathers[name, n] = Gather(
+                place, shards[name], wholes[name], start, rows, from_eighth, ways, *sems
+            )
             at += 1
             key = f"{name}.{n}"
             todo["z." + key], todo["o." + key], todo["L1." + key] = g.first, g.own, g.one
+            todo["R." + key] = g.relay
             todo["L2." + key], todo["L3." + key] = g.two, g.three
         eighth = shards[name].shape[1] // 16
         for n, (start, rows, wide) in enumerate(WAYS_OUT[name]):
-            sems = core_sem.at[NAMES.index(name)], link_send.at[going], link_recv.at[going]
+            sems = link_send.at[going], link_recv.at[going]
             s = Scatter(place, grads[name], wholes[name], outs[name], start, rows, wide * eighth, *sems)
             scatters[name, n] = s
             going += 1
             key = f"{name}.{n}"
-            todo["S1." + key] = functools.partial(s.one, n == 0, n == len(WAYS_OUT[name]) - 1)
+            todo["S0." + key], todo["S1." + key] = functools.partial(send_core, name, n), s.one
             todo["S2." + key], todo["S3." + key], todo["S4." + key] = s.two, s.three, s.four
             todo["S5." + key] = s.five
             todo["S6." + key] = functools.partial(finish_piece, name, s)
-        todo["S0." + name] = functools.partial(send_core, name)
-
-        def arrived(name=name):
-            for n in range(len(WAYS_IN[name])):
-                gathers[name, n].four()
-
-        todo["W." + name] = arrived
+        def arrived(some):
+            for one in some:
+                one.four()
+
+        mine = [gathers[name, n] for n in range(len(WAYS_IN[name]))]
+        if name == "out_b":
+            for n, one in enumerate(mine):
+                todo[f"W.{name}.{n}"] = one.four
+        else:
+            todo["W." + name] = functools.partial(arrived, mine)
 
     vec = Vectors(vec_ref)
     totals = Totals(place, short, long, tot, ar_send, ar_recv)
     state, scales, params = {}, {}, {}
-    for n in range(1, 13):
-        todo[f"A{n}m"] = totals.middle
-        todo[f"A{n}l"] = totals.late
+    sums_of = {}
+
+    def begin(n, values, extra=None):
+        sums_of[n] = totals.start(values, extra)
+
+    for n in range(1, 15):
+        todo[f"A{n}m"] = lambda n=n: sums_of[n].middle()
+        todo[f"A{n}l"] = lambda n=n: sums_of[n].late()
 
     image_copy = pltpu.make_async_copy(img_hbm, raw, io_sem.at[0])
     cot_copy = pltpu.make_async_copy(cot_hbm, cot, io_sem.at[1])
@@ -889,11 +938,11 @@
         count_out = sum((s // 2) * (s // 2) for s in side).astype(F32)
         at = lax.broadcasted_iota(jnp.int32, (8, 128), 0)
         counts = jnp.where(at == 0, count_in, jnp.where(at == 1, count_out, 0.0))
-        totals.start(column_sums(32, 2, square_terms(c1)), counts)
+        begin(1, column_sums(32, 2, square_terms(c1)), counts)
 
     @token("A1e")
     def _():
-        totals.end()
+        sums_of[1].end()
         state["inv_in"] = vec.put(1.0 / totals.wide(8))
         state["inv_out"] = vec.put(1.0 / totals.wide(9))
         set_norm("in_a", 0, 0, "inv_in", "chan_a")
@@ -929,11 +978,11 @@
     @token("A2s")
     def _():
         conv_mid(c2, cols_a, w_mid_a)
-        totals.start(column_sums(8, 2, masked_terms(c2)))
+        begin(2, column_sums(8, 2, masked_terms(c2)))
 
     @token("A2e")
     def _():
-        totals.end()
+        sums_of[2].end()
         set_norm("mid_a", 0, 0, "inv_out", "chan_a")
         act_mid(a2, c2, "mid_a")
 
@@ -951,11 +1000,11 @@
     def _():
         for j in range(4):
             c3[at_block(j, BLOCK), :] = mm(a2[...], w_out_a[:, at_block(j, LANES)])
-        totals.start([row for ref in (c3, cp) for j in range(4) for row in column_sums(8, 2, blocked(ref, j))])
+        begin(3, [row for ref in (c3, cp) for j in range(4) for row in column_sums(8, 2, blocked(ref, j))])
 
     @token("A3e")
     def _():
-        totals.end()
+        sums_of[3].end()
         for j in range(4):
             set_norm("out_a", j, 2 * j, "inv_out", None)
             set_norm("proj_a", j, 8 + 2 * j, "inv_out", None)
@@ -974,11 +1023,11 @@
     @token("A4s")
     def _():
         add_up(d1, 4, lambda k: feed[:, at_block(k, LANES)], lambda k: w_in_b[at_block(k, LANES), :])
-        totals.start(column_sums(8, 2, square_terms(d1)))
+        begin(4, column_sums(8, 2, square_terms(d1)))
 
     @token("A4e")
     def _():
-        totals.end()
+        sums_of[4].end()
         set_norm("in_b", 0, 0, "inv_out", "chan_b")
         s = scales["in_b", 0]
 
@@ -995,33 +1044,29 @@
     @token("A5s")
     def _():
         conv_mid(d2, cols_b, w_mid_b)
-        totals.start(column_sums(8, 2, masked_terms(d2)))
+        begin(5, column_sums(8, 2, masked_terms(d2)))
 
     @token("A5e")
     def _():
-        totals.end()
+        sums_of[5].end()
         set_norm("mid_b", 0, 0, "inv_out", "chan_b")
         act_mid(b2, d2, "mid_b")
 
-    @token("A6s")
-    def _():
-        for j in range(4):
+    PAIRS = ((0, 2), (1, 3))
+
+    def expand_b(n, pair):
+        for j in pair:
             d3[at_block(j, BLOCK), :] = mm(b2[...], w_out_b[:, at_block(j, LANES)])
-        totals.start([row for j in range(4) for row in column_sums(8, 2, blocked(d3, j))])
-
-    @token("A6e")
-    def _():
-        totals.end()
-        for j in range(4):
-            set_norm("out_b", j, 2 * j, "inv_out", None)
-
-    @token("A7s")
-    def _():
-        for one in gathers.values():
-            one.sent()
-        cot_copy.wait()
+        begin(n, [row for j in pair for row in column_sums(8, 2, blocked(d3, j))])
+
+    def set_out_b(n, pair):
+        sums_of[n].end()
+        for k, j in enumerate(pair):
+            set_norm("out_b", j, 2 * k, "inv_out", None)
+
+    def finish_b(n, pair):
         values = []
-        for j in range(4):
+        for j in pair:
             lanes = pl.ds(j * LANES, LANES)
 
             def finish(start, j=j, lanes=lanes):
@@ -1042,19 +1087,46 @@
 
             values += column_sums(SIDE, 2, finish)
             bo[(j + 1) * BLOCK - CHUNK : (j + 1) * BLOCK, :] = jnp.zeros((CHUNK, LANES), F32)
+        begin(n, values)
+
+    todo["A6s"], todo["A13s"] = (functools.partial(expand_b, n, pair) for n, pair in zip((6, 13), PAIRS))
+    todo["A6e"], todo["A13e"] = (functools.partial(set_out_b, n, pair) for n, pair in zip((6, 13), PAIRS))
+
+    @token("A7s")
+    def _():
+        cot_copy.wait()
+        finish_b(7, PAIRS[0])
+
+    @token("A14s")
+    def _():
+        finish_b(14, PAIRS[1])
         result_copy.start()
-        totals.start(values)
-
-    def keep_sums(at):
-        rows = totals.rows
+
+    @token("sent")
+    def _():
+        for one in gathers.values():
+            one.sent()
+
+    def keep_sums(n, at):
+        rows = sums_of[n].rows
         sums[at : at + rows, :] = tot[0:rows, :]
 
-    @token("A7e")
-    def _():
-        totals.end()
-        keep_sums(0)
-        for j in range(4):
-            set_back("out_b", j, 2 * j, 2 * j + 1)
+    def low_out_b(n, at, pair):
+        sums_of[n].end()
+        keep_sums(n, at)
+        for k, j in enumerate(pair):
+            set_back("out_b", j, 2 * k, 2 * k + 1)
+
+            def step(index, j=j):
+                start = pl.multiple_of(index * CHUNK, CHUNK)
+                rows = pl.ds(j * BLOCK + start, CHUNK)
+                grad = back("out_b", j, bo[rows, :] * gate_at(start), d3[rows, :]) * mask_at(start)
+                dout[pl.ds(start, CHUNK), pl.ds(j * LANES, LANES)] = grad.astype(BF16)
+
+            loop(BLOCK // CHUNK, step)
+
+    todo["A7e"] = functools.partial(low_out_b, 7, 0, PAIRS[0])
+    todo["A14e"] = functools.partial(low_out_b, 14, 16, PAIRS[1])
 
     def through_out(weight):
         add_up(dz, 4, lambda k: dout[:, at_block(k, LANES)], lambda k: weight[:, at_block(k, LANES)], mm_nt)
@@ -1070,30 +1142,30 @@
 
         return terms
 
+    def through_pair(pair):
+        return [mm_nt(dout[:, at_block(j, LANES)], w_out_b[:, at_block(j, LANES)]) for j in pair]
+
+    @token("D8")
+    def _():
+        first, second = through_pair(PAIRS[0])
+        dz[...] = first + second
+
     @token("A8s")
     def _():
-        for j in range(4):
-
-            def low_out_b(index, j=j):
-                start = pl.multiple_of(index * CHUNK, CHUNK)
-                rows = pl.ds(j * BLOCK + start, CHUNK)
-                grad = back("out_b", j, bo[rows, :] * gate_at(start), d3[rows, :]) * mask_at(start)
-                dout[pl.ds(start, CHUNK), pl.ds(j * LANES, LANES)] = grad.astype(BF16)
-
-            loop(BLOCK // CHUNK, low_out_b)
-        through_out(w_out_b)
+        first, second = through_pair(PAIRS[1])
+        dz[...] += first + second
         tell("out_b")
-        totals.start(column_sums(8, 2, slope_terms(dz, d2, "mid_b", "chan_b")))
+        begin(8, column_sums(8, 2, slope_terms(dz, d2, "mid_b", "chan_b")))
 
     def grad_out(act_ref, j):
         g_out[:, at_block(j, LANES)] = mm_tn(act_ref[...], dout[:, at_block(j, LANES)]).astype(BF16)
 
-    tokens("g.out_b", 2, 2, lambda j: grad_out(b2, j))
+    tokens("g.out_b", 2, 2, lambda k: grad_out(b2, 2 * (k % 2) + k // 2))
 
     @token("A8e")
     def _():
-        totals.end()
-        keep_sums(32)
+        sums_of[8].end()
+        keep_sums(8, 32)
         set_back("mid_b", 0, 0, 1)
 
     def low_mid(name, ref, shifts):
@@ -1118,7 +1190,7 @@
         low_mid("mid_b", d2, [(32 * (u - 1) + 4 * (v - 1)) % BLOCK for u, v in TAPS])
         add_up(dz, 9, lambda t: g_mid[at_block(t, BLOCK), :], lambda t: w_mid_b[at_block(t, LANES), :], mm_nt)
         tell("mid_b")
-        totals.start(column_sums(8, 2, slope_terms(dz, d1, "in_b", "chan_b")))
+        begin(9, column_sums(8, 2, slope_terms(dz, d1, "in_b", "chan_b")))
 
     def grad_mid(cols, t):
         g_mid[at_block(t, LANES), :] = mm_tn(cols[:, at_block(t, LANES)], dm[...]).astype(BF16)
@@ -1127,8 +1199,8 @@
 
     @token("A9e")
     def _():
-        totals.end()
-        keep_sums(40)
+        sums_of[9].end()
+        keep_sums(9, 40)
         set_back("in_b", 0, 0, 1)
 
     @token("A10s")
@@ -1155,7 +1227,7 @@
                 return grad, grad * hat("out_a", j, left), grad * hat("proj_a", j, right)
 
             values += column_sums(8, 3, join_back)
-        totals.start(values)
+        begin(10, values)
 
     def grad_in_b(j):
         g_in[at_block(j, LANES), :] = mm_tn(feed[:, at_block(j, LANES)], df[...]).astype(BF16)
@@ -1164,8 +1236,8 @@
 
     @token("A10e")
     def _():
-        totals.end()
-        keep_sums(48)
+        sums_of[10].end()
+        keep_sums(10, 48)
         for j in range(4):
             set_back("out_a", j, 3 * j, 3 * j + 1)
             set_back("proj_a", j, 3 * j, 3 * j + 2)
@@ -1185,7 +1257,7 @@
             loop(BLOCK // CHUNK, low_both)
         through_out(w_out_a)
         tell("out_a")
-        totals.start(column_sums(8, 2, slope_terms(dz, c2, "mid_a", "chan_a")))
+        begin(11, column_sums(8, 2, slope_terms(dz, c2, "mid_a", "chan_a")))
 
     tokens("g.out_a", 2, 2, lambda j: grad_out(a2, j))
 
@@ -1212,8 +1284,8 @@
 
     @token("A11e")
     def _():
-        totals.end()
-        keep_sums(96)
+        sums_of[11].end()
+        keep_sums(11, 96)
         set_back("mid_a", 0, 0, 1)
 
     @token("A12s")
@@ -1230,14 +1302,14 @@
                     grad = term if grad is None else grad + term
                 bo[pl.ds((2 * row_par + col_par) * BLOCK, BLOCK), :] = grad
         tell("mid_a")
-        totals.start(column_sums(32, 2, slope_terms(bo, c1, "in_a", "chan_a")))
+        begin(12, column_sums(32, 2, slope_terms(bo, c1, "in_a", "chan_a")))
 
     tokens("g.mid_a", 3, 3, lambda t: grad_mid(cols_a, t))
 
     @token("A12e")
     def _():
-        totals.end()
-        keep_sums(104)
+        sums_of[12].end()
+        keep_sums(12, 104)
         set_back("in_a", 0, 0, 1)
         for p in range(4):
 
@@ -1303,9 +1375,10 @@
             own_row(at + 4, owned[name], 0)
             own_row(at, owned[name], 1)
         block = place.f // 2
-        for name, at, step, gain in (("out_b", 0, 8, 4), ("out_a", 48, 12, 4), ("proj_a", 48, 12, 8)):
-            own_row(at + step * block + gain, owned[name], 0)
-            own_row(at + step * block, owned[name], 1)
+        pair_at = 16 * (block % 2) + 8 * (block // 2)
+        for name, at, gain in (("out_b", pair_at, 4), ("out_a", 48 + 12 * block, 4), ("proj_a", 48 + 12 * block, 8)):
+            own_row(at + gain, owned[name], 0)
+            own_row(at, owned[name], 1)
         for one in own_copies:
             one.start()
 
@@ -1438,16 +1511,15 @@
             pltpu.VMEM((8, 24, 128), F32),
             pltpu.VMEM((24, 128), F32),
             pltpu.VMEM((160, LANES), F32),
-            pltpu.VMEM((2, 18, 16, 128), F32),
-            pltpu.VMEM((2, 10, 64, 128), F32),
+            pltpu.VMEM((SHORT_SETS, 18, 16, 128), F32),
+            pltpu.VMEM((10, 64, 128), F32),
             pltpu.VMEM((64, 128), F32),
             pltpu.VMEM((112, 128), F32),
             pltpu.SemaphoreType.DMA((4,)),
             pltpu.SemaphoreType.DMA((pieces,)),
-            pltpu.SemaphoreType.DMA((pieces, 5)),
-            pltpu.SemaphoreType.DMA((7, 2)),
-            pltpu.SemaphoreType.DMA((2, 2, 3)),
-            pltpu.SemaphoreType.DMA((2, 2, 3)),
+            pltpu.SemaphoreType.DMA((pieces, 6)),
+            pltpu.SemaphoreType.DMA((SHORT_SETS + 1, 3)),
+            pltpu.SemaphoreType.DMA((SHORT_SETS + 1, 3)),
             pltpu.SemaphoreType.DMA((2,)),
             pltpu.SemaphoreType.DMA((2, 7)),
             pltpu.SemaphoreType.REGULAR((7,)),

time: 236 us -> 231 us (0.979)
  Pallas kernels: 235 us -> 230 us
    pallas_call x1, Pallas kernels: 230 us -> 225 us  [body_fast(): pl.pallas_call(step_kernel, out_shape=[jax.ShapeDtypeStruct(cotangent.sha...]
where the time goes in v5:
time: 231 us
  Pallas kernels  230 us (100%)
    pallas_call x1, Pallas kernels, body_fast(): pl.pallas_call(step_kernel, out_shape=[jax.ShapeDtypeStruct(cotangent.sha...  225 us
    pallas_call x1, Pallas kernels, finish_call(): pl.pallas_call(finish_kernel, out_shape=[jax.ShapeDtypeStruct(one.shape,...  4.89 us

profile of v5, /device:TPU:1, one launch (start us, length us, event | category | flops | bytes accessed | tf_op | source)
XLA Modules:
  0.0 230.6 jit_solution(2429905831774175718)
XLA Ops:
  0.7 224.9 %whole_step.1 = (bf16[7,7,4,2048]{3,2,1,0:T(4,128)(2,1)}, bf16[14,14,4,1024]{3,2,1,0:T(4,128)(2,1)}, f32[2,64]{1,0:T(2,128)}, f32[2,64]{1,0:T(2,128)}, f32[2,256...) custom-call(bf16[14,14,4,1024]{3,2,1,0:T(4,128)(2,1)} %bitcast.4, ...), custom_call_target="tpu_custom_call" | custom-call | tf_op jit(solution)/shard_map/whole_step/pallas_call | solution.py:1472
  225.5 4.9 %finish_step.1 = (bf16[7,7,4,2048]{3,2,1,0:T(4,128)(2,1)}, bf16[14,14,4,1024]{3,2,1,0:T(4,128)(2,1)}, f32[2,64]{1,0:T(2,128)}, f32[2,64]{1,0:T(2,128)}, f32[2,25...) custom-call(bf16[7,7,4,2048]{3,2,1,0:T(4,128)(2,1)} %get-tuple-eleme, ...), custom_call_target="tpu_custom_call" | custom-call | tf_op jit(solution)/shard_map/finish_step/pallas_call | solution.py:1427

commit v6 on v5

--- a/solution.py
+++ b/solution.py
@@ -18,7 +18,7 @@
 CHUNK = 32
 SIDE = 7
 ZYX, ZXY, YZX = range(3)
-SHORT_SETS = 4
+SHORT_SETS = 8
 TAPS = [(u, v) for u in range(3) for v in range(3)]
 LINK_PEERS = ((1, 0), (2, 0), (4, 0), (6, 0), (0, 2), (0, 1))
 CHIP_PEERS = tuple((a, b) for a in (7, 6, 5, 4, 3, 2, 1, 0) for b in (2, 0) if a or b)
@@ -27,7 +27,7 @@
     "mid_a": ((0, 96, 0, ((YZX, 4), (ZXY, 4))), (96, 96, 0, ((YZX, 4), (ZXY, 4))), (192, 96, 0, ((ZYX, 4), (ZXY, 4))), (288, 96, 0, ((YZX, 4), (ZXY, 4))), (384, 96, 0, ((YZX, 4), (ZXY, 4))), (480, 96, 0, ((ZYX, 4), (ZXY, 4)))),
     "out_a": ((0, 32, 0, ((ZXY, 5), (YZX, 3))), (32, 32, 0, ((ZXY, 5), (YZX, 3)))),
     "proj_a": ((0, 64, 0, ((ZXY, 5), (YZX, 3))), (64, 64, 0, ((ZXY, 5), (YZX, 3)))),
-    "in_b": ((0, 64, 0, ((YZX, 4), (ZXY, 4))), (64, 64, 0, ((YZX, 4), (ZXY, 4))), (128, 64, 0, ((ZYX, 4), (ZXY, 4))), (192, 64, 0, ((YZX, 4), (ZXY, 4)))),
+    "in_b": ((0, 128, 0, ((YZX, 4), (ZXY, 4))), (128, 128, 0, ((YZX, 4), (ZXY, 4)))),
     "mid_b": ((0, 96, 0, ((YZX, 4), (ZXY, 4))), (96, 96, 0, ((YZX, 4), (ZXY, 4))), (192, 96, 0, ((ZYX, 4), (ZXY, 4))), (288, 96, 0, ((YZX, 4), (ZXY, 4))), (384, 96, 0, ((YZX, 4), (ZXY, 4))), (480, 96, 0, ((ZYX, 4), (ZXY, 4)))),
     "out_b": ((0, 64, 0, ((ZXY, 2), (YZX, 2))), (0, 64, 4, ((ZXY, 2), (YZX, 2)))),
 }
@@ -41,25 +41,26 @@
     "out_b": ((0, 32, 5), (32, 32, 5)),
 }
 RUN = [
-    331, 379, 380, 385, 386, 357, 358, 351, 129, 387, 130, 352, 388, 360, 359, 135, 389, 361, 57, 137, 390,
-    362, 58, 138, 136, 401, 373, 63, 139, 81, 65, 140, 82, 66, 64, 402, 374, 376, 89, 106, 151, 397, 87, 68,
-    105, 67, 398, 88, 321, 90, 23, 369, 111, 152, 22, 92, 350, 79, 91, 370, 114, 147, 148, 21, 381, 382, 80,
-    383, 354, 384, 353, 391, 356, 75, 20, 76, 115, 116, 103, 113, 132, 112, 355, 392, 393, 104, 134, 323, 27,
-    26, 99, 133, 394, 364, 100, 395, 142, 363, 366, 131, 127, 60, 61, 128, 141, 25, 62, 123, 143, 396, 24, 70,
-    59, 124, 145, 328, 367, 377, 365, 69, 325, 31, 368, 85, 146, 30, 86, 84, 144, 83, 399, 73, 74, 93, 109,
-    29, 72, 371, 108, 110, 71, 107, 94, 322, 149, 97, 98, 400, 28, 35, 96, 34, 95, 372, 150, 118, 122, 121,
-    33, 77, 117, 120, 119, 78, 32, 324, 39, 101, 38, 102, 125, 326, 126, 37, 36, 43, 327, 15, 42, 14, 41, 13,
-    40, 47, 12, 19, 46, 378, 18, 17, 45, 44, 56, 16, 51, 344, 345, 50, 171, 195, 49, 172, 196, 48, 55, 339,
-    54, 340, 219, 53, 341, 163, 164, 165, 166, 220, 188, 187, 189, 243, 52, 3, 244, 167, 2, 212, 334, 190,
-    211, 168, 335, 191, 192, 1, 155, 156, 213, 179, 214, 180, 215, 0, 236, 267, 235, 7, 237, 329, 330, 6, 216,
-    346, 347, 173, 342, 203, 174, 268, 259, 238, 198, 5, 239, 204, 343, 169, 193, 197, 227, 261, 240, 175, 4,
-    11, 222, 336, 170, 10, 228, 217, 337, 338, 199, 157, 158, 159, 160, 246, 221, 184, 194, 241, 9, 223, 8,
-    260, 161, 245, 183, 262, 332, 333, 208, 348, 218, 182, 162, 247, 265, 181, 349, 207, 291, 286, 292, 185,
-    242, 176, 153, 232, 270, 206, 263, 154, 178, 205, 200, 209, 177, 230, 271, 229, 231, 186, 252, 287, 266,
-    264, 315, 251, 224, 295, 202, 269, 375, 201, 210, 233, 255, 294, 254, 288, 256, 283, 248, 275, 276, 226,
-    316, 289, 253, 280, 225, 319, 285, 234, 310, 311, 312, 284, 293, 299, 257, 272, 309, 300, 318, 290, 250,
-    281, 279, 278, 307, 249, 277, 317, 258, 302, 305, 304, 274, 313, 296, 273, 282, 320, 308, 297, 301, 303,
-    298, 314, 306,
+    365, 411, 412, 385, 415, 386, 416, 408, 390, 39, 165, 417, 391, 166, 389, 169, 418, 392, 38, 76, 99, 171,
+    419, 393, 100, 170, 420, 77, 82, 103, 394, 172, 121, 105, 173, 431, 80, 104, 405, 122, 174, 84, 107, 81,
+    127, 106, 185, 432, 406, 143, 144, 125, 108, 37, 149, 129, 427, 36, 126, 428, 83, 85, 355, 119, 43, 151,
+    401, 186, 181, 96, 130, 148, 42, 402, 413, 182, 384, 97, 128, 147, 120, 92, 152, 41, 115, 387, 141, 414,
+    421, 150, 116, 40, 357, 93, 167, 47, 46, 422, 423, 142, 424, 163, 175, 137, 138, 168, 395, 45, 425, 388,
+    396, 101, 164, 178, 426, 177, 78, 159, 109, 44, 160, 176, 102, 400, 362, 409, 112, 359, 51, 179, 399, 87,
+    79, 180, 50, 86, 110, 398, 90, 123, 91, 124, 397, 49, 113, 429, 114, 145, 131, 430, 89, 111, 403, 132, 88,
+    146, 135, 48, 136, 356, 183, 55, 184, 153, 54, 134, 133, 94, 404, 117, 157, 53, 154, 158, 118, 156, 155,
+    52, 95, 358, 59, 139, 58, 140, 161, 57, 162, 360, 56, 63, 361, 15, 62, 23, 14, 27, 22, 61, 26, 60, 13, 67,
+    12, 19, 25, 21, 66, 65, 20, 31, 18, 24, 17, 35, 30, 34, 64, 16, 33, 98, 410, 29, 378, 28, 32, 71, 70, 69,
+    379, 205, 206, 229, 230, 68, 75, 373, 374, 74, 253, 375, 197, 198, 199, 221, 200, 201, 254, 223, 202, 277,
+    225, 73, 72, 245, 3, 278, 2, 247, 301, 368, 226, 222, 224, 369, 189, 269, 1, 271, 250, 249, 190, 213, 0,
+    246, 214, 7, 376, 248, 363, 6, 377, 203, 364, 273, 237, 274, 227, 204, 228, 380, 238, 381, 5, 272, 207,
+    298, 261, 208, 209, 210, 231, 4, 251, 325, 11, 262, 370, 270, 233, 371, 252, 10, 372, 295, 322, 286, 255,
+    234, 191, 346, 192, 275, 257, 216, 276, 9, 193, 8, 285, 310, 194, 232, 258, 366, 297, 294, 367, 195, 279,
+    240, 319, 281, 382, 296, 219, 217, 256, 282, 196, 218, 383, 220, 334, 187, 188, 243, 320, 349, 241, 212,
+    302, 280, 264, 306, 244, 215, 265, 299, 242, 305, 236, 304, 211, 268, 323, 239, 309, 300, 330, 266, 289,
+    318, 326, 288, 293, 292, 235, 303, 263, 342, 260, 328, 312, 347, 407, 290, 329, 316, 333, 313, 324, 317,
+    267, 340, 259, 327, 336, 287, 343, 344, 314, 284, 337, 354, 291, 321, 283, 352, 315, 308, 351, 341, 353,
+    311, 307, 350, 345, 339, 348, 335, 338, 332, 331,
 ]
 
 
@@ -137,7 +138,7 @@
         self.col_0 = place.c * half + half * from_eighth // 8
         self.row_q = start + place.x * part
         self.row_o = start + part - place.x * part
-        self.arriving, self.leaving = [0] * 5, 0
+        self.arriving, self.leaving = [0] * 6, 0
         self.groups, at = {}, 0
         for way, eighths in groups:
             self.groups[way] = (at, half * eighths // 8)
@@ -192,22 +193,24 @@
     def own(self):
         for way, group in self.groups.items():
             if way == ZXY:
-                self.pass_own(self.start, self.rows, group, 0, (1, 0))
+                self.pass_own(self.start, self.rows, group, 5, (1, 0))
             else:
-                self.pass_own(self.row_q, self.part, group, 0, (1, 0))
-
-    def one(self):
-        self.arrive(0)
+                self.pass_own(self.row_q, self.part, group, 5, (1, 0))
+
+    def beside(self):
+        self.arrive(5)
         if YZX in self.groups:
             for bits in (6, 4, 2):
                 self.pass_on(1, self.row_q, self.part, self.groups[YZX], 1, (bits, 0))
+            self.pass_on(1, self.row_q, self.part, self.groups[YZX], 1, (0, 2))
+
+    def one(self):
+        self.arrive(0)
         for way, group in self.groups.items():
             for bits in (2, 4, 6):
                 if way != YZX:
                     self.pass_on(bits, self.row_q, self.part, group, 1, (1, 0))
                 self.pass_on(bits, self.row_q, self.part, group, 1, (0, 2))
-            if way == YZX:
-                self.pass_on(1, self.row_q, self.part, group, 1, (0, 2))
 
     def two(self):
         self.arrive(1)
@@ -505,16 +508,15 @@
         self.place, self.short, self.long, self.tot, self.send, self.recv = place, short, long, tot, send, recv
         self.began = 0
 
-    def start(self, rows_of_values, extra=None):
-        one = Total(self, 4 * len(rows_of_values) + (8 if extra is not None else 0))
+    def start(self, rows_of_values):
+        whole = not isinstance(rows_of_values, list)
+        one = Total(self, 8 if whole else 4 * len(rows_of_values))
         own = one.slot(self.place.c)
-        at = 0
-        for row in rows_of_values:
-            for lane in range(0, LANES, 128):
-                own[at : at + 1, :] = row[:, lane : lane + 128]
-                at += 1
-        if extra is not None:
-            own[at : at + 8, :] = extra
+        if whole:
+            own[...] = rows_of_values
+        for n, row in enumerate([] if whole else rows_of_values):
+            for k in range(4):
+                own[4 * n + k : 4 * n + k + 1, :] = row[:, 128 * k : 128 * (k + 1)]
         one.spread(self.place.c, ((0, 1),), 0)
         return one
 
@@ -529,7 +531,7 @@
 class Total:
     def __init__(self, all_of_them, rows):
         self.all, self.place, self.rows = all_of_them, all_of_them.place, rows
-        self.is_long = rows > 16
+        self.is_long = rows > 8
         self.set = SHORT_SETS
         if not self.is_long:
             self.set = all_of_them.began % SHORT_SETS
@@ -739,7 +741,7 @@
             at += 1
             key = f"{name}.{n}"
             todo["z." + key], todo["o." + key], todo["L1." + key] = g.first, g.own, g.one
-            todo["R." + key] = g.relay
+            todo["R." + key], todo["B." + key] = g.relay, g.beside
             todo["L2." + key], todo["L3." + key] = g.two, g.three
         eighth = shards[name].shape[1] // 16
         for n, (start, rows, wide) in enumerate(WAYS_OUT[name]):
@@ -768,10 +770,10 @@
     state, scales, params = {}, {}, {}
     sums_of = {}
 
-    def begin(n, values, extra=None):
-        sums_of[n] = totals.start(values, extra)
-
-    for n in range(1, 15):
+    def begin(n, values):
+        sums_of[n] = totals.start(values)
+
+    for n in range(1, 20):
         todo[f"A{n}m"] = lambda n=n: sums_of[n].middle()
         todo[f"A{n}l"] = lambda n=n: sums_of[n].late()
 
@@ -933,18 +935,25 @@
     def _():
         for p in range(4):
             c1[at_block(p, BLOCK), :] = mm(x[at_block(p, BLOCK), :], w_in_a[...])
+        begin(1, column_sums(32, 2, square_terms(c1)))
+
+    @token("A19s")
+    def _():
         side = [sides[i] for i in range(4)]
         count_in = sum(s * s for s in side).astype(F32)
         count_out = sum((s // 2) * (s // 2) for s in side).astype(F32)
         at = lax.broadcasted_iota(jnp.int32, (8, 128), 0)
-        counts = jnp.where(at == 0, count_in, jnp.where(at == 1, count_out, 0.0))
-        begin(1, column_sums(32, 2, square_terms(c1)), counts)
+        begin(19, jnp.where(at == 0, count_in, jnp.where(at == 1, count_out, 0.0)))
+
+    @token("A19e")
+    def _():
+        sums_of[19].end()
+        state["inv_in"] = vec.put(1.0 / totals.wide(0))
+        state["inv_out"] = vec.put(1.0 / totals.wide(1))
 
     @token("A1e")
     def _():
         sums_of[1].end()
-        state["inv_in"] = vec.put(1.0 / totals.wide(8))
-        state["inv_out"] = vec.put(1.0 / totals.wide(9))
         set_norm("in_a", 0, 0, "inv_in", "chan_a")
         s = scales["in_a", 0]
 
@@ -1053,54 +1062,48 @@
         act_mid(b2, d2, "mid_b")
 
     PAIRS = ((0, 2), (1, 3))
-
-    def expand_b(n, pair):
-        for j in pair:
-            d3[at_block(j, BLOCK), :] = mm(b2[...], w_out_b[:, at_block(j, LANES)])
-        begin(n, [row for j in pair for row in column_sums(8, 2, blocked(d3, j))])
-
-    def set_out_b(n, pair):
+    FORTH = {6: 0, 13: 2, 15: 1, 16: 3}
+    BACK = {7: 0, 14: 2, 17: 1, 18: 3}
+
+    def expand_b(n, j):
+        d3[at_block(j, BLOCK), :] = mm(b2[...], w_out_b[:, at_block(j, LANES)])
+        begin(n, column_sums(8, 2, blocked(d3, j)))
+
+    def set_out_b(n, j):
         sums_of[n].end()
-        for k, j in enumerate(pair):
-            set_norm("out_b", j, 2 * k, "inv_out", None)
-
-    def finish_b(n, pair):
-        values = []
-        for j in pair:
-            lanes = pl.ds(j * LANES, LANES)
-
-            def finish(start, j=j, lanes=lanes):
-                rows = pl.ds(j * BLOCK + start, CHUNK)
-                row = start // CHUNK
-                for col in range(SIDE):
-                    move[4 * col : 4 * col + 4, 0:LANES] = cot[row, col, :, lanes].astype(F32)
-                mask, gate, hidden = mask_at(start), gate_at(start), d3[rows, :]
-                pre = bo[rows, :] + gate * normed("out_b", j, hidden)
-                part = jax.nn.sigmoid(pre)
-                grad = move[:, 0:LANES] * mask * (part * (1.0 + pre * (1.0 - part)))
-                move[:, LANES : 2 * LANES] = pre * part * mask
-                for col in range(SIDE):
-                    cot[row, col, :, lanes] = move[4 * col : 4 * col + 4, LANES : 2 * LANES].astype(BF16)
-                bo[rows, :] = grad
-                grad = grad * gate
-                return grad, grad * hat("out_b", j, hidden)
-
-            values += column_sums(SIDE, 2, finish)
-            bo[(j + 1) * BLOCK - CHUNK : (j + 1) * BLOCK, :] = jnp.zeros((CHUNK, LANES), F32)
+        set_norm("out_b", j, 0, "inv_out", None)
+
+    def finish_b(n, j):
+        if n == 7:
+            cot_copy.wait()
+        lanes = pl.ds(j * LANES, LANES)
+
+        def finish(start):
+            rows = pl.ds(j * BLOCK + start, CHUNK)
+            row = start // CHUNK
+            for col in range(SIDE):
+                move[4 * col : 4 * col + 4, 0:LANES] = cot[row, col, :, lanes].astype(F32)
+            mask, gate, hidden = mask_at(start), gate_at(start), d3[rows, :]
+            pre = bo[rows, :] + gate * normed("out_b", j, hidden)
+            part = jax.nn.sigmoid(pre)
+            grad = move[:, 0:LANES] * mask * (part * (1.0 + pre * (1.0 - part)))
+            move[:, LANES : 2 * LANES] = pre * part * mask
+            for col in range(SIDE):
+                cot[row, col, :, lanes] = move[4 * col : 4 * col + 4, LANES : 2 * LANES].astype(BF16)
+            bo[rows, :] = grad
+            grad = grad * gate
+            return grad, grad * hat("out_b", j, hidden)
+
+        values = column_sums(SIDE, 2, finish)
+        bo[(j + 1) * BLOCK - CHUNK : (j + 1) * BLOCK, :] = jnp.zeros((CHUNK, LANES), F32)
         begin(n, values)
-
-    todo["A6s"], todo["A13s"] = (functools.partial(expand_b, n, pair) for n, pair in zip((6, 13), PAIRS))
-    todo["A6e"], todo["A13e"] = (functools.partial(set_out_b, n, pair) for n, pair in zip((6, 13), PAIRS))
-
-    @token("A7s")
-    def _():
-        cot_copy.wait()
-        finish_b(7, PAIRS[0])
-
-    @token("A14s")
-    def _():
-        finish_b(14, PAIRS[1])
-        result_copy.start()
+        if n == 18:
+            result_copy.start()
+
+    for n, j in FORTH.items():
+        todo[f"A{n}s"], todo[f"A{n}e"] = functools.partial(expand_b, n, j), functools.partial(set_out_b, n, j)
+    for n, j in BACK.items():
+        todo[f"A{n}s"] = functools.partial(finish_b, n, j)
 
     @token("sent")
     def _():
@@ -1111,22 +1114,21 @@
         rows = sums_of[n].rows
         sums[at : at + rows, :] = tot[0:rows, :]
 
-    def low_out_b(n, at, pair):
+    def low_out_b(n, j):
         sums_of[n].end()
-        keep_sums(n, at)
-        for k, j in enumerate(pair):
-            set_back("out_b", j, 2 * k, 2 * k + 1)
-
-            def step(index, j=j):
-                start = pl.multiple_of(index * CHUNK, CHUNK)
-                rows = pl.ds(j * BLOCK + start, CHUNK)
-                grad = back("out_b", j, bo[rows, :] * gate_at(start), d3[rows, :]) * mask_at(start)
-                dout[pl.ds(start, CHUNK), pl.ds(j * LANES, LANES)] = grad.astype(BF16)
-
-            loop(BLOCK // CHUNK, step)
-
-    todo["A7e"] = functools.partial(low_out_b, 7, 0, PAIRS[0])
-    todo["A14e"] = functools.partial(low_out_b, 14, 16, PAIRS[1])
+        keep_sums(n, 16 * (j % 2) + 8 * (j // 2))
+        set_back("out_b", j, 0, 1)
+
+        def step(index):
+            start = pl.multiple_of(index * CHUNK, CHUNK)
+            rows = pl.ds(j * BLOCK + start, CHUNK)
+            grad = back("out_b", j, bo[rows, :] * gate_at(start), d3[rows, :]) * mask_at(start)
+            dout[pl.ds(start, CHUNK), pl.ds(j * LANES, LANES)] = grad.astype(BF16)
+
+        loop(BLOCK // CHUNK, step)
+
+    for n, j in BACK.items():
+        todo[f"A{n}e"] = functools.partial(low_out_b, n, j)
 
     def through_out(weight):
         add_up(dz, 4, lambda k: dout[:, at_block(k, LANES)], lambda k: weight[:, at_block(k, LANES)], mm_nt)
@@ -1511,7 +1513,7 @@
             pltpu.VMEM((8, 24, 128), F32),
             pltpu.VMEM((24, 128), F32),
             pltpu.VMEM((160, LANES), F32),
-            pltpu.VMEM((SHORT_SETS, 18, 16, 128), F32),
+            pltpu.VMEM((SHORT_SETS, 18, 8, 128), F32),
             pltpu.VMEM((10, 64, 128), F32),
             pltpu.VMEM((64, 128), F32),
             pltpu.VMEM((112, 128), F32),

time: 231 us -> 227 us (0.983)
  Pallas kernels: 230 us -> 226 us
    pallas_call x1, Pallas kernels: 225 us -> 221 us  [body_fast(): pl.pallas_call(step_kernel, out_shape=[jax.ShapeDtypeStruct(cotangent.sha...]
where the time goes in v6:
time: 227 us
  Pallas kernels  226 us (100%)
    pallas_call x1, Pallas kernels, body_fast(): pl.pallas_call(step_kernel, out_shape=[jax.ShapeDtypeStruct(cotangent.sha...  221 us
    pallas_call x1, Pallas kernels, finish_call(): pl.pallas_call(finish_kernel, out_shape=[jax.ShapeDtypeStruct(one.shape,...  4.89 us

profile of v6, /device:TPU:1, one launch (start us, length us, event | category | flops | bytes accessed | tf_op | source)
XLA Modules:
  0.0 227.0 jit_solution(10863283320292032732)
XLA Ops:
  0.7 221.2 %whole_step.1 = (bf16[7,7,4,2048]{3,2,1,0:T(4,128)(2,1)}, bf16[14,14,4,1024]{3,2,1,0:T(4,128)(2,1)}, f32[2,64]{1,0:T(2,128)}, f32[2,64]{1,0:T(2,128)}, f32[2,256...) custom-call(bf16[14,14,4,1024]{3,2,1,0:T(4,128)(2,1)} %bitcast.4, ...), custom_call_target="tpu_custom_call" | custom-call | tf_op jit(solution)/shard_map/whole_step/pallas_call | solution.py:1474
  221.9 4.9 %finish_step.1 = (bf16[7,7,4,2048]{3,2,1,0:T(4,128)(2,1)}, bf16[14,14,4,1024]{3,2,1,0:T(4,128)(2,1)}, f32[2,64]{1,0:T(2,128)}, f32[2,64]{1,0:T(2,128)}, f32[2,25...) custom-call(bf16[7,7,4,2048]{3,2,1,0:T(4,128)(2,1)} %get-tuple-eleme, ...), custom_call_target="tpu_custom_call" | custom-call | tf_op jit(solution)/shard_map/finish_step/pallas_call | solution.py:1429

commit v7 on v6

--- a/solution.py
+++ b/solution.py
@@ -41,26 +41,26 @@
     "out_b": ((0, 32, 5), (32, 32, 5)),
 }
 RUN = [
-    365, 411, 412, 385, 415, 386, 416, 408, 390, 39, 165, 417, 391, 166, 389, 169, 418, 392, 38, 76, 99, 171,
-    419, 393, 100, 170, 420, 77, 82, 103, 394, 172, 121, 105, 173, 431, 80, 104, 405, 122, 174, 84, 107, 81,
-    127, 106, 185, 432, 406, 143, 144, 125, 108, 37, 149, 129, 427, 36, 126, 428, 83, 85, 355, 119, 43, 151,
-    401, 186, 181, 96, 130, 148, 42, 402, 413, 182, 384, 97, 128, 147, 120, 92, 152, 41, 115, 387, 141, 414,
-    421, 150, 116, 40, 357, 93, 167, 47, 46, 422, 423, 142, 424, 163, 175, 137, 138, 168, 395, 45, 425, 388,
-    396, 101, 164, 178, 426, 177, 78, 159, 109, 44, 160, 176, 102, 400, 362, 409, 112, 359, 51, 179, 399, 87,
-    79, 180, 50, 86, 110, 398, 90, 123, 91, 124, 397, 49, 113, 429, 114, 145, 131, 430, 89, 111, 403, 132, 88,
-    146, 135, 48, 136, 356, 183, 55, 184, 153, 54, 134, 133, 94, 404, 117, 157, 53, 154, 158, 118, 156, 155,
-    52, 95, 358, 59, 139, 58, 140, 161, 57, 162, 360, 56, 63, 361, 15, 62, 23, 14, 27, 22, 61, 26, 60, 13, 67,
-    12, 19, 25, 21, 66, 65, 20, 31, 18, 24, 17, 35, 30, 34, 64, 16, 33, 98, 410, 29, 378, 28, 32, 71, 70, 69,
-    379, 205, 206, 229, 230, 68, 75, 373, 374, 74, 253, 375, 197, 198, 199, 221, 200, 201, 254, 223, 202, 277,
-    225, 73, 72, 245, 3, 278, 2, 247, 301, 368, 226, 222, 224, 369, 189, 269, 1, 271, 250, 249, 190, 213, 0,
-    246, 214, 7, 376, 248, 363, 6, 377, 203, 364, 273, 237, 274, 227, 204, 228, 380, 238, 381, 5, 272, 207,
-    298, 261, 208, 209, 210, 231, 4, 251, 325, 11, 262, 370, 270, 233, 371, 252, 10, 372, 295, 322, 286, 255,
-    234, 191, 346, 192, 275, 257, 216, 276, 9, 193, 8, 285, 310, 194, 232, 258, 366, 297, 294, 367, 195, 279,
-    240, 319, 281, 382, 296, 219, 217, 256, 282, 196, 218, 383, 220, 334, 187, 188, 243, 320, 349, 241, 212,
-    302, 280, 264, 306, 244, 215, 265, 299, 242, 305, 236, 304, 211, 268, 323, 239, 309, 300, 330, 266, 289,
-    318, 326, 288, 293, 292, 235, 303, 263, 342, 260, 328, 312, 347, 407, 290, 329, 316, 333, 313, 324, 317,
-    267, 340, 259, 327, 336, 287, 343, 344, 314, 284, 337, 354, 291, 321, 283, 352, 315, 308, 351, 341, 353,
-    311, 307, 350, 345, 339, 348, 335, 338, 332, 331,
+    365, 411, 412, 385, 415, 386, 416, 390, 165, 417, 408, 391, 166, 384, 389, 39, 169, 76, 38, 418, 392, 170,
+    99, 171, 419, 77, 420, 394, 100, 103, 82, 393, 121, 172, 104, 105, 173, 431, 80, 405, 85, 83, 174, 122,
+    106, 107, 127, 84, 185, 432, 37, 406, 125, 143, 128, 81, 108, 129, 119, 144, 427, 355, 186, 428, 96, 413,
+    402, 43, 126, 130, 401, 42, 150, 120, 182, 147, 414, 181, 141, 149, 97, 41, 116, 93, 387, 115, 151, 36,
+    152, 92, 421, 40, 422, 148, 168, 142, 163, 357, 423, 138, 47, 175, 167, 137, 46, 395, 102, 45, 424, 164,
+    397, 177, 425, 388, 176, 396, 160, 426, 429, 109, 101, 362, 159, 78, 409, 111, 44, 359, 51, 79, 178, 86,
+    87, 50, 110, 398, 180, 124, 123, 179, 112, 183, 399, 49, 113, 400, 146, 89, 430, 145, 114, 132, 90, 88,
+    403, 356, 133, 131, 48, 55, 184, 134, 91, 54, 53, 154, 136, 135, 153, 155, 404, 156, 117, 94, 158, 157,
+    118, 52, 95, 358, 59, 139, 58, 140, 161, 162, 57, 360, 56, 63, 15, 361, 62, 14, 23, 27, 22, 26, 61, 60,
+    67, 13, 12, 21, 19, 66, 65, 20, 25, 31, 24, 18, 35, 30, 34, 17, 410, 29, 64, 16, 98, 33, 28, 32, 71, 378,
+    70, 69, 379, 205, 206, 229, 230, 68, 75, 373, 374, 74, 253, 375, 197, 221, 198, 254, 199, 222, 200, 277,
+    73, 201, 224, 202, 72, 245, 3, 278, 368, 2, 246, 223, 369, 189, 226, 225, 248, 1, 247, 269, 302, 190, 213,
+    250, 0, 270, 249, 7, 301, 272, 376, 377, 6, 214, 363, 203, 5, 271, 237, 204, 364, 227, 274, 273, 380, 381,
+    228, 207, 238, 325, 4, 208, 11, 349, 251, 298, 209, 10, 232, 261, 233, 294, 370, 371, 262, 372, 191, 252,
+    215, 256, 322, 231, 295, 9, 275, 192, 8, 193, 346, 276, 257, 366, 217, 194, 318, 280, 195, 239, 196, 367,
+    342, 293, 326, 382, 296, 210, 255, 216, 383, 350, 218, 281, 241, 187, 219, 285, 188, 263, 240, 242, 279,
+    220, 286, 212, 264, 320, 319, 304, 287, 234, 243, 266, 297, 265, 309, 211, 344, 343, 244, 333, 236, 258,
+    305, 235, 328, 303, 288, 260, 289, 290, 300, 317, 268, 407, 299, 352, 282, 327, 267, 341, 313, 310, 312,
+    259, 329, 284, 321, 351, 292, 314, 324, 337, 334, 336, 353, 306, 311, 345, 338, 291, 348, 323, 283, 316,
+    308, 335, 347, 315, 330, 307, 340, 332, 339, 354, 331,
 ]
 
 
@@ -550,10 +550,10 @@
     def spread(self, at, peers, phase):
         own = self.slot(at)
         for bits in peers:
-            push(own, own, self.all.send.at[self.set, phase], self.all.recv.at[self.set, phase], self.place.peer(*bits))
+            push(own, own, self.all.send.at[self.set], self.all.recv.at[2 * self.set + phase], self.place.peer(*bits))
 
     def gather(self, at, count, peers, phase):
-        await_bytes(self.slots(at, peers), self.all.recv.at[self.set, phase])
+        await_bytes(self.slots(at, peers), self.all.recv.at[2 * self.set + phase])
         total = self.slot(at)[...]
         for index in range(at + 1, at + count):
             total = total + self.slot(index)[...]
@@ -579,8 +579,7 @@
             self.all.tot[0 : self.rows, :] = self.gather(6, 4, 3, 2)
         else:
             self.all.tot[0 : self.rows, :] = self.gather(2, 16, 15, 1)
-        for phase, count in enumerate((1, 3, 3) if self.is_long else (1, 15)):
-            await_bytes(self.slots(0, count), self.all.send.at[self.set, phase])
+        await_bytes(self.slots(0, 7 if self.is_long else 16), self.all.send.at[self.set])
 
 
 def step_kernel(
@@ -1520,8 +1519,8 @@
             pltpu.SemaphoreType.DMA((4,)),
             pltpu.SemaphoreType.DMA((pieces,)),
             pltpu.SemaphoreType.DMA((pieces, 6)),
-            pltpu.SemaphoreType.DMA((SHORT_SETS + 1, 3)),
-            pltpu.SemaphoreType.DMA((SHORT_SETS + 1, 3)),
+            pltpu.SemaphoreType.DMA((SHORT_SETS + 1,)),
+            pltpu.SemaphoreType.DMA((2 * SHORT_SETS + 3,)),
             pltpu.SemaphoreType.DMA((2,)),
             pltpu.SemaphoreType.DMA((2, 7)),
             pltpu.SemaphoreType.REGULAR((7,)),

time: 227 us -> 226 us (level)
  no operation moved by 1% of the time
where the time goes in v7:
time: 226 us
  Pallas kernels  225 us (100%)
    pallas_call x1, Pallas kernels, body_fast(): pl.pallas_call(step_kernel, out_shape=[jax.ShapeDtypeStruct(cotangent.sha...  220 us
    pallas_call x1, Pallas kernels, finish_call(): pl.pallas_call(finish_kernel, out_shape=[jax.ShapeDtypeStruct(one.shape,...  4.89 us

profile of v7, /device:TPU:1, one launch (start us, length us, event | category | flops | bytes accessed | tf_op | source)
XLA Modules:
  0.0 225.9 jit_solution(17318306762131290740)
XLA Ops:
  0.7 220.2 %whole_step.1 = (bf16[7,7,4,2048]{3,2,1,0:T(4,128)(2,1)}, bf16[14,14,4,1024]{3,2,1,0:T(4,128)(2,1)}, f32[2,64]{1,0:T(2,128)}, f32[2,64]{1,0:T(2,128)}, f32[2,256...) custom-call(bf16[14,14,4,1024]{3,2,1,0:T(4,128)(2,1)} %bitcast.4, ...), custom_call_target="tpu_custom_call" | custom-call | tf_op jit(solution)/shard_map/whole_step/pallas_call | solution.py:1473
  220.9 4.9 %finish_step.1 = (bf16[7,7,4,2048]{3,2,1,0:T(4,128)(2,1)}, bf16[14,14,4,1024]{3,2,1,0:T(4,128)(2,1)}, f32[2,64]{1,0:T(2,128)}, f32[2,64]{1,0:T(2,128)}, f32[2,25...) custom-call(bf16[7,7,4,2048]{3,2,1,0:T(4,128)(2,1)} %get-tuple-eleme, ...), custom_call_target="tpu_custom_call" | custom-call | tf_op jit(solution)/shard_map/finish_step/pallas_call | solution.py:1428

commit v8 on v7

--- a/solution.py
+++ b/solution.py
@@ -41,10 +41,10 @@
     "out_b": ((0, 32, 5), (32, 32, 5)),
 }
 RUN = [
-    365, 411, 412, 385, 415, 386, 416, 390, 165, 417, 408, 391, 166, 384, 389, 39, 169, 76, 38, 418, 392, 170,
-    99, 171, 419, 77, 420, 394, 100, 103, 82, 393, 121, 172, 104, 105, 173, 431, 80, 405, 85, 83, 174, 122,
-    106, 107, 127, 84, 185, 432, 37, 406, 125, 143, 128, 81, 108, 129, 119, 144, 427, 355, 186, 428, 96, 413,
-    402, 43, 126, 130, 401, 42, 150, 120, 182, 147, 414, 181, 141, 149, 97, 41, 116, 93, 387, 115, 151, 36,
+    365, 411, 412, 385, 415, 386, 416, 390, 165, 417, 408, 391, 166, 389, 39, 169, 76, 38, 418, 392, 170, 99,
+    171, 419, 77, 420, 394, 100, 103, 82, 393, 121, 172, 104, 105, 173, 431, 80, 405, 85, 83, 174, 122, 106,
+    107, 127, 84, 185, 432, 37, 406, 125, 143, 128, 81, 108, 129, 119, 144, 427, 355, 186, 428, 96, 413, 402,
+    43, 126, 130, 401, 42, 150, 120, 182, 147, 414, 181, 141, 149, 97, 41, 116, 93, 387, 115, 151, 36, 384,
     152, 92, 421, 40, 422, 148, 168, 142, 163, 357, 423, 138, 47, 175, 167, 137, 46, 395, 102, 45, 424, 164,
     397, 177, 425, 388, 176, 396, 160, 426, 429, 109, 101, 362, 159, 78, 409, 111, 44, 359, 51, 79, 178, 86,
     87, 50, 110, 398, 180, 124, 123, 179, 112, 183, 399, 49, 113, 400, 146, 89, 430, 145, 114, 132, 90, 88,
@@ -801,8 +801,6 @@
                 at += 1
         norms[place.f] = block_ref[...]
         enter(place, ((0, 1),) + CHIP_PEERS)
-        for bits in (7, 6, 5, 4, 3, 2, 1):
-            push(block_ref, norms.at[place.f], nb_sem.at[0], nb_sem.at[1], place.peer(bits, 0))
 
     @token("prep")
     def _():
@@ -943,6 +941,8 @@
         count_out = sum((s // 2) * (s // 2) for s in side).astype(F32)
         at = lax.broadcasted_iota(jnp.int32, (8, 128), 0)
         begin(19, jnp.where(at == 0, count_in, jnp.where(at == 1, count_out, 0.0)))
+        for bits in (7, 6, 5, 4, 3, 2, 1):
+            push(block_ref, norms.at[place.f], nb_sem.at[0], nb_sem.at[1], place.peer(bits, 0))
 
     @token("A19e")
     def _():

time: 226 us -> 226 us (level)
  no operation moved by 1% of the time
where the time goes in v8:
time: 226 us
  Pallas kernels  225 us (100%)
    pallas_call x1, Pallas kernels, body_fast(): pl.pallas_call(step_kernel, out_shape=[jax.ShapeDtypeStruct(cotangent.sha...  220 us
    pallas_call x1, Pallas kernels, finish_call(): pl.pallas_call(finish_kernel, out_shape=[jax.ShapeDtypeStruct(one.shape,...  4.89 us

profile of v8, /device:TPU:1, one launch (start us, length us, event | category | flops | bytes accessed | tf_op | source)
XLA Modules:
  0.0 226.1 jit_solution(9746557938017911093)
XLA Ops:
  0.7 220.4 %whole_step.1 = (bf16[7,7,4,2048]{3,2,1,0:T(4,128)(2,1)}, bf16[14,14,4,1024]{3,2,1,0:T(4,128)(2,1)}, f32[2,64]{1,0:T(2,128)}, f32[2,64]{1,0:T(2,128)}, f32[2,256...) custom-call(bf16[14,14,4,1024]{3,2,1,0:T(4,128)(2,1)} %bitcast.4, ...), custom_call_target="tpu_custom_call" | custom-call | tf_op jit(solution)/shard_map/whole_step/pallas_call | solution.py:1473
  221.1 4.9 %finish_step.1 = (bf16[7,7,4,2048]{3,2,1,0:T(4,128)(2,1)}, bf16[14,14,4,1024]{3,2,1,0:T(4,128)(2,1)}, f32[2,64]{1,0:T(2,128)}, f32[2,64]{1,0:T(2,128)}, f32[2,25...) custom-call(bf16[7,7,4,2048]{3,2,1,0:T(4,128)(2,1)} %get-tuple-eleme, ...), custom_call_target="tpu_custom_call" | custom-call | tf_op jit(solution)/shard_map/finish_step/pallas_call | solution.py:1428
